TPU v7x, 128 devices: a whole 4x4x4 slice. The times are simulated.
128 devices in a mesh: tracer: 4 (over z), sub: 32 (over y, x, core).
Axes of the slice: x: 4, y: 4, z: 4, core: 2. Of those that a mesh axis runs over, the one named last changes fastest.
Arguments:
- factor_lower: float32 [4, 512, 256, 256], P('tracer', 'sub'), may hold values from -1 to 1
- factor_pivot: float32 [4, 512, 256, 256], P('tracer', 'sub'), may hold values from -3 to 3
- factor_upper: float32 [4, 512, 256, 256], P('tracer', 'sub'), may hold values from -1 to 1
- source_pattern: float32 [4, 512, 256], P('tracer', 'sub'), may hold values from -6 to 6
- regions: int32 [512, 256], P('sub'), may hold values from 0 to 599, as said below
- params: float32 [600], replicated, may hold values from -6 to 6
- obs_cells: int32 [4, 8192], P('tracer', 'sub'), may hold values from 0 to 131071, as said below
- obs_values: float32 [4, 8192], P('tracer', 'sub'), may hold values from -6 to 6
Outputs:
- gradient: float32 [600], replicated
- solution: float32 [4, 512, 256], P('tracer', 'sub')
Inputs may be any that keep to these rules, and one draw needn't show every extreme that they name: `regions`: A cell of block k carries a region within 3 of k * 600 // 512; the first cell of block 0 carries 0 and the last cell of block 511 carries 600 - 1. `obs_cells`: observations j * 256 to (j + 1) * 256 - 1 of a tracer lie in blocks j * 16 to (j + 1) * 16 - 1; the first two of them sit at the first and the last cell of those blocks. Cells may repeat.
All inputs are finite; a program needn't handle non-finite values.
Results may differ from a plain program's by a relative error of at most 0.0003.
Values sent between devices are 32-bit elements; how exact they have to be, the bound alone decides.
No kernel may reach another device: no remote copies, remote signals or barrier semaphores. Data moves between devices by JAX's collectives and lax.ppermute only.
A program may use at most 192 MiB of HBM per device.

v0:
```python
import jax
import jax.numpy as jnp
from jax import lax
from jax.sharding import PartitionSpec as P

exact_mode = lax.Precision.HIGHEST


def matvec(matrix, vector):
    return jnp.dot(matrix, vector, precision=exact_mode)


def matvec_t(matrix, vector):
    return jnp.dot(vector, matrix, precision=exact_mode)


def plain_sweep(matrices, terms, start, reverse):

    def plain_advance(carried, pair):
        matrix, term = pair
        carried = term + matvec(matrix, carried)
        return (carried, carried)

    final, states = lax.scan(plain_advance, start, (matrices, terms), reverse=reverse)
    return (states, final)


def adjoint_sweep(matrices, terms, start, reverse):

    def adjoint_advance(carried, pair):
        matrix, term = pair
        value = term + carried
        return (matvec_t(matrix, value), value)

    final, states = lax.scan(adjoint_advance, start, (matrices, terms), reverse=reverse)
    return (states, final)


def entering(matrices, offset, forward, transposed):
    sub_count = lax.axis_size("sub")
    offsets = lax.all_gather(offset[None], "sub", axis=0, tiled=True)
    my_index = lax.axis_index("sub")

    def fold_step(turn, carried):
        device = turn if forward else sub_count - 1 - turn
        matrix = lax.dynamic_index_in_dim(matrices, device, 0, keepdims=False)
        moved = matvec_t(matrix, carried) if transposed else matvec(matrix, carried)
        moved = moved + lax.dynamic_index_in_dim(offsets, device, 0, keepdims=False)
        applies = device < my_index if forward else device > my_index
        return jnp.where(applies, moved, carried)

    return lax.fori_loop(0, sub_count, fold_step, jnp.zeros_like(offset))


def shards(
    factor_lower, factor_pivot, factor_upper, source_pattern, regions, params, obs_cells, obs_values
):
    lower_mats = factor_lower[0]
    pivot_mats = factor_pivot[0]
    upper_mats = factor_upper[0]
    pattern = source_pattern[0]
    blocks = lower_mats.shape[0]
    cell_count = lower_mats.shape[1]
    sub_count = lax.axis_size("sub")
    my_index = lax.axis_index("sub")
    source_scale = float(blocks * sub_count) ** (-1.5)
    source = source_scale * pattern * jnp.take(params, regions, axis=0)
    zero_state = jnp.zeros((cell_count,), jnp.float32)
    identity = jnp.eye(cell_count, dtype=jnp.float32)

    def left_multiply(product, matrix):
        product = jnp.dot(matrix, product, precision=exact_mode)
        return (product, product)

    def right_multiply(product, matrix):
        product = jnp.dot(product, matrix, precision=exact_mode)
        return (product, product)

    comp_lower, lower_prefix = lax.scan(left_multiply, identity, lower_mats)
    comp_upper, upper_prefix = lax.scan(right_multiply, identity, upper_mats)
    unused_upper, upper_suffix = lax.scan(left_multiply, identity, upper_mats, reverse=True)
    unused_lower, lower_suffix = lax.scan(right_multiply, identity, lower_mats, reverse=True)
    upper_before = jnp.concatenate([identity[None], upper_prefix[:-1]], axis=0)
    lower_after = jnp.concatenate([lower_suffix[1:], identity[None]], axis=0)
    all_lower, all_upper = (
        lax.all_gather(comp_lower[None], "sub", axis=0, tiled=True),
        lax.all_gather(comp_upper[None], "sub", axis=0, tiled=True),
    )
    partial_states, forward_offset = plain_sweep(lower_mats, source, zero_state, False)
    forward_in = entering(all_lower, forward_offset, True, False)
    forward = partial_states + jnp.einsum(
        "kij,j->ki", lower_prefix, forward_in, precision=exact_mode
    )
    scaled = jnp.einsum("kij,kj->ki", pivot_mats, forward, precision=exact_mode)
    partial_states, upper_offset = plain_sweep(upper_mats, scaled, zero_state, True)
    solution_in = entering(all_upper, upper_offset, False, False)
    solution = partial_states + jnp.einsum(
        "kij,j->ki", upper_suffix, solution_in, precision=exact_mode
    )
    local_cells = obs_cells[0] - my_index * (blocks * cell_count)
    flat_cells = solution.reshape(-1)
    misfit = jnp.take(flat_cells, local_cells, axis=0) - obs_values[0]
    forcing = jnp.zeros((blocks * cell_count,), jnp.float32).at[local_cells].add(misfit)
    forcing = forcing.reshape(blocks, cell_count)
    partial_states, carried_offset = adjoint_sweep(upper_mats, forcing, zero_state, False)
    carried_in = entering(all_upper, carried_offset, True, True)
    carried = partial_states + jnp.einsum(
        "j,kji->ki", carried_in, upper_before, precision=exact_mode
    )
    unscaled = jnp.einsum("kji,kj->ki", pivot_mats, carried, precision=exact_mode)
    partial_states, adjoint_offset = adjoint_sweep(lower_mats, unscaled, zero_state, True)
    adjoint_in = entering(all_lower, adjoint_offset, False, True)
    adjoint = partial_states + jnp.einsum(
        "j,kji->ki", adjoint_in, lower_after, precision=exact_mode
    )
    terms = (pattern * adjoint).reshape(-1)
    partial_gradient = source_scale * jax.ops.segment_sum(
        terms, regions.reshape(-1), num_segments=params.shape[0]
    )
    gradient = lax.psum(partial_gradient, ("tracer", "sub"))
    return (gradient, solution[None])


def solution(mesh):
    return jax.shard_map(
        shards,
        mesh=mesh,
        in_specs=(
            P("tracer", "sub", None, None),
            P("tracer", "sub", None, None),
            P("tracer", "sub", None, None),
            P("tracer", "sub", None),
            P("sub", None),
            P(),
            P("tracer", "sub"),
            P("tracer", "sub"),
        ),
        out_specs=(P(), P("tracer", "sub", None)),
        check_vma=False,
    )
```

profile of v0, /device:TPU:1, one launch (start us, length us, event | category | flops | bytes accessed | tf_op | source)
XLA Modules:
  0.0 673.7 jit_solution(2311145240095780549)
XLA Ops:
  7.4 2.4 broadcast.50.clone2
  9.8 33.1 %while.174 = (s32[]{:T(128)}, f32[256,256]{1,0:T(8,128)S(1)}, f32[16,256,256]{2,1,0:T(8,128)}, f32[16,256,256]{2,1,0:T(8,128)}, s32[]{:T(128)}) while((s32[]{:T(128)}, f32[256,256]{1,0:T(8,128)S(1)}, f32[16,256,256]{2,1,0:T(8,128)}, f32[16,256,256]{2,1,0:T(8,128)}, s32[]{:T(128)}) %tuple.373), condition=%wide.region_3.4_spmd, body=%wide.region_2.3_spmd.sunk | while | flops 201326592 | bytes 1573949 | solution.py:79
  43.8 2.4 broadcast.50.clone.1
  46.2 36.6 %while.176 = (s32[]{:T(128)}, f32[256,256]{0,1:T(8,128)S(1)}, f32[16,256,256]{1,2,0:T(8,128)}, f32[16,256,256]{2,1,0:T(8,128)}, s32[]{:T(128)}) while((s32[]{:T(128)}, f32[256,256]{0,1:T(8,128)S(1)}, f32[16,256,256]{1,2,0:T(8,128)}, f32[16,256,256]{2,1,0:T(8,128)}, s32[]{:T(128)}) %tuple.369), condition=%wide.region_11.12_spmd, body=%wide.region_10.11_spmd.sunk | while | flops 201326592 | bytes 1573949 | solution.py:80
  57.6 2.3 bitcast_dynamic-update-slice_fusion.10
  83.7 16.7 %gather_fusion = f32[4096]{0:T(1024)S(1)} fusion(f32[600]{0:T(1024)S(1)} %copy-done, s32[4096]{0:T(1024)S(1)} %broadcast_clamp_fusion), kind=kCustom, calls=%fused_computation | custom fusion | bytes 49152 | tf_op jit(solution)/shard_map/jit(_take)/gather | solution.py:67
  100.4 22.1 %while.180 = (s32[]{:T(128)}, f32[256]{0:T(256)S(1)}, f32[16,256]{1,0:T(8,128)S(1)}, f32[16,256]{1,0:T(8,128)S(1)}, f32[16,256,256]{2,1,0:T(8,128)}, /*index=5*/s32[]{:T(128)}, s32[]{:T(128)}) while((s32[]{:T(128)}, f32[256]{0:T(256)S(1)}, f32[16,256]{1,0:T(8,128)S(1)}, f32[16,256]{1,0:T(8,128)S(1)}, f32[16,256,256]{2,1,0:T(8,128)}, ...), condition=%wide.region_1.2_spmd.clone, body=%wide.region_0.1_spmd.clone.sunk | while | flops 786947 | bytes 274015 | solution.py:24
  122.6 25.8 %all-gather.6 = f32[32,1,256]{2,1,0:T(1,128)S(1)} all-gather(f32[1,1,256]{2,1,0:T(1,128)S(1)} %bitcast.319), channel_id=3, replica_groups=mesh['tracer'=4,'sub'=32] {'sub'}, dimensions={0}, use_global_device_ids=true | all-gather | bytes 33792 | tf_op jit(solution)/shard_map/all_gather | solution.py:41
  148.4 2.4 broadcast.50.clone2.1
  150.8 33.1 %while.175 = (s32[]{:T(128)}, f32[256,256]{1,0:T(8,128)S(1)}, f32[16,256,256]{2,1,0:T(8,128)}, f32[16,256,256]{2,1,0:T(8,128)}, s32[]{:T(128)}, /*index=5*/s32[]{:T(128)}) while((s32[]{:T(128)}, f32[256,256]{1,0:T(8,128)S(1)}, f32[16,256,256]{2,1,0:T(8,128)}, f32[16,256,256]{2,1,0:T(8,128)}, s32[]{:T(128)}, /*index=5*/s32[]{:T(128)}) %tuple.370), condition=%wide.region_9.10_spmd, body=%wide.region_8.9_spmd.sunk | while | flops 201326592 | bytes 1573969 | solution.py:81
  183.9 4.3 slice.6
  188.3 2.4 broadcast.50.clone.2
  190.6 36.6 %while.179 = (s32[]{:T(128)}, f32[256,256]{0,1:T(8,128)S(1)}, f32[16,256,256]{1,2,0:T(8,128)}, f32[16,256,256]{2,1,0:T(8,128)}, s32[]{:T(128)}, /*index=5*/s32[]{:T(128)}) while((s32[]{:T(128)}, f32[256,256]{0,1:T(8,128)S(1)}, f32[16,256,256]{1,2,0:T(8,128)}, f32[16,256,256]{2,1,0:T(8,128)}, s32[]{:T(128)}, /*index=5*/s32[]{:T(128)}) %tuple.375), condition=%wide.region_24.25_spmd, body=%wide.region_23.24_spmd.sunk | while | flops 201326592 | bytes 1573969 | solution.py:82
  227.2 4.4 slice.7
  231.7 42.9 %while.181 = (s32[]{:T(128)}, f32[256]{0:T(256)S(1)}, s32[]{:T(128)}, f32[32,256,256]{2,1,0:T(8,128)}, f32[32,256]{1,0:T(8,128)S(1)}, /*index=5*/s32[]{:T(128)}, s32[]{:T(128)}) while((s32[]{:T(128)}, f32[256]{0:T(256)S(1)}, s32[]{:T(128)}, f32[32,256,256]{2,1,0:T(8,128)}, f32[32,256]{1,0:T(8,128)S(1)}, /*index=5*/s32[]{:T(128)}, ...), condition=%wide.region_5.6_spmd.clone, body=%wide.region_4.5_spmd.clone.sunk | while | flops 787460 | bytes 272998 | solution.py:52
  274.6 5.9 fusion.79
  280.6 3.5 fusion.58
  284.1 22.1 %while.182 = (s32[]{:T(128)}, f32[256]{0:T(256)S(1)}, f32[16,256]{1,0:T(8,128)S(1)}, f32[16,256]{1,0:T(8,128)S(1)}, f32[16,256,256]{2,1,0:T(8,128)}, /*index=5*/s32[]{:T(128)}, s32[]{:T(128)}, s32[]{:T(128)}) while((s32[]{:T(128)}, f32[256]{0:T(256)S(1)}, f32[16,256]{1,0:T(8,128)S(1)}, f32[16,256]{1,0:T(8,128)S(1)}, ...), condition=%wide.region_7.8_spmd.clone, body=%wide.region_6.7_spmd.clone.sunk | while | flops 786948 | bytes 273527 | solution.py:24
  306.3 23.6 %all-gather.7 = f32[32,1,256]{2,1,0:T(1,128)S(1)} all-gather(f32[1,1,256]{2,1,0:T(1,128)S(1)} %bitcast.317), channel_id=5, replica_groups=mesh['tracer'=4,'sub'=32] {'sub'}, dimensions={0}, use_global_device_ids=true | all-gather | bytes 33792 | tf_op jit(solution)/shard_map/all_gather | solution.py:41
  329.9 9.1 %copy.24 = f32[8192,256]{1,0:T(8,128)} copy(f32[8192,256]{0,1:T(8,128)} %all-gather.15.cloned.1.call-done) | data formatting | bytes 16777216 | tf_op jit(solution)/shard_map/all_gather | solution.py:87
  338.9 43.2 %while.183 = (s32[]{:T(128)}, f32[256]{0:T(256)S(1)}, s32[]{:T(128)}, f32[32,256,256]{2,1,0:T(8,128)}, f32[32,256]{1,0:T(8,128)S(1)}, /*index=5*/s32[]{:T(128)}, s32[]{:T(128)}, s32[]{:T(128)}, s32[]{:T(128)}) while((s32[]{:T(128)}, f32[256]{0:T(256)S(1)}, s32[]{:T(128)}, f32[32,256,256]{2,1,0:T(8,128)}, ...), condition=%wide.region_13.14_spmd.clone, body=%wide.region_12.13_spmd.clone.sunk | while | flops 787464 | bytes 272552 | solution.py:52
  382.1 5.8 fusion.80
  392.3 20.1 %while.177 = (s32[]{:T(128)}, f32[256]{0:T(256)S(1)}, f32[16,256]{1,0:T(8,128)S(1)}, f32[16,256]{1,0:T(8,128)S(1)}, f32[16,256,256]{2,1,0:T(8,128)}, /*index=5*/s32[]{:T(128)}, s32[]{:T(128)}) while((s32[]{:T(128)}, f32[256]{0:T(256)S(1)}, f32[16,256]{1,0:T(8,128)S(1)}, f32[16,256]{1,0:T(8,128)S(1)}, f32[16,256,256]{2,1,0:T(8,128)}, ...), condition=%wide.region_16.17_spmd, body=%wide.region_15.16_spmd.sunk | while | flops 786690 | bytes 271957 | solution.py:35
  412.3 22.1 %all-gather.8 = f32[32,1,256]{2,1,0:T(1,128)S(1)} all-gather(f32[1,1,256]{2,1,0:T(1,128)S(1)} %bitcast.346), channel_id=6, replica_groups=mesh['tracer'=4,'sub'=32] {'sub'}, dimensions={0}, use_global_device_ids=true | all-gather | bytes 33792 | tf_op jit(solution)/shard_map/all_gather | solution.py:41
  434.4 40.3 %while.184 = (s32[]{:T(128)}, f32[256]{0:T(256)S(1)}, s32[]{:T(128)}, f32[32,256,256]{2,1,0:T(8,128)}, f32[32,256]{1,0:T(8,128)S(1)}, /*index=5*/s32[]{:T(128)}, s32[]{:T(128)}) while((s32[]{:T(128)}, f32[256]{0:T(256)S(1)}, s32[]{:T(128)}, f32[32,256,256]{2,1,0:T(8,128)}, f32[32,256]{1,0:T(8,128)S(1)}, /*index=5*/s32[]{:T(128)}, ...), condition=%wide.region_18.19_spmd.clone, body=%wide.region_17.18_spmd.clone.sunk | while | flops 787460 | bytes 272998 | solution.py:52
  474.8 5.7 fusion.48
  482.6 20.1 %while.178 = (s32[]{:T(128)}, f32[256]{0:T(256)S(1)}, f32[16,256]{1,0:T(8,128)S(1)}, f32[16,256]{1,0:T(8,128)S(1)}, f32[16,256,256]{2,1,0:T(8,128)}, /*index=5*/s32[]{:T(128)}, s32[]{:T(128)}, s32[]{:T(128)}) while((s32[]{:T(128)}, f32[256]{0:T(256)S(1)}, f32[16,256]{1,0:T(8,128)S(1)}, f32[16,256]{1,0:T(8,128)S(1)}, ...), condition=%wide.region_20.21_spmd, body=%wide.region_19.20_spmd.sunk | while | flops 786691 | bytes 271469 | solution.py:35
  502.7 23.6 %all-gather.9 = f32[32,1,256]{2,1,0:T(1,128)S(1)} all-gather(f32[1,1,256]{2,1,0:T(1,128)S(1)} %bitcast.348), channel_id=7, replica_groups=mesh['tracer'=4,'sub'=32] {'sub'}, dimensions={0}, use_global_device_ids=true | all-gather | bytes 33792 | tf_op jit(solution)/shard_map/all_gather | solution.py:41
  526.3 40.6 %while.185 = (s32[]{:T(128)}, f32[256]{0:T(256)S(1)}, s32[]{:T(128)}, f32[32,256,256]{2,1,0:T(8,128)}, f32[32,256]{1,0:T(8,128)S(1)}, /*index=5*/s32[]{:T(128)}, s32[]{:T(128)}, s32[]{:T(128)}, s32[]{:T(128)}) while((s32[]{:T(128)}, f32[256]{0:T(256)S(1)}, s32[]{:T(128)}, f32[32,256,256]{2,1,0:T(8,128)}, ...), condition=%wide.region_22.23_spmd.clone, body=%wide.region_21.22_spmd.clone.sunk | while | flops 787464 | bytes 272552 | solution.py:52
  566.9 5.6 fusion.52
  572.5 28.8 %scatter_custom_fusion.1 = f32[600]{0:T(1024)S(1)} fusion(s32[4096]{0:T(1024)S(1)} %bitcast.351, f32[4096]{0:T(1024)S(1)} %bitcast.352, f32[]{:T(128)} %constant.358.clone.1), kind=kCustom, calls=%fused_computation.119 | custom fusion | flops 4096 | bytes 2404 | tf_op jit(solution)/shard_map/scatter-add | solution.py:117
  601.3 65.6 %psum.7 = f32[600]{0:T(1024)} all-reduce(f32[600]{0:T(1024)S(1)} %broadcast_multiply_fusion), channel_id=1, replica_groups=mesh['tracer'=4,'sub'=32] {'tracer','sub'}, use_global_device_ids=true, to_apply=%region_26.27 | all-reduce | flops 600 | bytes 4800 | tf_op jit(solution)/shard_map/psum | solution.py:120
  (994 shorter events, 388.4 us)
Async XLA Ops:
  7.2 76.5 %copy-start = (f32[600]{0:T(1024)S(1)}, f32[600]{0:T(1024)}, u32[]{:S(2)}) copy-start(f32[600]{0:T(1024)} %param.37) | copy-start | bytes 7204
  7.2 224.5 %all-gather.13.cloned.1.call-start = ((), (), s32[]{:S(2)}) async-start(), calls=%async_computation | async-start | bytes 8650752 | tf_op jit(solution)/shard_map/all_gather | solution.py:86
  43.0 0.7 copy-start.3
  43.7 286.2 %all-gather.15.cloned.1.call-start = ((), (), s32[]{:S(2)}) async-start(), calls=%async_computation.1 | async-start | bytes 8650752 | tf_op jit(solution)/shard_map/all_gather | solution.py:87
  46.2 37.4 %copy-start.5 = (s32[16,256]{1,0:T(8,128)S(1)}, s32[16,256]{1,0:T(8,128)}, u32[]{:S(2)}) copy-start(s32[16,256]{1,0:T(8,128)} %param.36) | copy-start | bytes 49156
  82.8 0.7 copy-start.4
  83.7 16.7 %copy-start.6 = (f32[1,16,256]{2,1,0:T(8,128)S(1)}, f32[1,16,256]{2,1,0:T(8,128)}, u32[]{:S(2)}) copy-start(f32[1,16,256]{2,1,0:T(8,128)} %param.35) | copy-start | bytes 49156
  150.8 33.1 %copy-start.7 = (s32[1,256]{1,0:T(1,128)S(1)}, s32[1,256]{1,0:T(1,128)}, u32[]{:S(2)}) copy-start(s32[1,256]{1,0:T(1,128)} %param.38) | copy-start | bytes 3076
  274.6 6.0 copy-start.1
  338.9 51.3 %copy-start.8 = (f32[1,256]{1,0:T(1,128)S(1)}, f32[1,256]{1,0:T(1,128)}, u32[]{:S(2)}) copy-start(f32[1,256]{1,0:T(1,128)} %param.39) | copy-start | bytes 3076
  474.7 5.8 copy-start.2
Sparse Core Ops, SparseCore 0:
  43.8 56.3 all-gather.12
  102.5 59.2 all-gather.14
where the time goes:
time: 682 us; the launch traced here: 674 us
  matrix products  395 us (58%)
  blocking collectives  161 us (24%)
  local copies, waits for them, and re-layouts  60.5 us (9%)
  other arithmetic  34.2 us (5%)
  between operations  14.5 us (2%)
  loops' own time  8.48 us (1%)
    dot_general x96, matrix products, matvec(): return jnp.dot(matrix, vector, precision=exact_mode)  118 us
    dot_general x96, matrix products, matvec_t(): return jnp.dot(vector, matrix, precision=exact_mode)  111 us
    all_gather x4, blocking collectives, entering(): offsets = lax.all_gather(offset[None], 'sub', axis=0, tiled=True)  95.1 us
    dot_general x32, matrix products, right_multiply(): product = jnp.dot(product, matrix, precision=exact_mode)  72.5 us
    psum x1, blocking collectives, shards(): gradient = lax.psum(partial_gradient, ('tracer', 'sub'))  65.6 us
    dot_general x32, matrix products, left_multiply(): product = jnp.dot(matrix, product, precision=exact_mode)  65.5 us
    scatter-add x1, other arithmetic, shards(): jax.ops.segment_sum(terms, regions.reshape(-1), num_segments=params.shape...  28.8 us
    gather x2, local copies, waits for them, and re-layouts, shards(): source = source_scale * pattern * jnp.take(params, regions, axis=0)  16.7 us
  transfers between devices with their start and end apart: 2, of which 0 were waited for; matrix products, arithmetic and copies ran while one was open for 35% of the time, Pallas kernels for 0%

commit v1 on v0

v1 whole, which is shorter than its diff:
```python
import functools

import jax
import jax.numpy as jnp
from jax import lax
from jax.experimental import pallas as pl
from jax.experimental.pallas import tpu as pltpu
from jax.sharding import PartitionSpec as P

F32 = jnp.float32
BF16 = jnp.bfloat16
B = 256
AUG = 264
WIN = 32
ROWS = B + WIN
NT = (((1,), (1,)), ((), ()))
NN = (((1,), (0,)), ((), ()))
MIB = 1 << 20
VM = pl.BlockSpec(memory_space=pltpu.VMEM)
SM = pl.BlockSpec(memory_space=pltpu.SMEM)
ANY = pl.BlockSpec(memory_space=pl.ANY)


def split(a):
    high = a.astype(BF16)
    return high, (a - high.astype(F32)).astype(BF16)


def dot3(a, b, dims):
    ah, al = split(a)
    bh, bl = split(b)
    d = functools.partial(lax.dot_general, dimension_numbers=dims, preferred_element_type=F32)
    return d(ah, bh) + (d(ah, bl) + d(al, bh))


def affine(first, second):
    product = dot3(first, second[:B], NN)
    return jnp.concatenate([product[:B], product[B:] + second[B:]], axis=0)


def spread(row):
    return jnp.broadcast_to(row, (128, row.shape[1])).T


def apply(row, mt):
    vb = spread(row)
    return jnp.concatenate(
        [
            jnp.sum(vb * mt[:, :128], axis=0, keepdims=True),
            jnp.sum(vb * mt[:, 128:], axis=0, keepdims=True),
        ],
        axis=1,
    )


def adjoint_column(row, mt):
    acc = mt[:, :128] * row[:, :128] + mt[:, 128:] * row[:, 128:]
    return jnp.sum(acc, axis=1, keepdims=True)


def to_row(column):
    return jnp.broadcast_to(column, (column.shape[0], 128)).T[0:1]


def apply_t(row, mt):
    return to_row(adjoint_column(row, mt))


def place(pos_ref):
    return pos_ref[0], pos_ref[1], pos_ref[2], pos_ref[3]


def row_coords():
    i = lax.broadcasted_iota(jnp.int32, (32, 128), 0)
    return i >> 3, (i >> 1) & 3, i & 1


def scatter_rows(out_ref, pieces):
    for half in range(2):
        total = jnp.zeros((32, 128), F32)
        for mask, row in pieces:
            total = total + jnp.where(mask, row[:, half * 128 : half * 128 + 128], 0.0)
        out_ref[:, half, :] = total


def gather_rows(ref, masks):
    halves = [ref[:, 0, :], ref[:, 1, :]]
    return [
        jnp.concatenate(
            [jnp.sum(jnp.where(m, h, 0.0), axis=0, keepdims=True) for h in halves], axis=1
        )
        for m in masks
    ]


def source_window(k, reg_ref, pat_ref, base, scale):
    rel = reg_ref[pl.ds(k, 1), :] - base
    w = lax.broadcasted_iota(jnp.int32, (WIN, B), 0)
    return jnp.where(w == rel, scale * pat_ref[pl.ds(k, 1), :], 0.0)


def composites_kernel(
    blocks, scale, pos_ref, par_ref, low_hbm, up_hbm, pat_ref, reg_ref,
    own_ref, send_ref, low, up, src, xs, rs, sems
):
    last = blocks - 1

    def copies(k):
        return (
            pltpu.make_async_copy(low_hbm.at[k], low.at[k], sems.at[0, k]),
            pltpu.make_async_copy(up_hbm.at[last - k], up.at[last - k], sems.at[1, k]),
        )

    for k in range(blocks):
        for c in copies(k):
            c.start()
    y, x, core, base = place(pos_ref)
    rel = reg_ref[...] - base
    value = jnp.zeros((blocks, B), F32)
    count = par_ref.shape[0]
    for w in range(WIN):
        value = jnp.where(rel == w, par_ref[jnp.clip(base + w, 0, count - 1)], value)
    src[...] = scale * pat_ref[...] * value
    for c in copies(0):
        c.wait()
    xs[...] = jnp.concatenate([low[0].T, jnp.broadcast_to(src[0:1, :], (8, B))], axis=0)
    rs[...] = up[last].T

    def step(k, carry):
        for c in copies(k):
            c.wait()
        moved = dot3(xs[...], low[k], NT)
        other = dot3(rs[...], up[last - k], NT)
        xs[...] = jnp.concatenate([moved[:B], moved[B:] + src[pl.ds(k, 1), :]], axis=0)
        rs[...] = other
        return carry

    lax.fori_loop(1, blocks, step, 0)
    zero = jnp.zeros((8, B), F32)

    @pl.when(core == 0)
    def _():
        own_ref[...] = xs[...]
        send_ref[:B, :] = rs[...]
        send_ref[B:, :] = zero

    @pl.when(core != 0)
    def _():
        send_ref[...] = xs[...]
        own_ref[:B, :] = rs[...]
        own_ref[B:, :] = zero


def chip_kernel(own_ref, got_ref, out_ref):
    out_ref[...] = affine(own_ref[...], got_ref[...])


def lines_kernel(
    blocks, scale, pos_ref, par_ref, low_hbm, up_hbm, piv_hbm, pat_ref, reg_ref, cells_ref, values_ref, dep_ref,
    y_ref, r_ref, f_ref, cnt_ref, sum_ref, pw_ref, low, up, piv, xs, sems
):
    last = blocks - 1
    y, x, core, base = place(pos_ref)

    def copies(k):
        return (
            pltpu.make_async_copy(low_hbm.at[k], low.at[k], sems.at[0, k]),
            pltpu.make_async_copy(up_hbm.at[last - k], up.at[last - k], sems.at[1, k]),
        )

    def pivot(k):
        return pltpu.make_async_copy(piv_hbm.at[k], piv.at[k], sems.at[2, k])

    for k in range(blocks):
        for c in copies(k):
            c.start()
    for k in range(blocks):
        pivot(last - k).start()

    local = cells_ref[...] - ((y * 4 + x) * 2 + core) * (blocks * B)
    high = local >> 8
    low_part = local & 255
    which = jnp.where(lax.broadcasted_iota(jnp.int32, (blocks, B), 0) == high, 1.0, 0.0)
    slot = jnp.where(lax.broadcasted_iota(jnp.int32, (B, B), 0) == low_part, 1.0, 0.0).astype(BF16)
    weighted = which * values_ref[...]
    v1, rest = weighted.astype(BF16), None
    rest = weighted - v1.astype(F32)
    v2, v3 = split(rest)
    d = functools.partial(lax.dot_general, dimension_numbers=NT, preferred_element_type=F32)
    cnt_ref[...] = d(which.astype(BF16), slot)
    sum_ref[...] = d(v1, slot) + (d(v2, slot) + d(v3, slot))
    wi = lax.broadcasted_iota(jnp.int32, (WIN, 128), 0)
    window = jnp.zeros((WIN, 128), F32)
    count = par_ref.shape[0]
    for w in range(WIN):
        window = jnp.where(wi == w, par_ref[jnp.clip(base + w, 0, count - 1)], window)
    pw_ref[...] = window

    for c in copies(0):
        c.wait()
    xs[0] = jnp.concatenate([low[0].T, source_window(0, reg_ref, pat_ref, base, scale)], axis=0)
    r_ref[last] = up[last].T

    def step(k, carry):
        for c in copies(k):
            c.wait()
        moved = dot3(xs[k - 1], low[k], NT)
        r_ref[last - k] = dot3(r_ref[last - k + 1], up[last - k], NT)
        xs[k] = jnp.concatenate(
            [moved[:B], moved[B:] + source_window(k, reg_ref, pat_ref, base, scale)], axis=0
        )
        return carry

    lax.fori_loop(1, blocks, step, 0)
    f_ref[...] = xs[last, B:, :]
    pivot(last).wait()
    y_ref[last] = dot3(xs[last], piv[last], NT)

    def back(i, carry):
        k = last - i
        pivot(k).wait()
        y_ref[k] = dot3(xs[k], piv[k], NT) + dot3(y_ref[k + 1], up[k], NT)
        return carry

    lax.fori_loop(1, blocks, back, 0)


def line_kernel(pos_ref, own_ref, r1_ref, r2_ref, r3_ref, maps_ref, row_ref, tail_ref):
    y, x, core, base = place(pos_ref)
    p = jnp.where(core == 0, x, 3 - x)
    i = lax.broadcasted_iota(jnp.int32, (AUG, B), 0)
    j = lax.broadcasted_iota(jnp.int32, (AUG, B), 1)
    eye = jnp.where(i == j, 1.0, 0.0)
    r1, r2, r3 = r1_ref[...], r2_ref[...], r3_ref[...]
    maps_ref[0] = jnp.where(p >= 1, r1, eye)
    maps_ref[1] = jnp.where(p >= 2, r2, eye)
    pre = affine(jnp.where(p >= 3, r3, eye), maps_ref[1])
    suf = affine(jnp.where(p <= 2, r3, eye), jnp.where(p <= 1, r2, eye))
    maps_ref[2] = affine(pre, maps_ref[0])
    maps_ref[3] = affine(suf, jnp.where(p <= 0, r1, eye))
    row_ref[...] = affine(affine(maps_ref[2], own_ref[...]), maps_ref[3])
    tail_ref[...] = row_ref[B:, :]


def entering_kernel(own_ref, maps_ref, y1_ref, y2_ref, t3_ref, chip_ref, next_ref):
    inner = y2_ref[B : B + 1, :] + apply(t3_ref[0:1, :], y2_ref[:B, :])
    row = y1_ref[B : B + 1, :] + apply(inner, y1_ref[:B, :])
    chip = maps_ref[2, B : B + 1, :] + apply(row, maps_ref[2, :B, :])
    following = own_ref[B : B + 1, :] + apply(chip, own_ref[:B, :])
    chip_ref[...] = jnp.broadcast_to(chip, (8, B))
    next_ref[...] = jnp.broadcast_to(following, (8, B))


def start_kernel(pos_ref, chip_ref, got_ref, pw_ref, y0_ref, near_ref, suf_ref, in_ref, out_ref):
    my_y, my_x, core, base = place(pos_ref)
    entering = jnp.where(core == 0, chip_ref[0:1, :], got_ref[0:1, :])
    vb = jnp.concatenate([spread(entering), pw_ref[...]], axis=0)
    in_ref[...] = vb
    y0 = y0_ref[0]
    v = jnp.concatenate(
        [
            jnp.sum(vb * y0[:, :128], axis=0, keepdims=True),
            jnp.sum(vb * y0[:, 128:], axis=0, keepdims=True),
        ],
        axis=1,
    )
    z1 = jnp.where(core == 1, apply(v, near_ref[:B, :]), v)
    z2 = apply(z1, suf_ref[0, :B, :])
    ty, tx, tc = row_coords()
    same = ty == my_y
    scatter_rows(
        out_ref,
        [
            (same & (tx == my_x) & (tc < core), v),
            (same & (tx < my_x), z1),
            (ty < my_y, z2),
        ],
    )


def spread_out(out_ref, pos_ref, first, near_ref, maps_ref, d1_ref, d2_ref, leftward):
    my_y, my_x, core, base = place(pos_ref)
    side = 1 if leftward else 0
    g = jnp.where(core == side, apply_t(first, near_ref[:B, :]), first)
    g2 = apply_t(g, maps_ref[0, :B, :])
    g3 = apply_t(g2, maps_ref[1, :B, :])
    h = apply_t(g, maps_ref[2, :B, :])
    h2 = apply_t(h, d1_ref[:B, :])
    h3 = apply_t(h2, d2_ref[:B, :])
    ty, tx, tc = row_coords()
    sign = -1 if leftward else 1
    dy, dx, dc = sign * (ty - my_y), sign * (tx - my_x), sign * (tc - core)
    same = dy == 0
    scatter_rows(
        out_ref,
        [
            (same & (dx == 0) & (dc > 0), first),
            (same & (dx == 1), g),
            (same & (dx == 2), g2),
            (same & (dx == 3), g3),
            (dy == 1, h),
            (dy == 2, h2),
            (dy == 3, h3),
        ],
    )


def collect(got_ref, pos_ref, near_ref, suf, leftward):
    my_y, my_x, core, base = place(pos_ref)
    sy, sx, sc = row_coords()
    same = sy == my_y
    part, mx, my = gather_rows(got_ref, [same & (sx == my_x), same & (sx != my_x), sy != my_y])
    m = mx + apply_t(my, suf)
    side = 0 if leftward else 1
    return part + jnp.where(core == side, apply_t(m, near_ref[:B, :]), m)


def middle_kernel(
    blocks, pos_ref, got_ref, near_ref, maps_ref, d1_ref, d2_ref, in_ref, y_ref, r_ref, cnt_ref, sum_ref,
    sol_ref, out_ref, acc_ref, sb, acc_r
):
    my_y, my_x, core, base = place(pos_ref)
    sy, sx, sc = row_coords()
    same = sy == my_y
    part, t1, t2, t3, y1, y2, y3 = gather_rows(
        got_ref,
        [same & (sx == my_x)]
        + [same & (sx == my_x + j) for j in (1, 2, 3)]
        + [sy == my_y + j for j in (1, 2, 3)],
    )
    yv = y1 + apply(y2 + apply(y3, d2_ref[:B, :]), d1_ref[:B, :])
    xv = t1 + apply(t2 + apply(t3, maps_ref[1, :B, :]), maps_ref[0, :B, :]) + apply(yv, maps_ref[2, :B, :])
    entering = part + jnp.where(core == 0, apply(xv, near_ref[:B, :]), xv)
    sb[...] = spread(entering)
    acc_ref[...] = jnp.zeros((ROWS, 128), F32)
    acc_r[...] = jnp.zeros((B, 128), F32)

    def step(k, carry):
        parts = []
        for half in range(2):
            lanes = slice(half * 128, half * 128 + 128)
            parts.append(
                jnp.sum(in_ref[...] * y_ref[k, :, lanes], axis=0, keepdims=True)
                + jnp.sum(sb[...] * r_ref[k, :, lanes], axis=0, keepdims=True)
            )
        row = jnp.concatenate(parts, axis=1)
        sol_ref[pl.ds(k, 1), :] = row
        forcing = cnt_ref[pl.ds(k, 1), :] * row - sum_ref[pl.ds(k, 1), :]
        left, right = forcing[:, :128], forcing[:, 128:]
        acc_ref[...] += y_ref[k, :, :128] * left + y_ref[k, :, 128:] * right
        acc_r[...] += r_ref[k, :, :128] * left + r_ref[k, :, 128:] * right
        return carry

    lax.fori_loop(0, blocks, step, 0)
    acc_ref[...] = jnp.broadcast_to(jnp.sum(acc_ref[...], axis=1, keepdims=True), (ROWS, 128))
    first = to_row(jnp.sum(acc_r[...], axis=1, keepdims=True))
    spread_out(out_ref, pos_ref, first, near_ref, maps_ref, d1_ref, d2_ref, False)


def return_kernel(
    pos_ref, got_ref, nearu_ref, sufu_ref, acc_ref, y0_ref, nearl_ref, maps_ref, d1_ref, d2_ref, out_ref, gw_ref
):
    c_in = collect(got_ref, pos_ref, nearu_ref, sufu_ref[0, :B, :], False)
    column = acc_ref[:, 0:1] + adjoint_column(c_in, y0_ref[0])
    gw_ref[...] = jnp.broadcast_to(column[B:], (WIN, 128))
    spread_out(out_ref, pos_ref, to_row(column[:B]), nearl_ref, maps_ref, d1_ref, d2_ref, True)


def window_kernel(scale, pos_ref, got_ref, near_ref, suf_ref, gw_ref, f_ref, out_ref):
    my_y, my_x, core, base = place(pos_ref)
    a_in = collect(got_ref, pos_ref, near_ref, suf_ref[0, :B, :], True)
    column = gw_ref[:, 0:1] + adjoint_column(a_in, f_ref[...])
    w = lax.broadcasted_iota(jnp.int32, (WIN, 128), 0)
    lane = lax.broadcasted_iota(jnp.int32, (WIN, 128), 1)
    row = jnp.sum(jnp.where(((base + w) & 127) == lane, column, 0.0), axis=0, keepdims=True)
    out_ref[...] = jnp.broadcast_to(row.reshape(1, 1, 128), out_ref.shape)


def total_kernel(blocks, groups, regions, tracers, got_ref, out_ref):
    total = got_ref[0:32, 0, :]
    for t in range(1, tracers):
        total = total + got_ref[32 * t : 32 * t + 32, 0, :]
    d = lax.broadcasted_iota(jnp.int32, (32, 128), 0)
    lane = lax.broadcasted_iota(jnp.int32, (32, 128), 1)
    base = (d * (blocks * regions)) // groups - 3
    tile = (base + ((lane - base) & 127)) >> 7
    for t in range(out_ref.shape[1] // 128 + 1):
        lo, hi = 128 * t, min(128 * t + 128, out_ref.shape[1])
        if hi > lo:
            row = jnp.sum(jnp.where(tile == t, total, 0.0), axis=0, keepdims=True)
            out_ref[:, lo:hi] = row[:, : hi - lo]


def device(y, x, core):
    return ((y % 4) * 4 + x % 4) * 2 + core


def shards(
    factor_lower, factor_pivot, factor_upper, source_pattern, regions, params, obs_cells, obs_values
):
    low, piv, up = factor_lower[0], factor_pivot[0], factor_upper[0]
    pat = source_pattern[0]
    blocks = low.shape[0]
    tracers = lax.axis_size("tracer")
    groups = blocks * lax.axis_size("sub")
    regions_all = params.shape[0]
    scale = float(groups) ** (-1.5)
    sub = lax.axis_index("sub")
    core = sub & 1
    pos = jnp.stack([sub >> 3, (sub >> 1) & 3, core, (sub * (blocks * regions_all)) // groups - 3])
    pos = pos.astype(jnp.int32)
    left = core == 0

    def shape(*dims):
        return jax.ShapeDtypeStruct(dims, F32)

    def call(kernel, outs, ins, scratch=(), limit=32, flops=0, traffic=0, name=None, grid=None, out_specs=None):
        return pl.pallas_call(
            kernel,
            out_shape=outs,
            in_specs=ins,
            out_specs=out_specs if out_specs is not None else jax.tree.map(lambda _: VM, outs),
            scratch_shapes=list(scratch),
            compiler_params=pltpu.CompilerParams(vmem_limit_bytes=limit * MIB),
            cost_estimate=pl.CostEstimate(flops=flops, bytes_accessed=traffic, transcendentals=0),
            name=name,
            **({"grid": grid} if grid else {}),
        )

    def swap(a):
        return lax.ppermute(a, "sub", [(d, d ^ 1) for d in range(32)])

    def along_x(a, j):
        pairs = [(device(y, x, 0), device(y, x + j, 0)) for y in range(4) for x in range(4)]
        pairs += [(device(y, x, 1), device(y, x - j, 1)) for y in range(4) for x in range(4)]
        return lax.ppermute(a, "sub", pairs)

    def along_y(a, j):
        pairs = [(device(y, x, 0), device(y + j, x, 0)) for y in range(4 - j) for x in range(4)]
        pairs += [(device(y, x, 1), device(y - j, x, 1)) for y in range(j, 4) for x in range(4)]
        return lax.ppermute(a, "sub", pairs)

    def exchange(a):
        return lax.all_to_all(a, "sub", 0, 0)

    block = (blocks, B, B)
    own, send = call(
        functools.partial(composites_kernel, blocks, scale),
        (shape(AUG, B), shape(AUG, B)),
        [SM, SM, ANY, ANY, VM, VM],
        [
            pltpu.VMEM(block, F32), pltpu.VMEM(block, F32), pltpu.VMEM((blocks, B), F32),
            pltpu.VMEM((AUG, B), F32), pltpu.VMEM((B, B), F32), pltpu.SemaphoreType.DMA((2, blocks)),
        ],
        flops=6 * 2 * 16 * B**3, traffic=8 * MIB, name="composites",
    )(pos, params, low, up, pat, regions)
    got = swap(send)
    chip = call(chip_kernel, shape(AUG, B), [VM, VM], flops=6 * B**3, name="chip")(own, got)
    other = swap(own)
    r1, r2, r3 = [along_x(chip, j) for j in (1, 2, 3)]
    yt, rt, ft, cnt, osum, pw = call(
        functools.partial(lines_kernel, blocks, scale),
        (
            shape(blocks, ROWS, B), shape(blocks, B, B), shape(WIN, B), shape(blocks, B), shape(blocks, B),
            shape(WIN, 128),
        ),
        [SM, SM, ANY, ANY, ANY, VM, VM, VM, VM, ANY],
        [
            pltpu.VMEM(block, F32), pltpu.VMEM(block, F32), pltpu.VMEM(block, F32),
            pltpu.VMEM((blocks, ROWS, B), F32), pltpu.SemaphoreType.DMA((3, blocks)),
        ],
        limit=40, flops=6 * 4 * 16 * B**3, traffic=21 * MIB, name="lines",
    )(pos, params, low, up, piv, pat, regions, obs_cells, obs_values, chip)
    maps, row, tail = call(
        line_kernel, (shape(4, AUG, B), shape(AUG, B), shape(8, B)), [SM, VM, VM, VM, VM],
        flops=6 * 6 * B**3, name="line",
    )(pos, chip, r1, r2, r3)
    y1, y2, y3 = along_y(row, 1), along_y(row, 2), along_y(tail, 3)
    maps_o = swap(maps)
    chip_in, following = call(
        entering_kernel, (shape(8, B), shape(8, B)), [VM] * 5, name="entering"
    )(own, maps, y1, y2, y3)
    following = swap(following)
    y1_o, y2_o = swap(y1), swap(y2)
    maps_l, maps_u = jnp.where(left, maps, maps_o), jnp.where(left, maps_o, maps)
    near_u, near_l = jnp.where(left, other, got), jnp.where(left, got, other)
    y1_l, y1_u = jnp.where(left, y1, y1_o), jnp.where(left, y1_o, y1)
    y2_l, y2_u = jnp.where(left, y2, y2_o), jnp.where(left, y2_o, y2)

    def at(shape_, index):
        return pl.BlockSpec(shape_, lambda i, *_: (index, 0, 0))

    def whole(*dims):
        return pl.BlockSpec(dims, lambda i: (0,) * len(dims))

    messages = shape(32, 2, 128)
    mspec = whole(32, 2, 128)
    vb, sent = call(
        start_kernel, (shape(ROWS, 128), messages),
        [SM, whole(8, B), whole(8, B), whole(WIN, 128), at((1, ROWS, B), 0), whole(AUG, B), at((1, AUG, B), 3)],
        name="start", grid=(1,), out_specs=(whole(ROWS, 128), mspec),
    )(pos, chip_in, following, pw, yt, near_u, maps_u)
    got_s = exchange(sent)
    sol, sent, acc = call(
        functools.partial(middle_kernel, blocks),
        (shape(blocks, B), messages, shape(ROWS, 128)),
        [SM] + [VM] * 10,
        [pltpu.VMEM((B, 128), F32), pltpu.VMEM((B, 128), F32)],
        name="middle",
    )(pos, got_s, near_u, maps_u, y1_u, y2_u, vb, yt, rt, cnt, osum)
    got_c = exchange(sent)
    sent, gw = call(
        return_kernel, (messages, shape(WIN, 128)),
        [
            SM, mspec, whole(AUG, B), at((1, AUG, B), 3), whole(ROWS, 128), at((1, ROWS, B), 0),
            whole(AUG, B), whole(4, AUG, B), whole(AUG, B), whole(AUG, B),
        ],
        name="return", grid=(1,), out_specs=(mspec, whole(WIN, 128)),
    )(pos, got_c, near_u, maps_u, acc, yt, near_l, maps_l, y1_l, y2_l)
    got_a = exchange(sent)
    spots = shape(32 * tracers, 1, 128)
    sent = call(
        functools.partial(window_kernel, scale), spots,
        [SM, mspec, whole(AUG, B), at((1, AUG, B), 3), whole(WIN, 128), whole(WIN, B)],
        name="window", grid=(1,), out_specs=whole(32 * tracers, 1, 128),
    )(pos, got_a, near_l, maps_l, gw, ft)
    spread_windows = lax.all_to_all(sent, ("tracer", "sub"), 0, 0)
    gradient = call(
        functools.partial(total_kernel, blocks, groups, regions_all, tracers), shape(1, regions_all), [VM],
        name="total",
    )(spread_windows)
    return (gradient.reshape(regions_all), sol[None])


def solution(mesh):
    return jax.shard_map(
        shards,
        mesh=mesh,
        in_specs=(
            P("tracer", "sub", None, None),
            P("tracer", "sub", None, None),
            P("tracer", "sub", None, None),
            P("tracer", "sub", None),
            P("sub", None),
            P(),
            P("tracer", "sub"),
            P("tracer", "sub"),
        ),
        out_specs=(P(), P("tracer", "sub", None)),
        check_vma=False,
    )
```

time: 682 us -> 149 us (0.22); the launches traced: 674 us -> 148 us
  matrix products: 395 us -> 0 us
  blocking collectives: 161 us -> 37.4 us
  local copies, waits for them, and re-layouts: 60.5 us -> 18.9 us
  Pallas kernels: 0 us -> 39.5 us
  other arithmetic: 34.2 us -> 3.56 us
  starting transfers between devices: 0.08 us -> 26.5 us
  waiting for transfers between devices: 0.05 us -> 21.5 us
  between operations: 14.5 us -> 0.89 us
  loops' own time: 8.48 us -> 0 us
    dot_general x262 -> x0, matrix products: 395 us -> none  [the longest x96 118 us: matvec(): return jnp.dot(matrix, vector, precision=exact_mode)]
    all_gather x4 -> x0, blocking collectives: 95.1 us -> none  [entering(): offsets = lax.all_gather(offset[None], 'sub', axis=0, tiled=True)]
    psum x1 -> x0, blocking collectives: 65.6 us -> none  [shards(): gradient = lax.psum(partial_gradient, ('tracer', 'sub'))]
    pallas_call x0 -> x10, Pallas kernels: none -> 39.5 us  [the longest x1 17.9 us: shards(): call(functools.partial(lines_kernel, blocks, scale), (shape(blocks, ROWS,...]
    all_to_all x0 -> x3, blocking collectives: none -> 37.4 us  [the longest x2 21.5 us: exchange(): return lax.all_to_all(a, 'sub', 0, 0)]
    scatter-add x2 -> x0, other arithmetic: 30.7 us -> none  [the longest x1 28.8 us: shards(): jax.ops.segment_sum(terms, regions.reshape(-1), num_segments=params.shape...]
    ppermute x0 -> x12, starting transfers between devices: none -> 20 us  [the longest x6 11.1 us: swap(): return lax.ppermute(a, 'sub', [(d, d ^ 1) for d in range(32)])]
    gather x3 -> x0, local copies, waits for them, and re-layouts: 18.4 us -> none  [the longest x2 16.7 us: shards(): source = source_scale * pattern * jnp.take(params, regions, axis=0)]
  transfers between devices with their start and end apart: 2 -> 13, of which waited for: 0 -> 6; matrix products, arithmetic and copies ran while one was open for 35% -> 2% of each run, Pallas kernels for 0% -> 14%
where the time goes in v1:
time: 149 us; the launch traced here: 148 us
  Pallas kernels  39.5 us (27%)
  blocking collectives  37.4 us (25%)
  starting transfers between devices  26.5 us (18%)
  waiting for transfers between devices  21.5 us (14%)
  local copies, waits for them, and re-layouts  18.9 us (13%)
  other arithmetic  3.56 us (2%)
    all_to_all x2, blocking collectives, exchange(): return lax.all_to_all(a, 'sub', 0, 0)  21.5 us
    unnamed x46, local copies, waits for them, and re-layouts  18.9 us
    pallas_call x1, Pallas kernels, shards(): call(functools.partial(lines_kernel, blocks, scale), (shape(blocks, ROWS,...  17.9 us
    all_to_all x1, blocking collectives, shards(): spread_windows = lax.all_to_all(sent, ('tracer', 'sub'), 0, 0)  16 us
    ppermute x6, starting transfers between devices, swap(): return lax.ppermute(a, 'sub', [(d, d ^ 1) for d in range(32)])  11.1 us
    ppermute x3, waiting for transfers between devices, along_x(): return lax.ppermute(a, 'sub', pairs)  10.4 us
    pallas_call x1, Pallas kernels, shards(): call(functools.partial(composites_kernel, blocks, scale), (shape(AUG, B),...  8.24 us
    all_to_all x1, starting transfers between devices, exchange(): return lax.all_to_all(a, 'sub', 0, 0)  6.53 us
  transfers between devices with their start and end apart: 13, of which 6 were waited for; matrix products, arithmetic and copies ran while one was open for 2% of the time, Pallas kernels for 14%

profile of v1, /device:TPU:1, one launch (start us, length us, event | category | flops | bytes accessed | tf_op | source)
XLA Modules:
  0.0 148.3 jit_solution(7728129672736578738)
XLA Ops:
  0.7 2.2 %copy-done.11 = f32[1,16,256,256]{3,2,1,0:T(8,128)S(1)} copy-done((f32[1,16,256,256]{3,2,1,0:T(8,128)S(1)}, f32[1,16,256,256]{3,2,1,0:T(8,128)}, u32[]{:S(2)}) %copy-start.11) | copy-done | bytes 4194328
  2.9 2.2 %copy-done.13 = f32[1,16,256,256]{3,2,1,0:T(8,128)S(1)} copy-done((f32[1,16,256,256]{3,2,1,0:T(8,128)S(1)}, f32[1,16,256,256]{3,2,1,0:T(8,128)}, u32[]{:S(2)}) %copy-start.13) | copy-done | bytes 4194328
  7.2 8.2 %composites.1 = (f32[264,256]{1,0:T(8,128)S(1)}, f32[264,256]{1,0:T(8,128)S(1)}) custom-call(s32[4]{0:T(128)S(1)} %pad_add_fusion.pos_ref, f32[600]{0:T(1024)S(1)} %copy-done.19, f32[16,256,256]{2,1,0:T(8,128)S(1)} %bitcast.9, f32[16,256,256]{2,1,0:T(8,128)S(1)} %bitcast.11, f32[16,256]{1,0:T(8,128)S(1)} %bitcast.13, s32[16,256]{1,0:T(8,128)S(1)} %copy-done.17), custom_call_target="tpu_custom_call" | custom-call | flops 3221225472 | bytes 8388608 | tf_op jit(solution)/shard_map/composites/pallas_call | solution.py:447
  15.5 1.5 %collective-permute-start = (f32[264,256]{1,0:T(8,128)S(1)}, f32[264,256]{1,0:T(8,128)S(1)}, u32[]{:S(2)}, u32[]{:S(2)}) collective-permute-start(f32[264,256]{1,0:T(8,128)S(1)} %get-tuple-element.23), channel_id=1, source_target_pairs={{0,1},{1,0},{2,3},{3,2},{4,5},{5,4},{6,7},{7,6},{8,9},{9,8},{10,11... | collective-permute-start | bytes 811016 | tf_op jit(solution)/shard_map/ppermute | solution.py:431
  18.5 1.4 collective-permute-start.3
  19.9 2.5 %collective-permute-start.2 = (f32[264,256]{1,0:T(8,128)S(1)}, f32[264,256]{1,0:T(8,128)S(1)}, u32[]{:S(2)}, u32[]{:S(2)}) collective-permute-start(f32[264,256]{1,0:T(8,128)S(1)} %chip.1.own_ref.dep_ref), channel_id=1, source_target_pairs={{0,4},{2,6},{4,0},{6,2},{8,12},{10,14},{12,8},{14,10},{16,20},{18,... | collective-permute-start | bytes 811016 | tf_op jit(solution)/shard_map/ppermute | solution.py:436
  23.5 1.6 %collective-permute-done.3.r3_ref = f32[264,256]{1,0:T(8,128)S(1)} collective-permute-done((f32[264,256]{1,0:T(8,128)S(1)}, f32[264,256]{1,0:T(8,128)S(1)}, u32[]{:S(2)}, u32[]{:S(2)}) %collective-permute-start.3) | collective-permute-done | bytes 270368 | tf_op jit(solution)/shard_map/ppermute | solution.py:436
  25.1 7.1 %collective-permute-done.2.r2_ref = f32[264,256]{1,0:T(8,128)S(1)} collective-permute-done((f32[264,256]{1,0:T(8,128)S(1)}, f32[264,256]{1,0:T(8,128)S(1)}, u32[]{:S(2)}, u32[]{:S(2)}) %collective-permute-start.2) | collective-permute-done | bytes 270368 | tf_op jit(solution)/shard_map/ppermute | solution.py:436
  32.2 1.6 %collective-permute-done.1.r1_ref = f32[264,256]{1,0:T(8,128)S(1)} collective-permute-done((f32[264,256]{1,0:T(8,128)S(1)}, f32[264,256]{1,0:T(8,128)S(1)}, u32[]{:S(2)}, u32[]{:S(2)}) %collective-permute-start.1) | collective-permute-done | bytes 270368 | tf_op jit(solution)/shard_map/ppermute | solution.py:436
  33.8 1.8 %line.1 = (f32[4,264,256]{2,1,0:T(8,128)S(1)}, f32[264,256]{1,0:T(8,128)S(1)}, f32[8,256]{1,0:T(8,128)S(1)}) custom-call(s32[4]{0:T(128)S(1)} %pad_add_fusion.pos_ref, f32[264,256]{1,0:T(8,128)S(1)} %chip.1.own_ref.dep_ref, f32[264,256]{1,0:T(8,128)S(1)} %collective-permute-done.1.r1_ref, f32[264,256]{1,0:T(8,128)S(1)} %collective-permute-done.2.r2_ref, ...), custom_call_target="tpu_custom_call" | custom-call | flops 603979776 | tf_op jit(solution)/shard_map/line/pallas_call | solution.py:474
  35.7 1.3 collective-permute-start.5
  37.0 5.6 %collective-permute-start.8 = (f32[264,256]{1,0:T(8,128)S(1)}, f32[264,256]{1,0:T(8,128)S(1)}, u32[]{:S(2)}, u32[]{:S(2)}) collective-permute-start(f32[264,256]{1,0:T(8,128)S(1)} %get-tuple-element.22.own_ref), channel_id=1, source_target_pairs={{0,1},{1,0},{2,3},{3,2},{4,5},{5,4},{6,7},{7,6},{8,9},{9,8},{10,11... | collective-permute-start | bytes 811016 | tf_op jit(solution)/shard_map/ppermute | solution.py:431
  42.6 1.3 collective-permute-start.4
  43.9 2.0 %collective-permute-start.9 = (f32[4,264,256]{2,1,0:T(8,128)S(1)}, f32[4,264,256]{2,1,0:T(8,128)S(1)}, u32[]{:S(2)}, u32[]{:S(2)}) collective-permute-start(f32[4,264,256]{2,1,0:T(8,128)S(1)} %get-tuple-element.24.maps_ref), channel_id=1, source_target_pairs={{0,1},{1,0},{2,3},{3,2},{4,5},{5,4},{6,7},{7,6},{8,9},{9,8},{10,11... | collective-permute-start | bytes 3244040 | tf_op jit(solution)/shard_map/ppermute | solution.py:431
  46.5 2.2 %copy-done.12 = f32[1,16,256,256]{3,2,1,0:T(8,128)S(1)} copy-done((f32[1,16,256,256]{3,2,1,0:T(8,128)S(1)}, f32[1,16,256,256]{3,2,1,0:T(8,128)}, u32[]{:S(2)}) %copy-start.12) | copy-done | bytes 4194328
  48.7 2.2 %copy-done.14 = f32[1,16,256,256]{3,2,1,0:T(8,128)S(1)} copy-done((f32[1,16,256,256]{3,2,1,0:T(8,128)S(1)}, f32[1,16,256,256]{3,2,1,0:T(8,128)}, u32[]{:S(2)}) %copy-start.14) | copy-done | bytes 4194328
  50.9 17.9 %lines.1 = (f32[16,288,256]{2,1,0:T(8,128)}, f32[16,256,256]{2,1,0:T(8,128)S(1)}, f32[32,256]{1,0:T(8,128)S(1)}, f32[16,256]{1,0:T(8,128)S(1)}, f32[16,256]{1,0:T(8,128)S(1)}, /*index=5*/f32[32,128]{1,0:T(8,128)S(1)}) custom-call(s32[4]{0:T(128)S(1)} %pad_add_fusion.pos_ref, f32[600]{0:T(1024)S(1)} %copy-done.20, f32[16,256,256]{2,1,0:T(8,128)S(1)} %bitcast.10, ...), custom_call_target="tpu_custom_call" | custom-call | flops 6442450944 | bytes 22020096 | tf_op jit(solution)/shard_map/lines/pallas_call | solution.py:461
  68.8 2.0 %copy-done.2 = f32[16,256,256]{2,1,0:T(8,128)} copy-done((f32[16,256,256]{2,1,0:T(8,128)}, f32[16,256,256]{2,1,0:T(8,128)S(1)}, u32[]{:S(2)}) %copy-start.2) | copy-done | bytes 4194328
  72.9 3.8 %collective-permute-done.6.t3_ref = f32[8,256]{1,0:T(8,128)S(1)} collective-permute-done((f32[8,256]{1,0:T(8,128)S(1)}, f32[8,256]{1,0:T(8,128)S(1)}, u32[]{:S(2)}, u32[]{:S(2)}) %collective-permute-start.6) | collective-permute-done | bytes 8224 | tf_op jit(solution)/shard_map/ppermute | solution.py:441
  76.7 1.5 entering.1
  78.1 1.3 collective-permute-start.7
  80.7 1.4 copy-done
  82.1 1.6 %start.1 = (f32[288,128]{1,0:T(8,128)S(1)}, f32[32,2,128]{2,1,0:T(2,128)}) custom-call(s32[4]{0:T(128)S(1)} %pad_add_fusion.pos_ref, f32[8,256]{1,0:T(8,128)S(1)} %get-tuple-element.27.chip_ref, f32[8,256]{1,0:T(8,128)S(1)} %collective-permute-done.7.got_ref, f32[32,128]{1,0:T(8,128)S(1)} %get-tuple-element.29.pw_ref, f32[16,288,256]{2,1,0:T(8,128)S(1)} %copy-done, ...), custom_call_target="tpu_custom_call" | custom-call | tf_op jit(solution)/shard_map/start/pallas_call | solution.py:498
  83.7 6.5 %all-to-all-start = ((f32[32,2,128]{2,1,0:T(2,128)}), f32[32,2,128]{2,1,0:T(2,128)S(1)}, u32[]{:S(2)}, u32[]{:S(2)}) async-start(f32[32,2,128]{2,1,0:T(2,128)} %get-tuple-element.31), calls=%async_computation | async-start | bytes 65536 | tf_op jit(solution)/shard_map/all_to_all | solution.py:444
  91.3 6.2 %all-to-all-done.got_ref = f32[32,2,128]{2,1,0:T(2,128)S(1)} async-done(((f32[32,2,128]{2,1,0:T(2,128)}), f32[32,2,128]{2,1,0:T(2,128)S(1)}, u32[]{:S(2)}, u32[]{:S(2)}) %all-to-all-start) | async-done | bytes 32800 | tf_op jit(solution)/shard_map/all_to_all | solution.py:444
  97.5 2.3 %copy-done.1 = f32[16,288,256]{2,1,0:T(8,128)S(1)} copy-done((f32[16,288,256]{2,1,0:T(8,128)S(1)}, f32[16,288,256]{2,1,0:T(8,128)}, u32[]{:S(2)}) %copy-start.1) | copy-done | bytes 4718616
  99.8 2.2 %copy-done.3 = f32[16,256,256]{2,1,0:T(8,128)S(1)} copy-done((f32[16,256,256]{2,1,0:T(8,128)S(1)}, f32[16,256,256]{2,1,0:T(8,128)}, u32[]{:S(2)}) %copy-start.3) | copy-done | bytes 4194328
  102.0 5.2 %middle.1 = (f32[16,256]{1,0:T(8,128)}, f32[32,2,128]{2,1,0:T(2,128)S(1)}, f32[288,128]{1,0:T(8,128)S(1)}) custom-call(s32[4]{0:T(128)S(1)} %pad_add_fusion.pos_ref, f32[32,2,128]{2,1,0:T(2,128)S(1)} %all-to-all-done.got_ref, f32[264,256]{1,0:T(8,128)S(1)} %get-tuple-element.49.near_ref.nearu_ref, ...), custom_call_target="tpu_custom_call" | custom-call | tf_op jit(solution)/shard_map/middle/pallas_call | solution.py:504
  107.2 10.7 %all_to_all.20.got_ref = f32[32,2,128]{2,1,0:T(2,128)S(1)} all-to-all(f32[32,2,128]{2,1,0:T(2,128)S(1)} %get-tuple-element.36), channel_id=1, replica_groups=mesh['tracer'=4,'sub'=32] {'sub'}, dimensions={0} | all-to-all | bytes 65536 | tf_op jit(solution)/shard_map/all_to_all | solution.py:444
  117.9 1.9 %return.1 = (f32[32,2,128]{2,1,0:T(2,128)S(1)}, f32[32,128]{1,0:T(8,128)S(1)}) custom-call(s32[4]{0:T(128)S(1)} %pad_add_fusion.pos_ref, f32[32,2,128]{2,1,0:T(2,128)S(1)} %all_to_all.20.got_ref, f32[264,256]{1,0:T(8,128)S(1)} %get-tuple-element.49.near_ref.nearu_ref, f32[4,264,256]{2,1,0:T(8,128)S(1)} %get-tuple-element.43.suf_ref.maps_ref.sufu_ref, ...), custom_call_target="tpu_custom_call" | custom-call | tf_op jit(solution)/shard_map/return/pallas_call | solution.py:512
  119.8 10.7 %all_to_all.21.got_ref = f32[32,2,128]{2,1,0:T(2,128)S(1)} all-to-all(f32[32,2,128]{2,1,0:T(2,128)S(1)} %get-tuple-element.38), channel_id=1, replica_groups=mesh['tracer'=4,'sub'=32] {'sub'}, dimensions={0} | all-to-all | bytes 65536 | tf_op jit(solution)/shard_map/all_to_all | solution.py:444
  131.7 16.0 %all_to_all.22.got_ref = f32[128,1,128]{2,1,0:T(1,128)S(1)} all-to-all(f32[128,1,128]{2,1,0:T(1,128)S(1)} %window.1), channel_id=1, replica_groups=mesh['tracer'=4,'sub'=32] {'tracer','sub'}, dimensions={0} | all-to-all | bytes 131072 | tf_op jit(solution)/shard_map/all_to_all | solution.py:527
  (59 shorter events, 11.4 us)
Async XLA Ops:
  0.7 2.2 %copy-start.11 = (f32[1,16,256,256]{3,2,1,0:T(8,128)S(1)}, f32[1,16,256,256]{3,2,1,0:T(8,128)}, u32[]{:S(2)}) copy-start(f32[1,16,256,256]{3,2,1,0:T(8,128)} %param.8) | copy-start | bytes 12582916
  2.9 2.2 %copy-start.13 = (f32[1,16,256,256]{3,2,1,0:T(8,128)S(1)}, f32[1,16,256,256]{3,2,1,0:T(8,128)}, u32[]{:S(2)}) copy-start(f32[1,16,256,256]{3,2,1,0:T(8,128)} %param.10) | copy-start | bytes 12582916
  15.5 2.7 %collective-permute-start = (f32[264,256]{1,0:T(8,128)S(1)}, f32[264,256]{1,0:T(8,128)S(1)}, u32[]{:S(2)}, u32[]{:S(2)}) collective-permute-start(f32[264,256]{1,0:T(8,128)S(1)} %get-tuple-element.23), channel_id=1, source_target_pairs={{0,1},{1,0},{2,3},{3,2},{4,5},{5,4},{6,7},{7,6},{8,9},{9,8},{10,11... | collective-permute-start | bytes 811016 | tf_op jit(solution)/shard_map/ppermute | solution.py:431
  18.4 28.0 %copy-start.16 = (f32[1,16,256]{2,1,0:T(8,128)S(1)}, f32[1,16,256]{2,1,0:T(8,128)}, u32[]{:S(2)}) copy-start(f32[1,16,256]{2,1,0:T(8,128)} %param.11) | copy-start | bytes 49156
  18.5 28.0 %copy-start.18 = (s32[16,256]{1,0:T(8,128)S(1)}, s32[16,256]{1,0:T(8,128)}, u32[]{:S(2)}) copy-start(s32[16,256]{1,0:T(8,128)} %reg_ref.3) | copy-start | bytes 49156
  18.5 28.0 %copy-start.20 = (f32[600]{0:T(1024)S(1)}, f32[600]{0:T(1024)}, u32[]{:S(2)}) copy-start(f32[600]{0:T(1024)} %par_ref.3) | copy-start | bytes 7204
  18.5 28.0 %copy-start.21 = (s32[1,256]{1,0:T(1,128)S(1)}, s32[1,256]{1,0:T(1,128)}, u32[]{:S(2)}) copy-start(s32[1,256]{1,0:T(1,128)} %cells_ref.1) | copy-start | bytes 3076
  18.5 28.0 %copy-start.22 = (f32[1,256]{1,0:T(1,128)S(1)}, f32[1,256]{1,0:T(1,128)}, u32[]{:S(2)}) copy-start(f32[1,256]{1,0:T(1,128)} %values_ref.1) | copy-start | bytes 3076
  18.5 6.6 %collective-permute-start.3 = (f32[264,256]{1,0:T(8,128)S(1)}, f32[264,256]{1,0:T(8,128)S(1)}, u32[]{:S(2)}, u32[]{:S(2)}) collective-permute-start(f32[264,256]{1,0:T(8,128)S(1)} %chip.1.own_ref.dep_ref), channel_id=1, source_target_pairs={{0,6},{2,0},{4,2},{6,4},{8,14},{10,8},{12,10},{14,12},{16,22},{18,... | collective-permute-start | bytes 811016 | tf_op jit(solution)/shard_map/ppermute | solution.py:436
  19.9 12.4 %collective-permute-start.2 = (f32[264,256]{1,0:T(8,128)S(1)}, f32[264,256]{1,0:T(8,128)S(1)}, u32[]{:S(2)}, u32[]{:S(2)}) collective-permute-start(f32[264,256]{1,0:T(8,128)S(1)} %chip.1.own_ref.dep_ref), channel_id=1, source_target_pairs={{0,4},{2,6},{4,0},{6,2},{8,12},{10,14},{12,8},{14,10},{16,20},{18,... | collective-permute-start | bytes 811016 | tf_op jit(solution)/shard_map/ppermute | solution.py:436
  22.3 11.5 %collective-permute-start.1 = (f32[264,256]{1,0:T(8,128)S(1)}, f32[264,256]{1,0:T(8,128)S(1)}, u32[]{:S(2)}, u32[]{:S(2)}) collective-permute-start(f32[264,256]{1,0:T(8,128)S(1)} %chip.1.own_ref.dep_ref), channel_id=1, source_target_pairs={{0,2},{2,4},{4,6},{6,0},{8,10},{10,12},{12,14},{14,8},{16,18},{18,... | collective-permute-start | bytes 811016 | tf_op jit(solution)/shard_map/ppermute | solution.py:436
  35.7 10.2 %collective-permute-start.5 = (f32[264,256]{1,0:T(8,128)S(1)}, f32[264,256]{1,0:T(8,128)S(1)}, u32[]{:S(2)}, u32[]{:S(2)}) collective-permute-start(f32[264,256]{1,0:T(8,128)S(1)} %get-tuple-element.25), channel_id=1, source_target_pairs={{0,16},{2,18},{4,20},{6,22},{8,24},{10,26},{12,28},{14,30},{17,1},... | collective-permute-start | bytes 811016 | tf_op jit(solution)/shard_map/ppermute | solution.py:441
  37.0 35.1 %collective-permute-start.8 = (f32[264,256]{1,0:T(8,128)S(1)}, f32[264,256]{1,0:T(8,128)S(1)}, u32[]{:S(2)}, u32[]{:S(2)}) collective-permute-start(f32[264,256]{1,0:T(8,128)S(1)} %get-tuple-element.22.own_ref), channel_id=1, source_target_pairs={{0,1},{1,0},{2,3},{3,2},{4,5},{5,4},{6,7},{7,6},{8,9},{9,8},{10,11... | collective-permute-start | bytes 811016 | tf_op jit(solution)/shard_map/ppermute | solution.py:431
  42.6 34.0 %collective-permute-start.4 = (f32[264,256]{1,0:T(8,128)S(1)}, f32[264,256]{1,0:T(8,128)}, u32[]{:S(2)}, u32[]{:S(2)}) collective-permute-start(f32[264,256]{1,0:T(8,128)S(1)} %get-tuple-element.25), channel_id=1, source_target_pairs={{0,8},{2,10},{4,12},{6,14},{8,16},{10,18},{12,20},{14,22},{16,24},... | collective-permute-start | bytes 811016 | tf_op jit(solution)/shard_map/ppermute | solution.py:441
  43.9 36.5 %collective-permute-start.9 = (f32[4,264,256]{2,1,0:T(8,128)S(1)}, f32[4,264,256]{2,1,0:T(8,128)S(1)}, u32[]{:S(2)}, u32[]{:S(2)}) collective-permute-start(f32[4,264,256]{2,1,0:T(8,128)S(1)} %get-tuple-element.24.maps_ref), channel_id=1, source_target_pairs={{0,1},{1,0},{2,3},{3,2},{4,5},{5,4},{6,7},{7,6},{8,9},{9,8},{10,11... | collective-permute-start | bytes 3244040 | tf_op jit(solution)/shard_map/ppermute | solution.py:431
  45.9 33.6 %collective-permute-start.11 = (f32[264,256]{1,0:T(8,128)S(1)}, f32[264,256]{1,0:T(8,128)S(1)}, u32[]{:S(2)}, u32[]{:S(2)}) collective-permute-start(f32[264,256]{1,0:T(8,128)S(1)} %collective-permute-done.5.y2_ref), channel_id=1, source_target_pairs={{0,1},{1,0},{2,3},{3,2},{4,5},{5,4},{6,7},{7,6},{8,9},{9,8},{10,11... | collective-permute-start | bytes 811016 | tf_op jit(solution)/shard_map/ppermute | solution.py:431
  46.5 2.2 %copy-start.12 = (f32[1,16,256,256]{3,2,1,0:T(8,128)S(1)}, f32[1,16,256,256]{3,2,1,0:T(8,128)}, u32[]{:S(2)}) copy-start(f32[1,16,256,256]{3,2,1,0:T(8,128)} %param.8) | copy-start | bytes 12582916
  48.7 2.2 %copy-start.14 = (f32[1,16,256,256]{3,2,1,0:T(8,128)S(1)}, f32[1,16,256,256]{3,2,1,0:T(8,128)}, u32[]{:S(2)}) copy-start(f32[1,16,256,256]{3,2,1,0:T(8,128)} %param.10) | copy-start | bytes 12582916
  70.9 7.3 %copy-start.7 = (f32[16,256]{1,0:T(8,128)}, f32[16,256]{1,0:T(8,128)S(1)}, u32[]{:S(2)}) copy-start(f32[16,256]{1,0:T(8,128)S(1)} %get-tuple-element.34.cnt_ref) | copy-start | bytes 49156
  70.9 7.3 %copy-start.9 = (f32[16,256]{1,0:T(8,128)}, f32[16,256]{1,0:T(8,128)S(1)}, u32[]{:S(2)}) copy-start(f32[16,256]{1,0:T(8,128)S(1)} %get-tuple-element.35.sum_ref) | copy-start | bytes 49156
  70.9 5.8 %collective-permute-start.6 = (f32[8,256]{1,0:T(8,128)S(1)}, f32[8,256]{1,0:T(8,128)S(1)}, u32[]{:S(2)}, u32[]{:S(2)}) collective-permute-start(f32[8,256]{1,0:T(8,128)S(1)} %get-tuple-element.26), channel_id=1, source_target_pairs={{0,24},{2,26},{4,28},{6,30},{25,1},{27,3},{29,5},{31,7},{32,56},{3... | collective-permute-start | bytes 24584 | tf_op jit(solution)/shard_map/ppermute | solution.py:441
  78.1 2.5 %collective-permute-start.7 = (f32[8,256]{1,0:T(8,128)S(1)}, f32[8,256]{1,0:T(8,128)S(1)}, u32[]{:S(2)}, u32[]{:S(2)}) collective-permute-start(f32[8,256]{1,0:T(8,128)S(1)} %get-tuple-element.28), channel_id=1, source_target_pairs={{0,1},{1,0},{2,3},{3,2},{4,5},{5,4},{6,7},{7,6},{8,9},{9,8},{10,11... | collective-permute-start | bytes 24584 | tf_op jit(solution)/shard_map/ppermute | solution.py:431
  79.5 10.7 %collective-permute-start.10 = (f32[264,256]{1,0:T(8,128)}, f32[264,256]{1,0:T(8,128)}, u32[]{:S(2)}, u32[]{:S(2)}) collective-permute-start(f32[264,256]{1,0:T(8,128)} %collective-permute-done.4.y1_ref), channel_id=1, source_target_pairs={{0,1},{1,0},{2,3},{3,2},{4,5},{5,4},{6,7},{7,6},{8,9},{9,8},{10,11... | collective-permute-start | bytes 811016 | tf_op jit(solution)/shard_map/ppermute | solution.py:431
  79.6 2.5 %copy-start = (f32[16,288,256]{2,1,0:T(8,128)S(1)}, f32[16,288,256]{2,1,0:T(8,128)}, u32[]{:S(2)}) copy-start(f32[16,288,256]{2,1,0:T(8,128)} %get-tuple-element.30.y0_ref.y_ref) | copy-start | bytes 14155780
  83.7 13.8 %copy-start.5 = (f32[264,256]{1,0:T(8,128)S(1)}, f32[264,256]{1,0:T(8,128)}, u32[]{:S(2)}) copy-start(f32[264,256]{1,0:T(8,128)} %get-tuple-element.45.d2_ref) | copy-start | bytes 811012
  83.7 13.8 %copy-start.8 = (f32[16,256]{1,0:T(8,128)S(1)}, f32[16,256]{1,0:T(8,128)}, u32[]{:S(2)}) copy-start(f32[16,256]{1,0:T(8,128)} %copy-done.7) | copy-start | bytes 49156
  83.7 13.8 %copy-start.10 = (f32[16,256]{1,0:T(8,128)S(1)}, f32[16,256]{1,0:T(8,128)}, u32[]{:S(2)}) copy-start(f32[16,256]{1,0:T(8,128)} %copy-done.9) | copy-start | bytes 49156
  83.7 13.8 %all-to-all-start = ((f32[32,2,128]{2,1,0:T(2,128)}), f32[32,2,128]{2,1,0:T(2,128)S(1)}, u32[]{:S(2)}, u32[]{:S(2)}) async-start(f32[32,2,128]{2,1,0:T(2,128)} %get-tuple-element.31), calls=%async_computation | async-start | bytes 65536 | tf_op jit(solution)/shard_map/all_to_all | solution.py:444
  97.5 2.3 %copy-start.1 = (f32[16,288,256]{2,1,0:T(8,128)S(1)}, f32[16,288,256]{2,1,0:T(8,128)}, u32[]{:S(2)}) copy-start(f32[16,288,256]{2,1,0:T(8,128)} %get-tuple-element.30.y0_ref.y_ref) | copy-start | bytes 14155780
  99.8 2.2 %copy-start.3 = (f32[16,256,256]{2,1,0:T(8,128)S(1)}, f32[16,256,256]{2,1,0:T(8,128)}, u32[]{:S(2)}) copy-start(f32[16,256,256]{2,1,0:T(8,128)} %copy-done.2) | copy-start | bytes 12582916
  102.0 15.9 %copy-start.4 = (f32[264,256]{1,0:T(8,128)S(1)}, f32[264,256]{1,0:T(8,128)}, u32[]{:S(2)}) copy-start(f32[264,256]{1,0:T(8,128)} %get-tuple-element.48.nearl_ref.near_ref) | copy-start | bytes 811012
  102.0 15.9 %copy-start.6 = (f32[264,256]{1,0:T(8,128)S(1)}, f32[264,256]{1,0:T(8,128)}, u32[]{:S(2)}) copy-start(f32[264,256]{1,0:T(8,128)} %get-tuple-element.44.d2_ref) | copy-start | bytes 811012
  (4 other events, 4.2 us)

commit v2 on v1

v2 whole, which is shorter than its diff:
```python
import functools

import jax
import jax.numpy as jnp
from jax import lax
from jax.experimental import pallas as pl
from jax.experimental.pallas import tpu as pltpu
from jax.sharding import PartitionSpec as P

F32 = jnp.float32
BF16 = jnp.bfloat16
B = 256
AUG = 264
WIN = 32
ROWS = B + WIN
NT = (((1,), (1,)), ((), ()))
NN = (((1,), (0,)), ((), ()))
MIB = 1 << 20
UNROLL = True
VM = pl.BlockSpec(memory_space=pltpu.VMEM)
SM = pl.BlockSpec(memory_space=pltpu.SMEM)
ANY = pl.BlockSpec(memory_space=pl.ANY)
HBM = pl.BlockSpec(memory_space=pltpu.HBM)


def split(a):
    high = a.astype(BF16)
    return high, (a - high.astype(F32)).astype(BF16)


def dot3(a, b, dims):
    ah, al = split(a)
    bh, bl = split(b)
    return lax.dot_general(
        jnp.concatenate([ah, ah, al], axis=1),
        jnp.concatenate([bh, bl, bh], axis=dims[0][1][0]),
        dims,
        preferred_element_type=F32,
    )


def unit():
    i = lax.broadcasted_iota(jnp.int32, (B, B), 0)
    return jnp.where(i == lax.broadcasted_iota(jnp.int32, (B, B), 1), 1.0, 0.0)


def advance(a, b, dims=NT):
    return a + dot3(a, b - unit(), dims)


def affine(first, second):
    product = advance(first, second[:B], NN)
    return jnp.concatenate([product[:B], product[B:] + second[B:]], axis=0)


def spread(row):
    return jnp.broadcast_to(row, (128, row.shape[1])).T


def apply(row, mt):
    vb = spread(row)
    return jnp.concatenate(
        [
            jnp.sum(vb * mt[:, :128], axis=0, keepdims=True),
            jnp.sum(vb * mt[:, 128:], axis=0, keepdims=True),
        ],
        axis=1,
    )


def adjoint_column(row, mt):
    acc = mt[:, :128] * row[:, :128] + mt[:, 128:] * row[:, 128:]
    return jnp.sum(acc, axis=1, keepdims=True)


def to_row(column):
    return jnp.broadcast_to(column, (column.shape[0], 128)).T[0:1]


def apply_t(row, mt):
    return to_row(adjoint_column(row, mt))


def place():
    sub = lax.axis_index("sub")
    return sub >> 3, (sub >> 1) & 3, sub & 1


def window_base(blocks, regions):
    groups = blocks * lax.axis_size("sub")
    return (lax.axis_index("sub") * (blocks * regions)) // groups - 3


def row_coords():
    i = lax.broadcasted_iota(jnp.int32, (32, 128), 0)
    return i >> 3, (i >> 1) & 3, i & 1


def scatter_rows(out_ref, pieces):
    for half in range(2):
        total = jnp.zeros((32, 128), F32)
        for mask, row in pieces:
            total = total + jnp.where(mask, row[:, half * 128 : half * 128 + 128], 0.0)
        out_ref[:, half, :] = total


def gather_rows(ref, masks):
    halves = [ref[:, 0, :], ref[:, 1, :]]
    return [
        jnp.concatenate(
            [jnp.sum(jnp.where(m, h, 0.0), axis=0, keepdims=True) for h in halves], axis=1
        )
        for m in masks
    ]


def source_window(k, reg_ref, pat_ref, base, scale):
    rel = reg_ref[pl.ds(k, 1), :] - base
    w = lax.broadcasted_iota(jnp.int32, (WIN, B), 0)
    return jnp.where(w == rel, scale * pat_ref[pl.ds(k, 1), :], 0.0)


def composites_kernel(
    blocks, scale, low_hbm, up_hbm, pat_hbm, reg_hbm, par_hbm,
    own_ref, send_ref, low, up, pat, reg, par, src, xa, xb, ra, rb, sems, small
):
    half = blocks // 2
    last = blocks - 1

    def copies(k):
        return (
            pltpu.make_async_copy(low_hbm.at[k], low.at[k], sems.at[0, k]),
            pltpu.make_async_copy(up_hbm.at[last - k], up.at[last - k], sems.at[1, k]),
        )

    extras = (
        pltpu.make_async_copy(par_hbm, par, small.at[0]),
        pltpu.make_async_copy(reg_hbm, reg, small.at[1]),
        pltpu.make_async_copy(pat_hbm, pat, small.at[2]),
    )
    for c in extras:
        c.start()
    for k in range(half):
        for c in copies(k) + copies(k + half):
            c.start()
    y, x, core = place()
    count = par.shape[0]
    base = window_base(blocks, count)
    for c in extras:
        c.wait()
    rel = reg[...] - base
    value = jnp.zeros((blocks, B), F32)
    for w in range(WIN):
        value = jnp.where(rel == w, par[jnp.clip(base + w, 0, count - 1)], value)
    src[...] = scale * pat[...] * value
    for c in copies(0) + copies(half):
        c.wait()
    xa[...] = jnp.concatenate([low[0].T, jnp.broadcast_to(src[0:1, :], (8, B))], axis=0)
    xb[...] = jnp.concatenate([low[half].T, jnp.broadcast_to(src[half : half + 1, :], (8, B))], axis=0)
    ra[...] = up[last].T
    rb[...] = up[last - half].T

    def step(k, carry):
        for c in copies(k) + copies(k + half):
            c.wait()
        a = advance(xa[...], low[k])
        b = advance(xb[...], low[k + half])
        c = advance(ra[...], up[last - k])
        d = advance(rb[...], up[last - half - k])
        xa[:B, :] = a[:B]
        xa[B:, :] = a[B:] + src[pl.ds(k, 1), :]
        xb[:B, :] = b[:B]
        xb[B:, :] = b[B:] + src[pl.ds(k + half, 1), :]
        ra[...] = c
        rb[...] = d
        return carry

    lax.fori_loop(1, half, step, 0, unroll=UNROLL)
    xs = affine(xa[...], xb[...])
    rs = advance(ra[...], rb[...], NN)
    zero = jnp.zeros((8, B), F32)

    @pl.when(core == 0)
    def _():
        own_ref[...] = xs
        send_ref[:B, :] = rs
        send_ref[B:, :] = zero

    @pl.when(core != 0)
    def _():
        send_ref[...] = xs
        own_ref[:B, :] = rs
        own_ref[B:, :] = zero


def chip_kernel(own_ref, got_ref, out_ref):
    out_ref[...] = affine(own_ref[...], got_ref[...])


def prefixes_kernel(
    blocks, scale, low_hbm, up_hbm, pat_ref, reg_ref, par_ref, cells_ref, values_ref, dep_ref,
    x_ref, r_ref, cnt_ref, sum_ref, pw_ref, low, up, sems
):
    last = blocks - 1
    y, x, core = place()

    def copies(k):
        return (
            pltpu.make_async_copy(low_hbm.at[k], low.at[k], sems.at[0, k]),
            pltpu.make_async_copy(up_hbm.at[last - k], up.at[last - k], sems.at[1, k]),
        )

    for k in range(blocks):
        for c in copies(k):
            c.start()
    count = par_ref.shape[0]
    base = window_base(blocks, count)
    local = cells_ref[...] - ((y * 4 + x) * 2 + core) * (blocks * B)
    high = local >> 8
    low_part = local & 255
    which = jnp.where(lax.broadcasted_iota(jnp.int32, (blocks, B), 0) == high, 1.0, 0.0)
    slot = jnp.where(lax.broadcasted_iota(jnp.int32, (B, B), 0) == low_part, 1.0, 0.0).astype(BF16)
    weighted = which * values_ref[...]
    v1 = weighted.astype(BF16)
    v2, v3 = split(weighted - v1.astype(F32))
    d = functools.partial(lax.dot_general, dimension_numbers=NT, preferred_element_type=F32)
    cnt_ref[...] = d(which.astype(BF16), slot)
    sum_ref[...] = d(v1, slot) + (d(v2, slot) + d(v3, slot))
    wi = lax.broadcasted_iota(jnp.int32, (WIN, 128), 0)
    window = jnp.zeros((WIN, 128), F32)
    for w in range(WIN):
        window = jnp.where(wi == w, par_ref[jnp.clip(base + w, 0, count - 1)], window)
    pw_ref[...] = window

    for c in copies(0):
        c.wait()
    x_ref[0] = jnp.concatenate([low[0].T, source_window(0, reg_ref, pat_ref, base, scale)], axis=0)
    r_ref[last] = up[last].T

    def step(k, carry):
        for c in copies(k):
            c.wait()
        moved = advance(x_ref[k - 1], low[k])
        r_ref[last - k] = advance(r_ref[last - k + 1], up[last - k])
        x_ref[k, :B, :] = moved[:B]
        x_ref[k, B:, :] = moved[B:] + source_window(k, reg_ref, pat_ref, base, scale)
        return carry

    lax.fori_loop(1, blocks, step, 0, unroll=UNROLL)


def lines_kernel(blocks, up_hbm, piv_hbm, x_ref, dep_ref, y_ref, token_ref, up, piv, sems):
    last = blocks - 1

    def copies(k):
        return (
            pltpu.make_async_copy(up_hbm.at[k], up.at[k], sems.at[0, k]),
            pltpu.make_async_copy(piv_hbm.at[k], piv.at[k], sems.at[1, k]),
        )

    for i in range(blocks):
        for c in copies(last - i):
            c.start()
    for c in copies(last):
        c.wait()
    y_ref[last] = dot3(x_ref[last], piv[last], NT)

    def back(i, carry):
        k = last - i
        for c in copies(k):
            c.wait()
        y_ref[k] = dot3(x_ref[k], piv[k], NT) + advance(y_ref[k + 1], up[k])
        return carry

    lax.fori_loop(1, blocks, back, 0, unroll=UNROLL)
    token_ref[...] = jnp.zeros((8, 128), F32)


def line_kernel(own_ref, r1_ref, r2_ref, r3_ref, dep_ref, maps_ref, row_ref, tail_ref):
    y, x, core = place()
    p = jnp.where(core == 0, x, 3 - x)
    i = lax.broadcasted_iota(jnp.int32, (AUG, B), 0)
    j = lax.broadcasted_iota(jnp.int32, (AUG, B), 1)
    eye = jnp.where(i == j, 1.0, 0.0)
    r1, r2, r3 = r1_ref[...], r2_ref[...], r3_ref[...]
    maps_ref[0] = jnp.where(p >= 1, r1, eye)
    maps_ref[1] = jnp.where(p >= 2, r2, eye)
    pre = affine(jnp.where(p >= 3, r3, eye), maps_ref[1])
    suf = affine(jnp.where(p <= 2, r3, eye), jnp.where(p <= 1, r2, eye))
    maps_ref[2] = affine(pre, maps_ref[0])
    maps_ref[3] = affine(suf, jnp.where(p <= 0, r1, eye))
    row_ref[...] = affine(affine(maps_ref[2], own_ref[...]), maps_ref[3])
    tail_ref[...] = row_ref[B:, :]


def entering_kernel(own_ref, maps_ref, y1_ref, y2_ref, t3_ref, dep_ref, chip_ref, next_ref):
    y, x, core = place()
    t1 = jnp.where(y >= 1, y1_ref[B : B + 1, :], 0.0)
    t2 = jnp.where(y >= 2, y2_ref[B : B + 1, :], 0.0)
    t3 = jnp.where(y >= 3, t3_ref[0:1, :], 0.0)
    row = t1 + apply(t2 + apply(t3, y2_ref[:B, :]), y1_ref[:B, :])
    chip = maps_ref[2, B : B + 1, :] + apply(row, maps_ref[2, :B, :])
    following = own_ref[B : B + 1, :] + apply(chip, own_ref[:B, :])
    chip_ref[...] = jnp.broadcast_to(chip, (8, B))
    next_ref[...] = jnp.broadcast_to(following, (8, B))


def start_kernel(chip_ref, got_ref, pw_ref, y_ref, near0_ref, near1_ref, maps_ref, mapso_ref, dep1_ref, dep2_ref, in_ref, out_ref):
    my_y, my_x, core = place()
    entering = jnp.where(core == 0, chip_ref[0:1, :], got_ref[0:1, :])
    vb = jnp.concatenate([spread(entering), pw_ref[...]], axis=0)
    in_ref[...] = vb
    v = jnp.concatenate(
        [
            jnp.sum(vb * y_ref[0, :, :128], axis=0, keepdims=True),
            jnp.sum(vb * y_ref[0, :, 128:], axis=0, keepdims=True),
        ],
        axis=1,
    )
    z1 = jnp.where(core == 1, apply(v, near1_ref[:B, :]), v)
    z2 = apply(z1, jnp.where(core == 1, maps_ref[3, :B, :], mapso_ref[3, :B, :]))
    ty, tx, tc = row_coords()
    same = ty == my_y
    scatter_rows(
        out_ref,
        [
            (same & (tx == my_x) & (tc < core), v),
            (same & (tx < my_x), z1),
            (ty < my_y, z2),
        ],
    )


class Maps:
    def __init__(self, core, side, near, maps, steps):
        self.mine = core == side
        self.near_refs, self.map_refs, self.step_refs = near, maps, steps

    def near(self):
        return jnp.where(self.mine, self.near_refs[0][:B, :], self.near_refs[1][:B, :])

    def line(self, i):
        return jnp.where(self.mine, self.map_refs[0][i, :B, :], self.map_refs[1][i, :B, :])

    def step(self, j):
        mine, other = self.step_refs[j - 1]
        return jnp.where(self.mine, mine[:B, :], other[:B, :])


def spread_out(out_ref, first, m, leftward):
    my_y, my_x, core = place()
    side = 1 if leftward else 0
    g = jnp.where(core == side, apply_t(first, m.near()), first)
    g2 = apply_t(g, m.line(0))
    g3 = apply_t(g2, m.line(1))
    h = apply_t(g, m.line(2))
    h2 = apply_t(h, m.step(1))
    h3 = apply_t(h2, m.step(2))
    ty, tx, tc = row_coords()
    sign = -1 if leftward else 1
    dy, dx, dc = sign * (ty - my_y), sign * (tx - my_x), sign * (tc - core)
    same = dy == 0
    scatter_rows(
        out_ref,
        [
            (same & (dx == 0) & (dc > 0), first),
            (same & (dx == 1), g),
            (same & (dx == 2), g2),
            (same & (dx == 3), g3),
            (dy == 1, h),
            (dy == 2, h2),
            (dy == 3, h3),
        ],
    )


def collect(got_ref, m, leftward):
    my_y, my_x, core = place()
    sy, sx, sc = row_coords()
    same = sy == my_y
    part, mx, my = gather_rows(got_ref, [same & (sx == my_x), same & (sx != my_x), sy != my_y])
    total = mx + apply_t(my, m.line(3))
    side = 0 if leftward else 1
    return part + jnp.where(core == side, apply_t(total, m.near()), total)


def middle_kernel(
    blocks, got_ref, got0_ref, other_ref, maps_ref, mapso_ref, y1_ref, y1o_ref, y2_ref, y2o_ref,
    in_ref, y_ref, r_ref, cnt_ref, sum_ref, sol_ref, out_ref, acc_ref, sb, acc_r
):
    my_y, my_x, core = place()
    m = Maps(core, 1, (got0_ref, other_ref), (maps_ref, mapso_ref), ((y1_ref, y1o_ref), (y2_ref, y2o_ref)))
    sy, sx, sc = row_coords()
    same = sy == my_y
    part, t1, t2, t3, y1, y2, y3 = gather_rows(
        got_ref,
        [same & (sx == my_x)]
        + [same & (sx == my_x + j) for j in (1, 2, 3)]
        + [sy == my_y + j for j in (1, 2, 3)],
    )
    yv = y1 + apply(y2 + apply(y3, m.step(2)), m.step(1))
    xv = t1 + apply(t2 + apply(t3, m.line(1)), m.line(0)) + apply(yv, m.line(2))
    entering = part + jnp.where(core == 0, apply(xv, m.near()), xv)
    sb[...] = spread(entering)
    acc_ref[...] = jnp.zeros((ROWS, 128), F32)
    acc_r[...] = jnp.zeros((B, 128), F32)

    for k in range(blocks):
        vb, wb = in_ref[...], sb[...]
        row = jnp.concatenate(
            [
                jnp.sum(vb * y_ref[k, :, half], axis=0, keepdims=True)
                + jnp.sum(wb * r_ref[k, :, half], axis=0, keepdims=True)
                for half in (slice(0, 128), slice(128, 256))
            ],
            axis=1,
        )
        sol_ref[k : k + 1, :] = row
        forcing = cnt_ref[k : k + 1, :] * row - sum_ref[k : k + 1, :]
        left, right = forcing[:, :128], forcing[:, 128:]
        acc_ref[...] += y_ref[k, :, :128] * left + y_ref[k, :, 128:] * right
        acc_r[...] += r_ref[k, :, :128] * left + r_ref[k, :, 128:] * right

    acc_ref[...] = jnp.broadcast_to(jnp.sum(acc_ref[...], axis=1, keepdims=True), (ROWS, 128))
    first = to_row(jnp.sum(acc_r[...], axis=1, keepdims=True))
    spread_out(out_ref, first, m, False)


def return_kernel(
    got_ref, got0_ref, other_ref, maps_ref, mapso_ref, y1_ref, y1o_ref, y2_ref, y2o_ref, acc_ref, y_ref,
    out_ref, gw_ref
):
    core = place()[2]
    upper = Maps(core, 1, (got0_ref, other_ref), (maps_ref, mapso_ref), None)
    lower = Maps(core, 0, (got0_ref, other_ref), (maps_ref, mapso_ref), ((y1_ref, y1o_ref), (y2_ref, y2o_ref)))
    c_in = collect(got_ref, upper, False)
    column = acc_ref[:, 0:1] + adjoint_column(c_in, y_ref[0])
    gw_ref[...] = jnp.broadcast_to(column[B:], (WIN, 128))
    spread_out(out_ref, to_row(column[:B]), lower, True)


def window_kernel(blocks, regions, got_ref, got0_ref, other_ref, maps_ref, mapso_ref, gw_ref, x_ref, out_ref):
    core = place()[2]
    base = window_base(blocks, regions)
    lower = Maps(core, 0, (got0_ref, other_ref), (maps_ref, mapso_ref), None)
    a_in = collect(got_ref, lower, True)
    column = gw_ref[:, 0:1] + adjoint_column(a_in, x_ref[blocks - 1, B:, :])
    w = lax.broadcasted_iota(jnp.int32, (WIN, 128), 0)
    lane = lax.broadcasted_iota(jnp.int32, (WIN, 128), 1)
    row = jnp.sum(jnp.where(((base + w) & 127) == lane, column, 0.0), axis=0, keepdims=True)
    out_ref[...] = jnp.broadcast_to(row.reshape(1, 1, 128), out_ref.shape)


def total_kernel(blocks, groups, regions, tracers, got_ref, out_ref):
    total = got_ref[0:32, 0, :]
    for t in range(1, tracers):
        total = total + got_ref[32 * t : 32 * t + 32, 0, :]
    d = lax.broadcasted_iota(jnp.int32, (32, 128), 0)
    lane = lax.broadcasted_iota(jnp.int32, (32, 128), 1)
    base = (d * (blocks * regions)) // groups - 3
    tile = (base + ((lane - base) & 127)) >> 7
    for t in range(out_ref.shape[1] // 128 + 1):
        lo, hi = 128 * t, min(128 * t + 128, out_ref.shape[1])
        if hi > lo:
            row = jnp.sum(jnp.where(tile == t, total, 0.0), axis=0, keepdims=True)
            out_ref[:, lo:hi] = row[:, : hi - lo]


def device(y, x, core):
    return ((y % 4) * 4 + x % 4) * 2 + core


def shards(
    factor_lower, factor_pivot, factor_upper, source_pattern, regions, params, obs_cells, obs_values
):
    low, piv, up = factor_lower[0], factor_pivot[0], factor_upper[0]
    pat = source_pattern[0]
    blocks = low.shape[0]
    tracers = lax.axis_size("tracer")
    groups = blocks * lax.axis_size("sub")
    regions_all = params.shape[0]
    scale = float(groups) ** (-1.5)
    def shape(*dims):
        return jax.ShapeDtypeStruct(dims, F32)

    def near(*dims):
        return pltpu.VMEM(dims, F32)

    def far(*arrays):
        return [pltpu.with_memory_space_constraint(a, pltpu.HBM) for a in arrays]

    def call(kernel, outs, ins, scratch=(), limit=8, flops=0, traffic=0, name=None):
        return pl.pallas_call(
            kernel,
            out_shape=outs,
            in_specs=ins,
            out_specs=jax.tree.map(lambda _: VM, outs),
            scratch_shapes=list(scratch),
            compiler_params=pltpu.CompilerParams(vmem_limit_bytes=limit * MIB),
            cost_estimate=pl.CostEstimate(flops=flops, bytes_accessed=traffic, transcendentals=0),
            name=name,
        )

    def swap(a):
        return lax.ppermute(a, "sub", [(d, d ^ 1) for d in range(32)])

    def along_x(a, j):
        pairs = [(device(y, x, 0), device(y, x + j, 0)) for y in range(4) for x in range(4)]
        pairs += [(device(y, x, 1), device(y, x - j, 1)) for y in range(4) for x in range(4)]
        return lax.ppermute(a, "sub", pairs)

    def along_y(a, j):
        pairs = [(device(y, x, 0), device(y + j, x, 0)) for y in range(4) for x in range(4)]
        pairs += [(device(y, x, 1), device(y - j, x, 1)) for y in range(4) for x in range(4)]
        return lax.ppermute(a, "sub", pairs)

    def exchange(a):
        return lax.all_to_all(a, "sub", 0, 0)

    block = (blocks, B, B)
    own, send = call(
        functools.partial(composites_kernel, blocks, scale),
        (shape(AUG, B), shape(AUG, B)),
        [HBM] * 5,
        [
            pltpu.VMEM(block, F32), pltpu.VMEM(block, F32), pltpu.VMEM((blocks, B), F32),
            pltpu.VMEM((blocks, B), jnp.int32), pltpu.SMEM((regions_all,), F32), pltpu.VMEM((blocks, B), F32),
            pltpu.VMEM((AUG, B), F32), pltpu.VMEM((AUG, B), F32), pltpu.VMEM((B, B), F32), pltpu.VMEM((B, B), F32),
            pltpu.SemaphoreType.DMA((2, blocks)), pltpu.SemaphoreType.DMA((3,)),
        ],
        limit=20, flops=6 * 2 * 16 * B**3, traffic=8 * MIB, name="composites",
    )(*far(low, up, pat, regions, params))
    got = swap(send)
    chip = call(chip_kernel, shape(AUG, B), [VM, VM], flops=6 * B**3, name="chip")(own, got)
    r1, r2, r3 = [along_x(chip, j) for j in (1, 2, 3)]
    other = swap(own)
    xt, rt, cnt, osum, pw = call(
        functools.partial(prefixes_kernel, blocks, scale),
        (near(blocks, ROWS, B), near(blocks, B, B), near(blocks, B), near(blocks, B), near(WIN, 128)),
        [HBM, HBM, VM, VM, SM, VM, VM, ANY],
        [pltpu.VMEM(block, F32), pltpu.VMEM(block, F32), pltpu.SemaphoreType.DMA((2, blocks))],
        limit=14, flops=6 * 2 * 16 * B**3, traffic=8 * MIB, name="prefixes",
    )(*far(low, up), pat, regions, params, obs_cells, obs_values, chip)
    maps, row, tail = call(
        line_kernel, (shape(4, AUG, B), shape(AUG, B), shape(8, B)), [VM, VM, VM, VM, ANY],
        flops=6 * 6 * B**3, name="line",
    )(chip, r1, r2, r3, cnt)
    y1, y2, y3 = along_y(row, 1), along_y(row, 2), along_y(tail, 3)
    maps_o = swap(maps)
    yt, token = call(
        functools.partial(lines_kernel, blocks),
        (near(blocks, ROWS, B), near(8, 128)),
        [HBM, HBM, VM, ANY],
        [pltpu.VMEM(block, F32), pltpu.VMEM(block, F32), pltpu.SemaphoreType.DMA((2, blocks))],
        limit=14, flops=6 * 2 * 16 * B**3, traffic=8 * MIB, name="lines",
    )(*far(up, piv), xt, tail)
    chip_in, following = call(
        entering_kernel, (shape(8, B), shape(8, B)), [VM] * 5 + [ANY], name="entering"
    )(own, maps, y1, y2, y3, token)
    following = swap(following)
    y1_o, y2_o = [swap(a) for a in lax.optimization_barrier((y1, y2, token))[:2]]
    messages = shape(32, 2, 128)
    vb, sent = call(start_kernel, (near(ROWS, 128), messages), [VM] * 8 + [ANY] * 2, name="start")(
        chip_in, following, pw, yt, other, got, maps, maps_o, y1_o, y2_o
    )
    got_s = exchange(sent)
    sol, sent, acc = call(
        functools.partial(middle_kernel, blocks),
        (shape(blocks, B), messages, near(ROWS, 128)),
        [VM] * 14,
        [pltpu.VMEM((B, 128), F32), pltpu.VMEM((B, 128), F32)],
        name="middle",
    )(got_s, got, other, maps, maps_o, y1, y1_o, y2, y2_o, vb, yt, rt, cnt, osum)
    got_c = exchange(sent)
    sent, gw = call(return_kernel, (messages, near(WIN, 128)), [VM] * 11, name="return")(
        got_c, got, other, maps, maps_o, y1, y1_o, y2, y2_o, acc, yt
    )
    got_a = exchange(sent)
    sent = call(
        functools.partial(window_kernel, blocks, regions_all), shape(32 * tracers, 1, 128), [VM] * 7, name="window"
    )(got_a, got, other, maps, maps_o, gw, xt)
    spread_windows = lax.all_to_all(sent, ("tracer", "sub"), 0, 0)
    gradient = call(
        functools.partial(total_kernel, blocks, groups, regions_all, tracers), shape(1, regions_all), [VM],
        name="total",
    )(spread_windows)
    return (gradient.reshape(regions_all), sol[None])


def solution(mesh):
    return jax.shard_map(
        shards,
        mesh=mesh,
        in_specs=(
            P("tracer", "sub", None, None),
            P("tracer", "sub", None, None),
            P("tracer", "sub", None, None),
            P("tracer", "sub", None),
            P("sub", None),
            P(),
            P("tracer", "sub"),
            P("tracer", "sub"),
        ),
        out_specs=(P(), P("tracer", "sub", None)),
        check_vma=False,
    )
```

time: 149 us -> 110 us (0.74)
  local copies, waits for them, and re-layouts: 18.9 us -> 0.02 us
  waiting for transfers between devices: 21.5 us -> 6.67 us
  blocking collectives: 37.4 us -> 51.1 us
  starting transfers between devices: 26.5 us -> 14 us
  other arithmetic: 3.56 us -> 0.61 us
  Pallas kernels: 39.5 us -> 37 us
    unnamed x46 -> x10, local copies, waits for them, and re-layouts: 18.9 us -> 0.02 us
    all_to_all x2 -> x3, blocking collectives: 21.5 us -> 35.1 us  [exchange(): return lax.all_to_all(a, 'sub', 0, 0)]
    ppermute x3, waiting for transfers between devices: 10.4 us -> 1.45 us  [along_x(): return lax.ppermute(a, 'sub', pairs)]
    all_to_all x1 -> x0, starting transfers between devices: 6.53 us -> none  [exchange(): return lax.all_to_all(a, 'sub', 0, 0)]
    ppermute x6, starting transfers between devices: 11.1 us -> 4.84 us  [swap(): return lax.ppermute(a, 'sub', [(d, d ^ 1) for d in range(32)])]
    all_to_all x1 -> x0, waiting for transfers between devices: 6.16 us -> none  [exchange(): return lax.all_to_all(a, 'sub', 0, 0)]
    select_n x4 -> x0, other arithmetic: 2.88 us -> none  [the longest x1 1.07 us: shards(): y1_l, y1_u = (jnp.where(left, y1, y1_o), jnp.where(left, y1_o, y1))]
    pallas_call x1, Pallas kernels: 5.2 us -> 3.58 us  [shards(): call(functools.partial(middle_kernel, blocks), (shape(blocks, B), message...]
  transfers between devices with their start and end apart: 13 -> 12, of which waited for: 6 -> 4; matrix products, arithmetic and copies ran while one was open for 2% -> 0% of each run, Pallas kernels for 14% -> 19%
where the time goes in v2:
time: 110 us
  blocking collectives  51.1 us (46%)
  Pallas kernels  37 us (34%)
  starting transfers between devices  14 us (13%)
  waiting for transfers between devices  6.67 us (6%)
    all_to_all x3, blocking collectives, exchange(): return lax.all_to_all(a, 'sub', 0, 0)  35.1 us
    all_to_all x1, blocking collectives, shards(): spread_windows = lax.all_to_all(sent, ('tracer', 'sub'), 0, 0)  16 us
    pallas_call x1, Pallas kernels, shards(): call(functools.partial(lines_kernel, blocks), (near(blocks, ROWS, B), nea...  11.4 us
    pallas_call x1, Pallas kernels, shards(): call(functools.partial(prefixes_kernel, blocks, scale), (near(blocks, ROW...  8.87 us
    pallas_call x1, Pallas kernels, shards(): call(functools.partial(composites_kernel, blocks, scale), (shape(AUG, B),...  8.73 us
    ppermute x3, starting transfers between devices, along_x(): return lax.ppermute(a, 'sub', pairs)  4.97 us
    ppermute x6, starting transfers between devices, swap(): return lax.ppermute(a, 'sub', [(d, d ^ 1) for d in range(32)])  4.84 us
    ppermute x3, starting transfers between devices, along_y(): return lax.ppermute(a, 'sub', pairs)  4.2 us
  transfers between devices with their start and end apart: 12, of which 4 were waited for; matrix products, arithmetic and copies ran while one was open for 0% of the time, Pallas kernels for 19%

profile of v2, /device:TPU:1, one launch (start us, length us, event | category | flops | bytes accessed | tf_op | source)
XLA Modules:
  0.0 110.2 jit_solution(3012996967983863862)
XLA Ops:
  0.7 8.7 %composites.1 = (f32[264,256]{1,0:T(8,128)S(1)}, f32[264,256]{1,0:T(8,128)S(1)}) custom-call(f32[16,256,256]{2,1,0:T(8,128)} %bitcast.11, f32[16,256,256]{2,1,0:T(8,128)} %bitcast.7, f32[16,256]{1,0:T(8,128)} %bitcast.5, s32[16,256]{1,0:T(8,128)} %reg_ref.1, f32[600]{0:T(1024)} %par_ref.1), custom_call_target="tpu_custom_call" | custom-call | flops 3221225472 | bytes 8388608 | tf_op jit(solution)/shard_map/composites/pallas_call | solution.py:521
  9.4 1.5 %collective-permute-start = (f32[264,256]{1,0:T(8,128)S(1)}, f32[264,256]{1,0:T(8,128)S(1)}, u32[]{:S(2)}, u32[]{:S(2)}) collective-permute-start(f32[264,256]{1,0:T(8,128)S(1)} %get-tuple-element.26), channel_id=1, source_target_pairs={{0,1},{1,0},{2,3},{3,2},{4,5},{5,4},{6,7},{7,6},{8,9},{9,8},{10,11... | collective-permute-start | bytes 811016 | tf_op jit(solution)/shard_map/ppermute | solution.py:505
  10.9 1.2 %collective-permute-done.got_ref.near1_ref.got0_ref = f32[264,256]{1,0:T(8,128)S(1)} collective-permute-done((f32[264,256]{1,0:T(8,128)S(1)}, f32[264,256]{1,0:T(8,128)S(1)}, u32[]{:S(2)}, u32[]{:S(2)}) %collective-permute-start) | collective-permute-done | bytes 270368 | tf_op jit(solution)/shard_map/ppermute | solution.py:505
  12.1 0.3 chip.1.dep_ref.own_ref
  12.4 1.4 %collective-permute-start.3 = (f32[264,256]{1,0:T(8,128)S(1)}, f32[264,256]{1,0:T(8,128)S(1)}, u32[]{:S(2)}, u32[]{:S(2)}) collective-permute-start(f32[264,256]{1,0:T(8,128)S(1)} %chip.1.dep_ref.own_ref), channel_id=1, source_target_pairs={{0,6},{2,0},{4,2},{6,4},{8,14},{10,8},{12,10},{14,12},{16,22},{18,... | collective-permute-start | bytes 811016 | tf_op jit(solution)/shard_map/ppermute | solution.py:510
  13.7 2.4 %collective-permute-start.2 = (f32[264,256]{1,0:T(8,128)S(1)}, f32[264,256]{1,0:T(8,128)S(1)}, u32[]{:S(2)}, u32[]{:S(2)}) collective-permute-start(f32[264,256]{1,0:T(8,128)S(1)} %chip.1.dep_ref.own_ref), channel_id=1, source_target_pairs={{0,4},{2,6},{4,0},{6,2},{8,12},{10,14},{12,8},{14,10},{16,20},{18,... | collective-permute-start | bytes 811016 | tf_op jit(solution)/shard_map/ppermute | solution.py:510
  16.2 1.2 %collective-permute-start.1 = (f32[264,256]{1,0:T(8,128)S(1)}, f32[264,256]{1,0:T(8,128)S(1)}, u32[]{:S(2)}, u32[]{:S(2)}) collective-permute-start(f32[264,256]{1,0:T(8,128)S(1)} %chip.1.dep_ref.own_ref), channel_id=1, source_target_pairs={{0,2},{2,4},{4,6},{6,0},{8,10},{10,12},{12,14},{14,8},{16,18},{18,... | collective-permute-start | bytes 811016 | tf_op jit(solution)/shard_map/ppermute | solution.py:510
  17.4 8.9 %prefixes.1 = (f32[16,288,256]{2,1,0:T(8,128)S(1)}, f32[16,256,256]{2,1,0:T(8,128)S(1)}, f32[16,256]{1,0:T(8,128)S(1)}, f32[16,256]{1,0:T(8,128)S(1)}, f32[32,128]{1,0:T(8,128)S(1)}) custom-call(f32[16,256,256]{2,1,0:T(8,128)} %bitcast.12, f32[16,256,256]{2,1,0:T(8,128)} %bitcast.8, f32[16,256]{1,0:T(8,128)S(1)} %bitcast.6, s32[16,256]{1,0:T(8,128)S(1)} %copy-done.1, ...), custom_call_target="tpu_custom_call" | custom-call | flops 3221225472 | bytes 8388608 | tf_op jit(solution)/shard_map/prefixes/pallas_call | solution.py:537
  26.3 1.4 %collective-permute-done.1.r1_ref = f32[264,256]{1,0:T(8,128)S(1)} collective-permute-done((f32[264,256]{1,0:T(8,128)S(1)}, f32[264,256]{1,0:T(8,128)S(1)}, u32[]{:S(2)}, u32[]{:S(2)}) %collective-permute-start.1) | collective-permute-done | bytes 270368 | tf_op jit(solution)/shard_map/ppermute | solution.py:510
  27.7 1.3 %line.1 = (f32[4,264,256]{2,1,0:T(8,128)S(1)}, f32[264,256]{1,0:T(8,128)S(1)}, f32[8,256]{1,0:T(8,128)S(1)}) custom-call(f32[264,256]{1,0:T(8,128)S(1)} %chip.1.dep_ref.own_ref, f32[264,256]{1,0:T(8,128)S(1)} %collective-permute-done.1.r1_ref, f32[264,256]{1,0:T(8,128)S(1)} %collective-permute-done.2.r2_ref, f32[264,256]{1,0:T(8,128)S(1)} %collective-permute-done.3.r3_ref, ...), custom_call_target="tpu_custom_call" | custom-call | flops 603979776 | tf_op jit(solution)/shard_map/line/pallas_call | solution.py:544
  29.0 1.8 %collective-permute-start.9 = (f32[4,264,256]{2,1,0:T(8,128)S(1)}, f32[4,264,256]{2,1,0:T(8,128)S(1)}, u32[]{:S(2)}, u32[]{:S(2)}) collective-permute-start(f32[4,264,256]{2,1,0:T(8,128)S(1)} %get-tuple-element.28.maps_ref), channel_id=1, source_target_pairs={{0,1},{1,0},{2,3},{3,2},{4,5},{5,4},{6,7},{7,6},{8,9},{9,8},{10,11... | collective-permute-start | bytes 3244040 | tf_op jit(solution)/shard_map/ppermute | solution.py:505
  30.8 0.1 collective-permute-start.8
  30.9 2.9 %collective-permute-start.5 = (f32[264,256]{1,0:T(8,128)S(1)}, f32[264,256]{1,0:T(8,128)S(1)}, u32[]{:S(2)}, u32[]{:S(2)}) collective-permute-start(f32[264,256]{1,0:T(8,128)S(1)} %get-tuple-element.29), channel_id=1, source_target_pairs={{0,16},{2,18},{4,20},{6,22},{8,24},{10,26},{12,28},{14,30},{16,0},... | collective-permute-start | bytes 811016 | tf_op jit(solution)/shard_map/ppermute | solution.py:515
  33.8 0.8 collective-permute-start.4
  34.6 11.4 %lines.1 = (f32[16,288,256]{2,1,0:T(8,128)S(1)}, f32[8,128]{1,0:T(8,128)S(1)}) custom-call(f32[16,256,256]{2,1,0:T(8,128)} %bitcast.9, f32[16,256,256]{2,1,0:T(8,128)} %bitcast.10, f32[16,288,256]{2,1,0:T(8,128)S(1)} %get-tuple-element.31.x_ref, f32[8,256]{1,0:T(8,128)S(1)} %get-tuple-element.30.dep_ref), custom_call_target="tpu_custom_call" | custom-call | flops 3221225472 | bytes 8388608 | tf_op jit(solution)/shard_map/lines/pallas_call | solution.py:550
  46.0 0.7 collective-permute-start.10
  46.6 0.1 collective-permute-start.11
  46.7 0.5 collective-permute-start.6
  47.2 3.2 %collective-permute-done.6.t3_ref = f32[8,256]{1,0:T(8,128)S(1)} collective-permute-done((f32[8,256]{1,0:T(8,128)S(1)}, f32[8,256]{1,0:T(8,128)S(1)}, u32[]{:S(2)}, u32[]{:S(2)}) %collective-permute-start.6) | collective-permute-done | bytes 8224 | tf_op jit(solution)/shard_map/ppermute | solution.py:515
  50.4 0.5 entering.1
  51.0 0.7 collective-permute-start.7
  51.7 0.8 collective-permute-done.7.got_ref
  52.5 0.4 start.1
  52.9 13.6 %all_to_all.20.got_ref = f32[32,2,128]{2,1,0:T(2,128)S(1)} all-to-all(f32[32,2,128]{2,1,0:T(2,128)S(1)} %get-tuple-element.39), channel_id=1, replica_groups=mesh['tracer'=4,'sub'=32] {'sub'}, dimensions={0} | all-to-all | bytes 65536 | tf_op jit(solution)/shard_map/all_to_all | solution.py:518
  66.5 3.6 %middle.1 = (f32[16,256]{1,0:T(8,128)}, f32[32,2,128]{2,1,0:T(2,128)S(1)}, f32[288,128]{1,0:T(8,128)S(1)}) custom-call(f32[32,2,128]{2,1,0:T(2,128)S(1)} %all_to_all.20.got_ref, f32[264,256]{1,0:T(8,128)S(1)} %collective-permute-done.got_ref.near1_ref.got0_ref, f32[264,256]{1,0:T(8,128)S(1)} %collective-permute-done.8.near0_ref.other_ref, ...), custom_call_target="tpu_custom_call" | custom-call | tf_op jit(solution)/shard_map/middle/pallas_call | solution.py:567
  70.1 10.7 %all_to_all.21.got_ref = f32[32,2,128]{2,1,0:T(2,128)S(1)} all-to-all(f32[32,2,128]{2,1,0:T(2,128)S(1)} %get-tuple-element.43), channel_id=1, replica_groups=mesh['tracer'=4,'sub'=32] {'sub'}, dimensions={0} | all-to-all | bytes 65536 | tf_op jit(solution)/shard_map/all_to_all | solution.py:518
  80.8 1.4 %return.1 = (f32[32,2,128]{2,1,0:T(2,128)S(1)}, f32[32,128]{1,0:T(8,128)S(1)}) custom-call(f32[32,2,128]{2,1,0:T(2,128)S(1)} %all_to_all.21.got_ref, f32[264,256]{1,0:T(8,128)S(1)} %collective-permute-done.got_ref.near1_ref.got0_ref, f32[264,256]{1,0:T(8,128)S(1)} %collective-permute-done.8.near0_ref.other_ref, ...), custom_call_target="tpu_custom_call" | custom-call | tf_op jit(solution)/shard_map/return/pallas_call | solution.py:575
  82.2 10.7 %all_to_all.22.got_ref = f32[32,2,128]{2,1,0:T(2,128)S(1)} all-to-all(f32[32,2,128]{2,1,0:T(2,128)S(1)} %get-tuple-element.45), channel_id=1, replica_groups=mesh['tracer'=4,'sub'=32] {'sub'}, dimensions={0} | all-to-all | bytes 65536 | tf_op jit(solution)/shard_map/all_to_all | solution.py:518
  93.0 0.5 window.1
  93.5 16.0 %all_to_all.23.got_ref = f32[128,1,128]{2,1,0:T(1,128)S(1)} all-to-all(f32[128,1,128]{2,1,0:T(1,128)S(1)} %window.1), channel_id=1, replica_groups=mesh['tracer'=4,'sub'=32] {'tracer','sub'}, dimensions={0} | all-to-all | bytes 131072 | tf_op jit(solution)/shard_map/all_to_all | solution.py:582
  109.5 0.1 total.1
  109.6 0.6 reduce
  (18 shorter events, 0.0 us)
Async XLA Ops:
  0.6 16.7 %copy-start = (f32[1,16,256]{2,1,0:T(8,128)S(1)}, f32[1,16,256]{2,1,0:T(8,128)}, u32[]{:S(2)}) copy-start(f32[1,16,256]{2,1,0:T(8,128)} %param.11) | copy-start | bytes 49156
  0.6 16.7 %copy-start.1 = (s32[16,256]{1,0:T(8,128)S(1)}, s32[16,256]{1,0:T(8,128)}, u32[]{:S(2)}) copy-start(s32[16,256]{1,0:T(8,128)} %reg_ref.1) | copy-start | bytes 49156
  0.7 16.7 %copy-start.2 = (f32[600]{0:T(1024)S(1)}, f32[600]{0:T(1024)}, u32[]{:S(2)}) copy-start(f32[600]{0:T(1024)} %par_ref.1) | copy-start | bytes 7204
  0.7 16.7 %copy-start.3 = (s32[1,256]{1,0:T(1,128)S(1)}, s32[1,256]{1,0:T(1,128)}, u32[]{:S(2)}) copy-start(s32[1,256]{1,0:T(1,128)} %cells_ref.1) | copy-start | bytes 3076
  0.7 16.7 %copy-start.4 = (f32[1,256]{1,0:T(1,128)S(1)}, f32[1,256]{1,0:T(1,128)}, u32[]{:S(2)}) copy-start(f32[1,256]{1,0:T(1,128)} %values_ref.1) | copy-start | bytes 3076
  9.4 2.7 %collective-permute-start = (f32[264,256]{1,0:T(8,128)S(1)}, f32[264,256]{1,0:T(8,128)S(1)}, u32[]{:S(2)}, u32[]{:S(2)}) collective-permute-start(f32[264,256]{1,0:T(8,128)S(1)} %get-tuple-element.26), channel_id=1, source_target_pairs={{0,1},{1,0},{2,3},{3,2},{4,5},{5,4},{6,7},{7,6},{8,9},{9,8},{10,11... | collective-permute-start | bytes 811016 | tf_op jit(solution)/shard_map/ppermute | solution.py:505
  12.4 13.9 %collective-permute-start.3 = (f32[264,256]{1,0:T(8,128)S(1)}, f32[264,256]{1,0:T(8,128)S(1)}, u32[]{:S(2)}, u32[]{:S(2)}) collective-permute-start(f32[264,256]{1,0:T(8,128)S(1)} %chip.1.dep_ref.own_ref), channel_id=1, source_target_pairs={{0,6},{2,0},{4,2},{6,4},{8,14},{10,8},{12,10},{14,12},{16,22},{18,... | collective-permute-start | bytes 811016 | tf_op jit(solution)/shard_map/ppermute | solution.py:510
  13.7 12.5 %collective-permute-start.2 = (f32[264,256]{1,0:T(8,128)S(1)}, f32[264,256]{1,0:T(8,128)S(1)}, u32[]{:S(2)}, u32[]{:S(2)}) collective-permute-start(f32[264,256]{1,0:T(8,128)S(1)} %chip.1.dep_ref.own_ref), channel_id=1, source_target_pairs={{0,4},{2,6},{4,0},{6,2},{8,12},{10,14},{12,8},{14,10},{16,20},{18,... | collective-permute-start | bytes 811016 | tf_op jit(solution)/shard_map/ppermute | solution.py:510
  16.2 11.5 %collective-permute-start.1 = (f32[264,256]{1,0:T(8,128)S(1)}, f32[264,256]{1,0:T(8,128)S(1)}, u32[]{:S(2)}, u32[]{:S(2)}) collective-permute-start(f32[264,256]{1,0:T(8,128)S(1)} %chip.1.dep_ref.own_ref), channel_id=1, source_target_pairs={{0,2},{2,4},{4,6},{6,0},{8,10},{10,12},{12,14},{14,8},{16,18},{18,... | collective-permute-start | bytes 811016 | tf_op jit(solution)/shard_map/ppermute | solution.py:510
  29.0 23.5 %collective-permute-start.9 = (f32[4,264,256]{2,1,0:T(8,128)S(1)}, f32[4,264,256]{2,1,0:T(8,128)S(1)}, u32[]{:S(2)}, u32[]{:S(2)}) collective-permute-start(f32[4,264,256]{2,1,0:T(8,128)S(1)} %get-tuple-element.28.maps_ref), channel_id=1, source_target_pairs={{0,1},{1,0},{2,3},{3,2},{4,5},{5,4},{6,7},{7,6},{8,9},{9,8},{10,11... | collective-permute-start | bytes 3244040 | tf_op jit(solution)/shard_map/ppermute | solution.py:505
  30.8 20.9 %collective-permute-start.8 = (f32[264,256]{1,0:T(8,128)S(1)}, f32[264,256]{1,0:T(8,128)S(1)}, u32[]{:S(2)}, u32[]{:S(2)}) collective-permute-start(f32[264,256]{1,0:T(8,128)S(1)} %get-tuple-element.25.own_ref), channel_id=1, source_target_pairs={{0,1},{1,0},{2,3},{3,2},{4,5},{5,4},{6,7},{7,6},{8,9},{9,8},{10,11... | collective-permute-start | bytes 811016 | tf_op jit(solution)/shard_map/ppermute | solution.py:505
  30.9 15.1 %collective-permute-start.5 = (f32[264,256]{1,0:T(8,128)S(1)}, f32[264,256]{1,0:T(8,128)S(1)}, u32[]{:S(2)}, u32[]{:S(2)}) collective-permute-start(f32[264,256]{1,0:T(8,128)S(1)} %get-tuple-element.29), channel_id=1, source_target_pairs={{0,16},{2,18},{4,20},{6,22},{8,24},{10,26},{12,28},{14,30},{16,0},... | collective-permute-start | bytes 811016 | tf_op jit(solution)/shard_map/ppermute | solution.py:515
  33.8 12.2 %collective-permute-start.4 = (f32[264,256]{1,0:T(8,128)S(1)}, f32[264,256]{1,0:T(8,128)S(1)}, u32[]{:S(2)}, u32[]{:S(2)}) collective-permute-start(f32[264,256]{1,0:T(8,128)S(1)} %get-tuple-element.29), channel_id=1, source_target_pairs={{0,8},{2,10},{4,12},{6,14},{8,16},{10,18},{12,20},{14,22},{16,24},... | collective-permute-start | bytes 811016 | tf_op jit(solution)/shard_map/ppermute | solution.py:515
  46.0 6.5 %collective-permute-start.10 = (f32[264,256]{1,0:T(8,128)S(1)}, f32[264,256]{1,0:T(8,128)S(1)}, u32[]{:S(2)}, u32[]{:S(2)}) collective-permute-start(f32[264,256]{1,0:T(8,128)S(1)} %collective-permute-done.4.y1_ref), channel_id=1, source_target_pairs={{0,1},{1,0},{2,3},{3,2},{4,5},{5,4},{6,7},{7,6},{8,9},{9,8},{10,11... | collective-permute-start | bytes 811016 | tf_op jit(solution)/shard_map/ppermute | solution.py:505
  46.6 5.9 %collective-permute-start.11 = (f32[264,256]{1,0:T(8,128)S(1)}, f32[264,256]{1,0:T(8,128)S(1)}, u32[]{:S(2)}, u32[]{:S(2)}) collective-permute-start(f32[264,256]{1,0:T(8,128)S(1)} %collective-permute-done.5.y2_ref), channel_id=1, source_target_pairs={{0,1},{1,0},{2,3},{3,2},{4,5},{5,4},{6,7},{7,6},{8,9},{9,8},{10,11... | collective-permute-start | bytes 811016 | tf_op jit(solution)/shard_map/ppermute | solution.py:505
  46.7 3.7 %collective-permute-start.6 = (f32[8,256]{1,0:T(8,128)S(1)}, f32[8,256]{1,0:T(8,128)S(1)}, u32[]{:S(2)}, u32[]{:S(2)}) collective-permute-start(f32[8,256]{1,0:T(8,128)S(1)} %get-tuple-element.30.dep_ref), channel_id=1, source_target_pairs={{0,24},{2,26},{4,28},{6,30},{8,0},{10,2},{12,4},{14,6},{16,8},{18,... | collective-permute-start | bytes 24584 | tf_op jit(solution)/shard_map/ppermute | solution.py:515
  51.0 1.5 %collective-permute-start.7 = (f32[8,256]{1,0:T(8,128)S(1)}, f32[8,256]{1,0:T(8,128)S(1)}, u32[]{:S(2)}, u32[]{:S(2)}) collective-permute-start(f32[8,256]{1,0:T(8,128)S(1)} %get-tuple-element.34), channel_id=1, source_target_pairs={{0,1},{1,0},{2,3},{3,2},{4,5},{5,4},{6,7},{7,6},{8,9},{9,8},{10,11... | collective-permute-start | bytes 24584 | tf_op jit(solution)/shard_map/ppermute | solution.py:505

commit v3 on v2

--- a/solution.py
+++ b/solution.py
@@ -16,7 +16,8 @@
 NT = (((1,), (1,)), ((), ()))
 NN = (((1,), (0,)), ((), ()))
 MIB = 1 << 20
-UNROLL = True
+PARTS = 4
+DEPTH = 2
 VM = pl.BlockSpec(memory_space=pltpu.VMEM)
 SM = pl.BlockSpec(memory_space=pltpu.SMEM)
 ANY = pl.BlockSpec(memory_space=pl.ANY)
@@ -39,13 +40,15 @@
     )
 
 
-def unit():
-    i = lax.broadcasted_iota(jnp.int32, (B, B), 0)
-    return jnp.where(i == lax.broadcasted_iota(jnp.int32, (B, B), 1), 1.0, 0.0)
+def less_unit(b):
+    i = lax.broadcasted_iota(jnp.int32, (128, 128), 0)
+    unit = jnp.where(i == lax.broadcasted_iota(jnp.int32, (128, 128), 1), 1.0, 0.0)
+    top = jnp.concatenate([b[:128, :128] - unit, b[:128, 128:]], axis=1)
+    return jnp.concatenate([top, jnp.concatenate([b[128:, :128], b[128:, 128:] - unit], axis=1)], axis=0)
 
 
 def advance(a, b, dims=NT):
-    return a + dot3(a, b - unit(), dims)
+    return a + dot3(a, less_unit(b), dims)
 
 
 def affine(first, second):
@@ -121,28 +124,37 @@
 
 
 def composites_kernel(
-    blocks, scale, low_hbm, up_hbm, pat_hbm, reg_hbm, par_hbm,
-    own_ref, send_ref, low, up, pat, reg, par, src, xa, xb, ra, rb, sems, small
+    blocks, scale, low_hbm, up_hbm, pat_hbm, reg_hbm, par,
+    own_ref, send_ref, low, up, pat, reg, src, xs, rs, sems, small
 ):
-    half = blocks // 2
+    run = blocks // PARTS
     last = blocks - 1
 
     def copies(k):
-        return (
-            pltpu.make_async_copy(low_hbm.at[k], low.at[k], sems.at[0, k]),
-            pltpu.make_async_copy(up_hbm.at[last - k], up.at[last - k], sems.at[1, k]),
-        )
+        return [
+            pltpu.make_async_copy(low_hbm.at[k + i * run], low.at[k + i * run], sems.at[0, k + i * run])
+            for i in range(PARTS)
+        ] + [
+            pltpu.make_async_copy(
+                up_hbm.at[last - k - i * run], up.at[last - k - i * run], sems.at[1, last - k - i * run]
+            )
+            for i in range(PARTS)
+        ]
 
     extras = (
-        pltpu.make_async_copy(par_hbm, par, small.at[0]),
         pltpu.make_async_copy(reg_hbm, reg, small.at[1]),
         pltpu.make_async_copy(pat_hbm, pat, small.at[2]),
     )
+
+    def begin(k):
+        if k < run:
+            for c in copies(k):
+                c.start()
+
     for c in extras:
         c.start()
-    for k in range(half):
-        for c in copies(k) + copies(k + half):
-            c.start()
+    for k in range(DEPTH):
+        begin(k)
     y, x, core = place()
     count = par.shape[0]
     base = window_base(blocks, count)
@@ -153,43 +165,46 @@
     for w in range(WIN):
         value = jnp.where(rel == w, par[jnp.clip(base + w, 0, count - 1)], value)
     src[...] = scale * pat[...] * value
-    for c in copies(0) + copies(half):
-        c.wait()
-    xa[...] = jnp.concatenate([low[0].T, jnp.broadcast_to(src[0:1, :], (8, B))], axis=0)
-    xb[...] = jnp.concatenate([low[half].T, jnp.broadcast_to(src[half : half + 1, :], (8, B))], axis=0)
-    ra[...] = up[last].T
-    rb[...] = up[last - half].T
-
-    def step(k, carry):
-        for c in copies(k) + copies(k + half):
+    for k in range(run):
+        for c in copies(k):
             c.wait()
-        a = advance(xa[...], low[k])
-        b = advance(xb[...], low[k + half])
-        c = advance(ra[...], up[last - k])
-        d = advance(rb[...], up[last - half - k])
-        xa[:B, :] = a[:B]
-        xa[B:, :] = a[B:] + src[pl.ds(k, 1), :]
-        xb[:B, :] = b[:B]
-        xb[B:, :] = b[B:] + src[pl.ds(k + half, 1), :]
-        ra[...] = c
-        rb[...] = d
-        return carry
-
-    lax.fori_loop(1, half, step, 0, unroll=UNROLL)
-    xs = affine(xa[...], xb[...])
-    rs = advance(ra[...], rb[...], NN)
-    zero = jnp.zeros((8, B), F32)
+        begin(k + DEPTH)
+        if k == 0:
+            for i in range(PARTS):
+                xs[i, :B, :] = low[i * run].T
+                xs[i, B:, :] = jnp.broadcast_to(src[i * run : i * run + 1, :], (AUG - B, B))
+                rs[i] = up[last - i * run].T
+            continue
+        moved = [advance(xs[i], low[k + i * run]) for i in range(PARTS)]
+        other = [advance(rs[i], up[last - k - i * run]) for i in range(PARTS)]
+        for i in range(PARTS):
+            row = k + i * run
+            xs[i, :B, :] = moved[i][:B]
+            xs[i, B:, :] = moved[i][B:] + src[row : row + 1, :]
+            rs[i] = other[i]
+    for i in (0, 2):
+        moved = advance(xs[i], xs[i + 1, :B, :], NN)
+        other = advance(rs[i], rs[i + 1], NN)
+        xs[i, :B, :] = moved[:B]
+        xs[i, B:, :] = moved[B:] + xs[i + 1, B:, :]
+        rs[i] = other
+    moved = advance(xs[0], xs[2, :B, :], NN)
+    other = advance(rs[0], rs[2], NN)
+    xs[1, :B, :] = moved[:B]
+    xs[1, B:, :] = moved[B:] + xs[2, B:, :]
+    rs[1] = other
+    zero = jnp.zeros((AUG - B, B), F32)
 
     @pl.when(core == 0)
     def _():
-        own_ref[...] = xs
-        send_ref[:B, :] = rs
+        own_ref[...] = xs[1]
+        send_ref[:B, :] = rs[1]
         send_ref[B:, :] = zero
 
     @pl.when(core != 0)
     def _():
-        send_ref[...] = xs
-        own_ref[:B, :] = rs
+        send_ref[...] = xs[1]
+        own_ref[:B, :] = rs[1]
         own_ref[B:, :] = zero
 
 
@@ -198,21 +213,17 @@
 
 
 def prefixes_kernel(
-    blocks, scale, low_hbm, up_hbm, pat_ref, reg_ref, par_ref, cells_ref, values_ref, dep_ref,
-    x_ref, r_ref, cnt_ref, sum_ref, pw_ref, low, up, sems
+    blocks, scale, low, piv_hbm, pat_ref, reg_ref, par_ref, cells_ref, values_ref, dep_ref,
+    z_ref, f_ref, cnt_ref, sum_ref, pw_ref, piv, xa, xb, sems
 ):
-    last = blocks - 1
     y, x, core = place()
-
-    def copies(k):
-        return (
-            pltpu.make_async_copy(low_hbm.at[k], low.at[k], sems.at[0, k]),
-            pltpu.make_async_copy(up_hbm.at[last - k], up.at[last - k], sems.at[1, k]),
-        )
+    half = blocks // 2
+
+    def copy(k):
+        return pltpu.make_async_copy(piv_hbm.at[k], piv.at[k], sems.at[k])
 
     for k in range(blocks):
-        for c in copies(k):
-            c.start()
+        copy(k).start()
     count = par_ref.shape[0]
     base = window_base(blocks, count)
     local = cells_ref[...] - ((y * 4 + x) * 2 + core) * (blocks * B)
@@ -232,57 +243,62 @@
         window = jnp.where(wi == w, par_ref[jnp.clip(base + w, 0, count - 1)], window)
     pw_ref[...] = window
 
-    for c in copies(0):
-        c.wait()
-    x_ref[0] = jnp.concatenate([low[0].T, source_window(0, reg_ref, pat_ref, base, scale)], axis=0)
-    r_ref[last] = up[last].T
-
-    def step(k, carry):
-        for c in copies(k):
-            c.wait()
-        moved = advance(x_ref[k - 1], low[k])
-        r_ref[last - k] = advance(r_ref[last - k + 1], up[last - k])
-        x_ref[k, :B, :] = moved[:B]
-        x_ref[k, B:, :] = moved[B:] + source_window(k, reg_ref, pat_ref, base, scale)
-        return carry
-
-    lax.fori_loop(1, blocks, step, 0, unroll=UNROLL)
-
-
-def lines_kernel(blocks, up_hbm, piv_hbm, x_ref, dep_ref, y_ref, token_ref, up, piv, sems):
+    def window(k):
+        return source_window(k, reg_ref, pat_ref, base, scale)
+
+    for ref, at in ((xa, 0), (xb, half)):
+        ref[0, :B, :] = low[at].T
+        ref[0, B:, :] = window(at)
+    for k in range(1, half):
+        a = advance(xa[k - 1], low[k])
+        b = advance(xb[k - 1], low[k + half])
+        xa[k, :B, :] = a[:B]
+        xa[k, B:, :] = a[B:] + window(k)
+        xb[k, :B, :] = b[:B]
+        xb[k, B:, :] = b[B:] + window(k + half)
+        if k == 2:
+            for i in range(blocks):
+                copy(i).wait()
+        if k >= 2:
+            z_ref[k - 2] = dot3(xa[k - 2], piv[k - 2], NT)
+    for k in range(half):
+        full = advance(xa[half - 1], xb[k, :B, :], NN)
+        full = jnp.concatenate([full[:B], full[B:] + xb[k, B:, :]], axis=0)
+        if k < 2:
+            z_ref[half - 2 + k] = dot3(xa[half - 2 + k], piv[half - 2 + k], NT)
+        z_ref[half + k] = dot3(full, piv[half + k], NT)
+    f_ref[...] = full[B:]
+
+
+def lines_kernel(blocks, up, z_ref, dep_ref, y_ref, token_ref, parts):
+    half = blocks // 2
     last = blocks - 1
-
-    def copies(k):
-        return (
-            pltpu.make_async_copy(up_hbm.at[k], up.at[k], sems.at[0, k]),
-            pltpu.make_async_copy(piv_hbm.at[k], piv.at[k], sems.at[1, k]),
-        )
-
-    for i in range(blocks):
-        for c in copies(last - i):
-            c.start()
-    for c in copies(last):
-        c.wait()
-    y_ref[last] = dot3(x_ref[last], piv[last], NT)
-
-    def back(i, carry):
-        k = last - i
-        for c in copies(k):
-            c.wait()
-        y_ref[k] = dot3(x_ref[k], piv[k], NT) + advance(y_ref[k + 1], up[k])
-        return carry
-
-    lax.fori_loop(1, blocks, back, 0, unroll=UNROLL)
+    y_ref[last, :ROWS, :] = z_ref[last]
+    y_ref[last, ROWS:, :] = up[last].T
+    parts[half - 1, :ROWS, :] = z_ref[half - 1]
+    parts[half - 1, ROWS:, :] = up[half - 1].T
+    for k in range(half - 2, -1, -1):
+        a = advance(y_ref[k + half + 1], up[k + half])
+        b = advance(parts[k + 1], up[k])
+        y_ref[k + half, :ROWS, :] = a[:ROWS] + z_ref[k + half]
+        y_ref[k + half, ROWS:, :] = a[ROWS:]
+        parts[k, :ROWS, :] = b[:ROWS] + z_ref[k]
+        parts[k, ROWS:, :] = b[ROWS:]
+    for k in range(half):
+        full = advance(y_ref[half], parts[k, ROWS:, :], NN)
+        y_ref[k, :ROWS, :] = full[:ROWS] + parts[k, :ROWS, :]
+        y_ref[k, ROWS:, :] = full[ROWS:]
     token_ref[...] = jnp.zeros((8, 128), F32)
 
 
-def line_kernel(own_ref, r1_ref, r2_ref, r3_ref, dep_ref, maps_ref, row_ref, tail_ref):
+def line_kernel(own_ref, mine_ref, r1_ref, r2_ref, r3_ref, dep_ref, maps_ref, row_ref, tail_ref):
     y, x, core = place()
     p = jnp.where(core == 0, x, 3 - x)
     i = lax.broadcasted_iota(jnp.int32, (AUG, B), 0)
     j = lax.broadcasted_iota(jnp.int32, (AUG, B), 1)
     eye = jnp.where(i == j, 1.0, 0.0)
     r1, r2, r3 = r1_ref[...], r2_ref[...], r3_ref[...]
+    maps_ref[4] = mine_ref[...]
     maps_ref[0] = jnp.where(p >= 1, r1, eye)
     maps_ref[1] = jnp.where(p >= 2, r2, eye)
     pre = affine(jnp.where(p >= 3, r3, eye), maps_ref[1])
@@ -290,7 +306,7 @@
     maps_ref[2] = affine(pre, maps_ref[0])
     maps_ref[3] = affine(suf, jnp.where(p <= 0, r1, eye))
     row_ref[...] = affine(affine(maps_ref[2], own_ref[...]), maps_ref[3])
-    tail_ref[...] = row_ref[B:, :]
+    tail_ref[...] = row_ref[B : B + 8, :]
 
 
 def entering_kernel(own_ref, maps_ref, y1_ref, y2_ref, t3_ref, dep_ref, chip_ref, next_ref):
@@ -305,15 +321,15 @@
     next_ref[...] = jnp.broadcast_to(following, (8, B))
 
 
-def start_kernel(chip_ref, got_ref, pw_ref, y_ref, near0_ref, near1_ref, maps_ref, mapso_ref, dep1_ref, dep2_ref, in_ref, out_ref):
+def start_kernel(chip_ref, got_ref, pw_ref, y_ref, near1_ref, maps_ref, mapso_ref, dep1_ref, dep2_ref, in_ref, out_ref):
     my_y, my_x, core = place()
     entering = jnp.where(core == 0, chip_ref[0:1, :], got_ref[0:1, :])
     vb = jnp.concatenate([spread(entering), pw_ref[...]], axis=0)
     in_ref[...] = vb
     v = jnp.concatenate(
         [
-            jnp.sum(vb * y_ref[0, :, :128], axis=0, keepdims=True),
-            jnp.sum(vb * y_ref[0, :, 128:], axis=0, keepdims=True),
+            jnp.sum(vb * y_ref[0, :ROWS, :128], axis=0, keepdims=True),
+            jnp.sum(vb * y_ref[0, :ROWS, 128:], axis=0, keepdims=True),
         ],
         axis=1,
     )
@@ -334,10 +350,10 @@
 class Maps:
     def __init__(self, core, side, near, maps, steps):
         self.mine = core == side
-        self.near_refs, self.map_refs, self.step_refs = near, maps, steps
+        self.near_ref, self.map_refs, self.step_refs = near, maps, steps
 
     def near(self):
-        return jnp.where(self.mine, self.near_refs[0][:B, :], self.near_refs[1][:B, :])
+        return jnp.where(self.mine, self.near_ref[:B, :], self.map_refs[1][4, :B, :])
 
     def line(self, i):
         return jnp.where(self.mine, self.map_refs[0][i, :B, :], self.map_refs[1][i, :B, :])
@@ -385,11 +401,11 @@
 
 
 def middle_kernel(
-    blocks, got_ref, got0_ref, other_ref, maps_ref, mapso_ref, y1_ref, y1o_ref, y2_ref, y2o_ref,
-    in_ref, y_ref, r_ref, cnt_ref, sum_ref, sol_ref, out_ref, acc_ref, sb, acc_r
+    blocks, got_ref, got0_ref, maps_ref, mapso_ref, y1_ref, y1o_ref, y2_ref, y2o_ref,
+    in_ref, y_ref, cnt_ref, sum_ref, sol_ref, out_ref, acc_ref, sb, acc_r
 ):
     my_y, my_x, core = place()
-    m = Maps(core, 1, (got0_ref, other_ref), (maps_ref, mapso_ref), ((y1_ref, y1o_ref), (y2_ref, y2o_ref)))
+    m = Maps(core, 1, got0_ref, (maps_ref, mapso_ref), ((y1_ref, y1o_ref), (y2_ref, y2o_ref)))
     sy, sx, sc = row_coords()
     same = sy == my_y
     part, t1, t2, t3, y1, y2, y3 = gather_rows(
@@ -409,8 +425,8 @@
         vb, wb = in_ref[...], sb[...]
         row = jnp.concatenate(
             [
-                jnp.sum(vb * y_ref[k, :, half], axis=0, keepdims=True)
-                + jnp.sum(wb * r_ref[k, :, half], axis=0, keepdims=True)
+                jnp.sum(vb * y_ref[k, :ROWS, half], axis=0, keepdims=True)
+                + jnp.sum(wb * y_ref[k, ROWS:, half], axis=0, keepdims=True)
                 for half in (slice(0, 128), slice(128, 256))
             ],
             axis=1,
@@ -418,8 +434,8 @@
         sol_ref[k : k + 1, :] = row
         forcing = cnt_ref[k : k + 1, :] * row - sum_ref[k : k + 1, :]
         left, right = forcing[:, :128], forcing[:, 128:]
-        acc_ref[...] += y_ref[k, :, :128] * left + y_ref[k, :, 128:] * right
-        acc_r[...] += r_ref[k, :, :128] * left + r_ref[k, :, 128:] * right
+        acc_ref[...] += y_ref[k, :ROWS, :128] * left + y_ref[k, :ROWS, 128:] * right
+        acc_r[...] += y_ref[k, ROWS:, :128] * left + y_ref[k, ROWS:, 128:] * right
 
     acc_ref[...] = jnp.broadcast_to(jnp.sum(acc_ref[...], axis=1, keepdims=True), (ROWS, 128))
     first = to_row(jnp.sum(acc_r[...], axis=1, keepdims=True))
@@ -427,24 +443,24 @@
 
 
 def return_kernel(
-    got_ref, got0_ref, other_ref, maps_ref, mapso_ref, y1_ref, y1o_ref, y2_ref, y2o_ref, acc_ref, y_ref,
+    got_ref, got0_ref, maps_ref, mapso_ref, y1_ref, y1o_ref, y2_ref, y2o_ref, acc_ref, y_ref,
     out_ref, gw_ref
 ):
     core = place()[2]
-    upper = Maps(core, 1, (got0_ref, other_ref), (maps_ref, mapso_ref), None)
-    lower = Maps(core, 0, (got0_ref, other_ref), (maps_ref, mapso_ref), ((y1_ref, y1o_ref), (y2_ref, y2o_ref)))
+    upper = Maps(core, 1, got0_ref, (maps_ref, mapso_ref), None)
+    lower = Maps(core, 0, got0_ref, (maps_ref, mapso_ref), ((y1_ref, y1o_ref), (y2_ref, y2o_ref)))
     c_in = collect(got_ref, upper, False)
-    column = acc_ref[:, 0:1] + adjoint_column(c_in, y_ref[0])
+    column = acc_ref[:, 0:1] + adjoint_column(c_in, y_ref[0, :ROWS, :])
     gw_ref[...] = jnp.broadcast_to(column[B:], (WIN, 128))
     spread_out(out_ref, to_row(column[:B]), lower, True)
 
 
-def window_kernel(blocks, regions, got_ref, got0_ref, other_ref, maps_ref, mapso_ref, gw_ref, x_ref, out_ref):
+def window_kernel(blocks, regions, got_ref, got0_ref, maps_ref, mapso_ref, gw_ref, f_ref, out_ref):
     core = place()[2]
     base = window_base(blocks, regions)
-    lower = Maps(core, 0, (got0_ref, other_ref), (maps_ref, mapso_ref), None)
+    lower = Maps(core, 0, got0_ref, (maps_ref, mapso_ref), None)
     a_in = collect(got_ref, lower, True)
-    column = gw_ref[:, 0:1] + adjoint_column(a_in, x_ref[blocks - 1, B:, :])
+    column = gw_ref[:, 0:1] + adjoint_column(a_in, f_ref[...])
     w = lax.broadcasted_iota(jnp.int32, (WIN, 128), 0)
     lane = lax.broadcasted_iota(jnp.int32, (WIN, 128), 1)
     row = jnp.sum(jnp.where(((base + w) & 127) == lane, column, 0.0), axis=0, keepdims=True)
@@ -518,67 +534,68 @@
         return lax.all_to_all(a, "sub", 0, 0)
 
     block = (blocks, B, B)
-    own, send = call(
+    own, send, low_near, up_near = call(
         functools.partial(composites_kernel, blocks, scale),
-        (shape(AUG, B), shape(AUG, B)),
-        [HBM] * 5,
+        (shape(AUG, B), shape(AUG, B), near(*block), near(*block)),
+        [HBM] * 4 + [SM],
         [
-            pltpu.VMEM(block, F32), pltpu.VMEM(block, F32), pltpu.VMEM((blocks, B), F32),
-            pltpu.VMEM((blocks, B), jnp.int32), pltpu.SMEM((regions_all,), F32), pltpu.VMEM((blocks, B), F32),
-            pltpu.VMEM((AUG, B), F32), pltpu.VMEM((AUG, B), F32), pltpu.VMEM((B, B), F32), pltpu.VMEM((B, B), F32),
+            pltpu.VMEM((blocks, B), F32), pltpu.VMEM((blocks, B), jnp.int32),
+            pltpu.VMEM((blocks, B), F32), pltpu.VMEM((PARTS, AUG, B), F32), pltpu.VMEM((PARTS, B, B), F32),
             pltpu.SemaphoreType.DMA((2, blocks)), pltpu.SemaphoreType.DMA((3,)),
         ],
-        limit=20, flops=6 * 2 * 16 * B**3, traffic=8 * MIB, name="composites",
-    )(*far(low, up, pat, regions, params))
+        limit=12, flops=6 * 2 * 16 * B**3, traffic=8 * MIB, name="composites",
+    )(*far(low, up, pat, regions), params)
     got = swap(send)
     chip = call(chip_kernel, shape(AUG, B), [VM, VM], flops=6 * B**3, name="chip")(own, got)
     r1, r2, r3 = [along_x(chip, j) for j in (1, 2, 3)]
-    other = swap(own)
-    xt, rt, cnt, osum, pw = call(
+    zt, ft, cnt, osum, pw = call(
         functools.partial(prefixes_kernel, blocks, scale),
-        (near(blocks, ROWS, B), near(blocks, B, B), near(blocks, B), near(blocks, B), near(WIN, 128)),
-        [HBM, HBM, VM, VM, SM, VM, VM, ANY],
-        [pltpu.VMEM(block, F32), pltpu.VMEM(block, F32), pltpu.SemaphoreType.DMA((2, blocks))],
+        (near(blocks, ROWS, B), near(WIN, B), near(blocks, B), near(blocks, B), near(WIN, 128)),
+        [VM, HBM, VM, VM, SM, VM, VM, ANY],
+        [
+            pltpu.VMEM(block, F32), pltpu.VMEM((blocks // 2, ROWS, B), F32),
+            pltpu.VMEM((blocks // 2, ROWS, B), F32), pltpu.SemaphoreType.DMA((blocks,)),
+        ],
         limit=14, flops=6 * 2 * 16 * B**3, traffic=8 * MIB, name="prefixes",
-    )(*far(low, up), pat, regions, params, obs_cells, obs_values, chip)
+    )(low_near, *far(piv), pat, regions, params, obs_cells, obs_values, chip)
     maps, row, tail = call(
-        line_kernel, (shape(4, AUG, B), shape(AUG, B), shape(8, B)), [VM, VM, VM, VM, ANY],
+        line_kernel, (shape(5, AUG, B), shape(AUG, B), shape(8, B)), [VM, VM, VM, VM, VM, ANY],
         flops=6 * 6 * B**3, name="line",
-    )(chip, r1, r2, r3, cnt)
+    )(chip, own, r1, r2, r3, cnt)
     y1, y2, y3 = along_y(row, 1), along_y(row, 2), along_y(tail, 3)
     maps_o = swap(maps)
     yt, token = call(
         functools.partial(lines_kernel, blocks),
-        (near(blocks, ROWS, B), near(8, 128)),
-        [HBM, HBM, VM, ANY],
-        [pltpu.VMEM(block, F32), pltpu.VMEM(block, F32), pltpu.SemaphoreType.DMA((2, blocks))],
-        limit=14, flops=6 * 2 * 16 * B**3, traffic=8 * MIB, name="lines",
-    )(*far(up, piv), xt, tail)
+        (near(blocks, ROWS + B, B), near(8, 128)),
+        [VM, VM, ANY],
+        [pltpu.VMEM((blocks // 2, ROWS + B, B), F32)],
+        limit=12, flops=6 * 3 * 16 * B**3, traffic=8 * MIB, name="lines",
+    )(up_near, zt, y3)
     chip_in, following = call(
         entering_kernel, (shape(8, B), shape(8, B)), [VM] * 5 + [ANY], name="entering"
     )(own, maps, y1, y2, y3, token)
     following = swap(following)
     y1_o, y2_o = [swap(a) for a in lax.optimization_barrier((y1, y2, token))[:2]]
     messages = shape(32, 2, 128)
-    vb, sent = call(start_kernel, (near(ROWS, 128), messages), [VM] * 8 + [ANY] * 2, name="start")(
-        chip_in, following, pw, yt, other, got, maps, maps_o, y1_o, y2_o
+    vb, sent = call(start_kernel, (near(ROWS, 128), messages), [VM] * 7 + [ANY] * 2, name="start")(
+        chip_in, following, pw, yt, got, maps, maps_o, y1_o, y2_o
     )
     got_s = exchange(sent)
     sol, sent, acc = call(
         functools.partial(middle_kernel, blocks),
         (shape(blocks, B), messages, near(ROWS, 128)),
-        [VM] * 14,
+        [VM] * 12,
         [pltpu.VMEM((B, 128), F32), pltpu.VMEM((B, 128), F32)],
         name="middle",
-    )(got_s, got, other, maps, maps_o, y1, y1_o, y2, y2_o, vb, yt, rt, cnt, osum)
+    )(got_s, got, maps, maps_o, y1, y1_o, y2, y2_o, vb, yt, cnt, osum)
     got_c = exchange(sent)
-    sent, gw = call(return_kernel, (messages, near(WIN, 128)), [VM] * 11, name="return")(
-        got_c, got, other, maps, maps_o, y1, y1_o, y2, y2_o, acc, yt
+    sent, gw = call(return_kernel, (messages, near(WIN, 128)), [VM] * 10, name="return")(
+        got_c, got, maps, maps_o, y1, y1_o, y2, y2_o, acc, yt
     )
     got_a = exchange(sent)
     sent = call(
-        functools.partial(window_kernel, blocks, regions_all), shape(32 * tracers, 1, 128), [VM] * 7, name="window"
-    )(got_a, got, other, maps, maps_o, gw, xt)
+        functools.partial(window_kernel, blocks, regions_all), shape(32 * tracers, 1, 128), [VM] * 6, name="window"
+    )(got_a, got, maps, maps_o, gw, ft)
     spread_windows = lax.all_to_all(sent, ("tracer", "sub"), 0, 0)
     gradient = call(
         functools.partial(total_kernel, blocks, groups, regions_all, tracers), shape(1, regions_all), [VM],

time: 110 us -> 105 us (0.955)
  Pallas kernels: 37 us -> 29.3 us
  starting transfers between devices: 14 us -> 15.3 us
    pallas_call x4, Pallas kernels: 14.4 us -> 8.91 us  [the longest x1 5.77 us: shards(): call(functools.partial(lines_kernel, blocks), (near(blocks, ROWS + B, B),...]
    ppermute x3, waiting for transfers between devices: 1.45 us -> 2.67 us  [along_x(): return lax.ppermute(a, 'sub', pairs)]
    pallas_call x1, Pallas kernels: 8.87 us -> 7.66 us  [shards(): call(functools.partial(prefixes_kernel, blocks, scale), (near(blocks, ROW...]
    ppermute x6 -> x5, starting transfers between devices: 4.84 us -> 5.34 us  [swap(): return lax.ppermute(a, 'sub', [(d, d ^ 1) for d in range(32)])]
  transfers between devices with their start and end apart: 12 -> 11, of which waited for: 4 -> 5; matrix products, arithmetic and copies ran while one was open for 0% -> 0% of each run, Pallas kernels for 19% -> 13%
where the time goes in v3:
time: 105 us; the launch traced here: 104 us
  blocking collectives  50.5 us (48%)
  Pallas kernels  29.3 us (28%)
  starting transfers between devices  15.3 us (15%)
  waiting for transfers between devices  7.2 us (7%)
    all_to_all x3, blocking collectives, exchange(): return lax.all_to_all(a, 'sub', 0, 0)  34.5 us
    all_to_all x1, blocking collectives, shards(): spread_windows = lax.all_to_all(sent, ('tracer', 'sub'), 0, 0)  16 us
    pallas_call x1, Pallas kernels, shards(): call(functools.partial(composites_kernel, blocks, scale), (shape(AUG, B),...  7.69 us
    pallas_call x1, Pallas kernels, shards(): call(functools.partial(prefixes_kernel, blocks, scale), (near(blocks, ROW...  7.66 us
    pallas_call x1, Pallas kernels, shards(): call(functools.partial(lines_kernel, blocks), (near(blocks, ROWS + B, B),...  5.77 us
    ppermute x5, starting transfers between devices, swap(): return lax.ppermute(a, 'sub', [(d, d ^ 1) for d in range(32)])  5.34 us
    ppermute x3, starting transfers between devices, along_y(): return lax.ppermute(a, 'sub', pairs)  4.99 us
    ppermute x3, starting transfers between devices, along_x(): return lax.ppermute(a, 'sub', pairs)  4.96 us
  transfers between devices with their start and end apart: 11, of which 5 were waited for; matrix products, arithmetic and copies ran while one was open for 0% of the time, Pallas kernels for 13%

profile of v3, /device:TPU:1, one launch (start us, length us, event | category | flops | bytes accessed | tf_op | source)
XLA Modules:
  0.0 104.3 jit_solution(15805763244263893673)
XLA Ops:
  0.6 0.7 copy-done.2
  1.3 7.7 %composites.1 = (f32[264,256]{1,0:T(8,128)S(1)}, f32[264,256]{1,0:T(8,128)S(1)}, f32[16,256,256]{2,1,0:T(8,128)S(1)}, f32[16,256,256]{2,1,0:T(8,128)S(1)}) custom-call(f32[16,256,256]{2,1,0:T(8,128)} %bitcast.7, f32[16,256,256]{2,1,0:T(8,128)} %bitcast.8, f32[16,256]{1,0:T(8,128)} %bitcast.5, s32[16,256]{1,0:T(8,128)} %reg_ref.1, f32[600]{0:T(1024)S(1)} %copy-done.2), custom_call_target="tpu_custom_call" | custom-call | flops 3221225472 | bytes 8388608 | tf_op jit(solution)/shard_map/composites/pallas_call | solution.py:537
  9.0 1.5 %collective-permute-start = (f32[264,256]{1,0:T(8,128)S(1)}, f32[264,256]{1,0:T(8,128)S(1)}, u32[]{:S(2)}, u32[]{:S(2)}) collective-permute-start(f32[264,256]{1,0:T(8,128)S(1)} %get-tuple-element.28), channel_id=1, source_target_pairs={{0,1},{1,0},{2,3},{3,2},{4,5},{5,4},{6,7},{7,6},{8,9},{9,8},{10,11... | collective-permute-start | bytes 811016 | tf_op jit(solution)/shard_map/ppermute | solution.py:521
  10.5 1.2 %collective-permute-done.got_ref.near1_ref.got0_ref = f32[264,256]{1,0:T(8,128)S(1)} collective-permute-done((f32[264,256]{1,0:T(8,128)S(1)}, f32[264,256]{1,0:T(8,128)S(1)}, u32[]{:S(2)}, u32[]{:S(2)}) %collective-permute-start) | collective-permute-done | bytes 270368 | tf_op jit(solution)/shard_map/ppermute | solution.py:521
  11.7 0.3 chip.1.dep_ref.own_ref
  12.0 1.4 %collective-permute-start.3 = (f32[264,256]{1,0:T(8,128)S(1)}, f32[264,256]{1,0:T(8,128)S(1)}, u32[]{:S(2)}, u32[]{:S(2)}) collective-permute-start(f32[264,256]{1,0:T(8,128)S(1)} %chip.1.dep_ref.own_ref), channel_id=1, source_target_pairs={{0,6},{2,0},{4,2},{6,4},{8,14},{10,8},{12,10},{14,12},{16,22},{18,... | collective-permute-start | bytes 811016 | tf_op jit(solution)/shard_map/ppermute | solution.py:526
  13.4 2.4 %collective-permute-start.2 = (f32[264,256]{1,0:T(8,128)S(1)}, f32[264,256]{1,0:T(8,128)S(1)}, u32[]{:S(2)}, u32[]{:S(2)}) collective-permute-start(f32[264,256]{1,0:T(8,128)S(1)} %chip.1.dep_ref.own_ref), channel_id=1, source_target_pairs={{0,4},{2,6},{4,0},{6,2},{8,12},{10,14},{12,8},{14,10},{16,20},{18,... | collective-permute-start | bytes 811016 | tf_op jit(solution)/shard_map/ppermute | solution.py:526
  15.8 1.2 %collective-permute-start.1 = (f32[264,256]{1,0:T(8,128)S(1)}, f32[264,256]{1,0:T(8,128)S(1)}, u32[]{:S(2)}, u32[]{:S(2)}) collective-permute-start(f32[264,256]{1,0:T(8,128)S(1)} %chip.1.dep_ref.own_ref), channel_id=1, source_target_pairs={{0,2},{2,4},{4,6},{6,0},{8,10},{10,12},{12,14},{14,8},{16,18},{18,... | collective-permute-start | bytes 811016 | tf_op jit(solution)/shard_map/ppermute | solution.py:526
  17.0 7.7 %prefixes.1 = (f32[16,288,256]{2,1,0:T(8,128)S(1)}, f32[32,256]{1,0:T(8,128)S(1)}, f32[16,256]{1,0:T(8,128)S(1)}, f32[16,256]{1,0:T(8,128)S(1)}, f32[32,128]{1,0:T(8,128)S(1)}) custom-call(f32[16,256,256]{2,1,0:T(8,128)S(1)} %get-tuple-element.29.low, f32[16,256,256]{2,1,0:T(8,128)} %bitcast.9, f32[16,256]{1,0:T(8,128)S(1)} %bitcast.6, ...), custom_call_target="tpu_custom_call" | custom-call | flops 3221225472 | bytes 8388608 | tf_op jit(solution)/shard_map/prefixes/pallas_call | solution.py:551
  24.7 1.0 collective-permute-done.2.r2_ref
  25.7 1.6 %collective-permute-done.1.r1_ref = f32[264,256]{1,0:T(8,128)S(1)} collective-permute-done((f32[264,256]{1,0:T(8,128)S(1)}, f32[264,256]{1,0:T(8,128)S(1)}, u32[]{:S(2)}, u32[]{:S(2)}) %collective-permute-start.1) | collective-permute-done | bytes 270368 | tf_op jit(solution)/shard_map/ppermute | solution.py:526
  27.3 1.3 %line.1 = (f32[5,264,256]{2,1,0:T(8,128)S(1)}, f32[264,256]{1,0:T(8,128)S(1)}, f32[8,256]{1,0:T(8,128)S(1)}) custom-call(f32[264,256]{1,0:T(8,128)S(1)} %chip.1.dep_ref.own_ref, f32[264,256]{1,0:T(8,128)S(1)} %get-tuple-element.27.own_ref.mine_ref, f32[264,256]{1,0:T(8,128)S(1)} %collective-permute-done.1.r1_ref, ...), custom_call_target="tpu_custom_call" | custom-call | flops 603979776 | tf_op jit(solution)/shard_map/line/pallas_call | solution.py:561
  28.6 2.0 %collective-permute-start.8 = (f32[5,264,256]{2,1,0:T(8,128)S(1)}, f32[5,264,256]{2,1,0:T(8,128)S(1)}, u32[]{:S(2)}, u32[]{:S(2)}) collective-permute-start(f32[5,264,256]{2,1,0:T(8,128)S(1)} %get-tuple-element.31.maps_ref), channel_id=1, source_target_pairs={{0,1},{1,0},{2,3},{3,2},{4,5},{5,4},{6,7},{7,6},{8,9},{9,8},{10,11... | collective-permute-start | bytes 4055048 | tf_op jit(solution)/shard_map/ppermute | solution.py:521
  30.6 1.3 %collective-permute-start.6 = (f32[8,256]{1,0:T(8,128)S(1)}, f32[8,256]{1,0:T(8,128)S(1)}, u32[]{:S(2)}, u32[]{:S(2)}) collective-permute-start(f32[8,256]{1,0:T(8,128)S(1)} %get-tuple-element.33), channel_id=1, source_target_pairs={{0,24},{2,26},{4,28},{6,30},{8,0},{10,2},{12,4},{14,6},{16,8},{18,... | collective-permute-start | bytes 24584 | tf_op jit(solution)/shard_map/ppermute | solution.py:531
  31.9 2.6 %collective-permute-start.5 = (f32[264,256]{1,0:T(8,128)S(1)}, f32[264,256]{1,0:T(8,128)S(1)}, u32[]{:S(2)}, u32[]{:S(2)}) collective-permute-start(f32[264,256]{1,0:T(8,128)S(1)} %get-tuple-element.32), channel_id=1, source_target_pairs={{0,16},{2,18},{4,20},{6,22},{8,24},{10,26},{12,28},{14,30},{16,0},... | collective-permute-start | bytes 811016 | tf_op jit(solution)/shard_map/ppermute | solution.py:531
  34.5 1.1 %collective-permute-start.4 = (f32[264,256]{1,0:T(8,128)S(1)}, f32[264,256]{1,0:T(8,128)S(1)}, u32[]{:S(2)}, u32[]{:S(2)}) collective-permute-start(f32[264,256]{1,0:T(8,128)S(1)} %get-tuple-element.32), channel_id=1, source_target_pairs={{0,8},{2,10},{4,12},{6,14},{8,16},{10,18},{12,20},{14,22},{16,24},... | collective-permute-start | bytes 811016 | tf_op jit(solution)/shard_map/ppermute | solution.py:531
  35.6 5.8 %lines.1 = (f32[16,544,256]{2,1,0:T(8,128)S(1)}, f32[8,128]{1,0:T(8,128)S(1)}) custom-call(f32[16,256,256]{2,1,0:T(8,128)S(1)} %get-tuple-element.34.up, f32[16,288,256]{2,1,0:T(8,128)S(1)} %get-tuple-element.35.z_ref, f32[8,256]{1,0:T(8,128)S(1)} %collective-permute-done.6.dep_ref.t3_ref), custom_call_target="tpu_custom_call" | custom-call | flops 4831838208 | bytes 8388608 | tf_op jit(solution)/shard_map/lines/pallas_call | solution.py:567
  41.4 2.5 %collective-permute-done.4.y1_ref = f32[264,256]{1,0:T(8,128)S(1)} collective-permute-done((f32[264,256]{1,0:T(8,128)S(1)}, f32[264,256]{1,0:T(8,128)S(1)}, u32[]{:S(2)}, u32[]{:S(2)}) %collective-permute-start.4) | collective-permute-done | bytes 270368 | tf_op jit(solution)/shard_map/ppermute | solution.py:531
  43.9 1.3 %collective-permute-start.9 = (f32[264,256]{1,0:T(8,128)S(1)}, f32[264,256]{1,0:T(8,128)S(1)}, u32[]{:S(2)}, u32[]{:S(2)}) collective-permute-start(f32[264,256]{1,0:T(8,128)S(1)} %collective-permute-done.4.y1_ref), channel_id=1, source_target_pairs={{0,1},{1,0},{2,3},{3,2},{4,5},{5,4},{6,7},{7,6},{8,9},{9,8},{10,11... | collective-permute-start | bytes 811016 | tf_op jit(solution)/shard_map/ppermute | solution.py:521
  45.2 0.5 entering.1
  45.7 0.6 collective-permute-start.7
  46.3 0.8 collective-permute-done.7.got_ref
  47.1 0.4 start.1
  47.6 13.0 %all_to_all.20.got_ref = f32[32,2,128]{2,1,0:T(2,128)S(1)} all-to-all(f32[32,2,128]{2,1,0:T(2,128)S(1)} %get-tuple-element.43), channel_id=1, replica_groups=mesh['tracer'=4,'sub'=32] {'sub'}, dimensions={0} | all-to-all | bytes 65536 | tf_op jit(solution)/shard_map/all_to_all | solution.py:534
  60.6 3.6 %middle.1 = (f32[16,256]{1,0:T(8,128)}, f32[32,2,128]{2,1,0:T(2,128)S(1)}, f32[288,128]{1,0:T(8,128)S(1)}) custom-call(f32[32,2,128]{2,1,0:T(2,128)S(1)} %all_to_all.20.got_ref, f32[264,256]{1,0:T(8,128)S(1)} %collective-permute-done.got_ref.near1_ref.got0_ref, f32[5,264,256]{2,1,0:T(8,128)S(1)} %get-tuple-element.31.maps_ref, ...), custom_call_target="tpu_custom_call" | custom-call | tf_op jit(solution)/shard_map/middle/pallas_call | solution.py:584
  64.2 10.7 %all_to_all.21.got_ref = f32[32,2,128]{2,1,0:T(2,128)S(1)} all-to-all(f32[32,2,128]{2,1,0:T(2,128)S(1)} %get-tuple-element.46), channel_id=1, replica_groups=mesh['tracer'=4,'sub'=32] {'sub'}, dimensions={0} | all-to-all | bytes 65536 | tf_op jit(solution)/shard_map/all_to_all | solution.py:534
  74.9 1.4 %return.1 = (f32[32,2,128]{2,1,0:T(2,128)S(1)}, f32[32,128]{1,0:T(8,128)S(1)}) custom-call(f32[32,2,128]{2,1,0:T(2,128)S(1)} %all_to_all.21.got_ref, f32[264,256]{1,0:T(8,128)S(1)} %collective-permute-done.got_ref.near1_ref.got0_ref, f32[5,264,256]{2,1,0:T(8,128)S(1)} %get-tuple-element.31.maps_ref, f32[5,264,256]{2,1,0:T(8,128)S(1)} %collective-permute-done.8.mapso_ref, ...), custom_call_target="tpu_custom_call" | custom-call | tf_op jit(solution)/shard_map/return/pallas_call | solution.py:592
  76.3 10.7 %all_to_all.22.got_ref = f32[32,2,128]{2,1,0:T(2,128)S(1)} all-to-all(f32[32,2,128]{2,1,0:T(2,128)S(1)} %get-tuple-element.48), channel_id=1, replica_groups=mesh['tracer'=4,'sub'=32] {'sub'}, dimensions={0} | all-to-all | bytes 65536 | tf_op jit(solution)/shard_map/all_to_all | solution.py:534
  87.1 0.5 window.1
  87.6 16.0 %all_to_all.23.got_ref = f32[128,1,128]{2,1,0:T(1,128)S(1)} all-to-all(f32[128,1,128]{2,1,0:T(1,128)S(1)} %window.1), channel_id=1, replica_groups=mesh['tracer'=4,'sub'=32] {'tracer','sub'}, dimensions={0} | all-to-all | bytes 131072 | tf_op jit(solution)/shard_map/all_to_all | solution.py:599
  103.6 0.1 total.1
  103.7 0.6 reduce
  (18 shorter events, 0.0 us)
Async XLA Ops:
  0.6 0.7 copy-start.2
  1.3 15.6 %copy-start = (f32[1,16,256]{2,1,0:T(8,128)S(1)}, f32[1,16,256]{2,1,0:T(8,128)}, u32[]{:S(2)}) copy-start(f32[1,16,256]{2,1,0:T(8,128)} %param.11) | copy-start | bytes 49156
  1.3 15.6 %copy-start.1 = (s32[16,256]{1,0:T(8,128)S(1)}, s32[16,256]{1,0:T(8,128)}, u32[]{:S(2)}) copy-start(s32[16,256]{1,0:T(8,128)} %reg_ref.1) | copy-start | bytes 49156
  1.3 15.6 %copy-start.3 = (f32[600]{0:T(1024)S(1)}, f32[600]{0:T(1024)}, u32[]{:S(2)}) copy-start(f32[600]{0:T(1024)} %par_ref.1) | copy-start | bytes 7204
  1.3 15.6 %copy-start.4 = (s32[1,256]{1,0:T(1,128)S(1)}, s32[1,256]{1,0:T(1,128)}, u32[]{:S(2)}) copy-start(s32[1,256]{1,0:T(1,128)} %cells_ref.1) | copy-start | bytes 3076
  1.3 15.6 %copy-start.5 = (f32[1,256]{1,0:T(1,128)S(1)}, f32[1,256]{1,0:T(1,128)}, u32[]{:S(2)}) copy-start(f32[1,256]{1,0:T(1,128)} %values_ref.1) | copy-start | bytes 3076
  9.0 2.7 %collective-permute-start = (f32[264,256]{1,0:T(8,128)S(1)}, f32[264,256]{1,0:T(8,128)S(1)}, u32[]{:S(2)}, u32[]{:S(2)}) collective-permute-start(f32[264,256]{1,0:T(8,128)S(1)} %get-tuple-element.28), channel_id=1, source_target_pairs={{0,1},{1,0},{2,3},{3,2},{4,5},{5,4},{6,7},{7,6},{8,9},{9,8},{10,11... | collective-permute-start | bytes 811016 | tf_op jit(solution)/shard_map/ppermute | solution.py:521
  12.0 12.7 %collective-permute-start.3 = (f32[264,256]{1,0:T(8,128)S(1)}, f32[264,256]{1,0:T(8,128)S(1)}, u32[]{:S(2)}, u32[]{:S(2)}) collective-permute-start(f32[264,256]{1,0:T(8,128)S(1)} %chip.1.dep_ref.own_ref), channel_id=1, source_target_pairs={{0,6},{2,0},{4,2},{6,4},{8,14},{10,8},{12,10},{14,12},{16,22},{18,... | collective-permute-start | bytes 811016 | tf_op jit(solution)/shard_map/ppermute | solution.py:526
  13.4 12.3 %collective-permute-start.2 = (f32[264,256]{1,0:T(8,128)S(1)}, f32[264,256]{1,0:T(8,128)S(1)}, u32[]{:S(2)}, u32[]{:S(2)}) collective-permute-start(f32[264,256]{1,0:T(8,128)S(1)} %chip.1.dep_ref.own_ref), channel_id=1, source_target_pairs={{0,4},{2,6},{4,0},{6,2},{8,12},{10,14},{12,8},{14,10},{16,20},{18,... | collective-permute-start | bytes 811016 | tf_op jit(solution)/shard_map/ppermute | solution.py:526
  15.8 11.5 %collective-permute-start.1 = (f32[264,256]{1,0:T(8,128)S(1)}, f32[264,256]{1,0:T(8,128)S(1)}, u32[]{:S(2)}, u32[]{:S(2)}) collective-permute-start(f32[264,256]{1,0:T(8,128)S(1)} %chip.1.dep_ref.own_ref), channel_id=1, source_target_pairs={{0,2},{2,4},{4,6},{6,0},{8,10},{10,12},{12,14},{14,8},{16,18},{18,... | collective-permute-start | bytes 811016 | tf_op jit(solution)/shard_map/ppermute | solution.py:526
  28.6 18.5 %collective-permute-start.8 = (f32[5,264,256]{2,1,0:T(8,128)S(1)}, f32[5,264,256]{2,1,0:T(8,128)S(1)}, u32[]{:S(2)}, u32[]{:S(2)}) collective-permute-start(f32[5,264,256]{2,1,0:T(8,128)S(1)} %get-tuple-element.31.maps_ref), channel_id=1, source_target_pairs={{0,1},{1,0},{2,3},{3,2},{4,5},{5,4},{6,7},{7,6},{8,9},{9,8},{10,11... | collective-permute-start | bytes 4055048 | tf_op jit(solution)/shard_map/ppermute | solution.py:521
  30.6 5.0 %collective-permute-start.6 = (f32[8,256]{1,0:T(8,128)S(1)}, f32[8,256]{1,0:T(8,128)S(1)}, u32[]{:S(2)}, u32[]{:S(2)}) collective-permute-start(f32[8,256]{1,0:T(8,128)S(1)} %get-tuple-element.33), channel_id=1, source_target_pairs={{0,24},{2,26},{4,28},{6,30},{8,0},{10,2},{12,4},{14,6},{16,8},{18,... | collective-permute-start | bytes 24584 | tf_op jit(solution)/shard_map/ppermute | solution.py:531
  31.9 9.5 %collective-permute-start.5 = (f32[264,256]{1,0:T(8,128)S(1)}, f32[264,256]{1,0:T(8,128)S(1)}, u32[]{:S(2)}, u32[]{:S(2)}) collective-permute-start(f32[264,256]{1,0:T(8,128)S(1)} %get-tuple-element.32), channel_id=1, source_target_pairs={{0,16},{2,18},{4,20},{6,22},{8,24},{10,26},{12,28},{14,30},{16,0},... | collective-permute-start | bytes 811016 | tf_op jit(solution)/shard_map/ppermute | solution.py:531
  34.5 9.4 %collective-permute-start.4 = (f32[264,256]{1,0:T(8,128)S(1)}, f32[264,256]{1,0:T(8,128)S(1)}, u32[]{:S(2)}, u32[]{:S(2)}) collective-permute-start(f32[264,256]{1,0:T(8,128)S(1)} %get-tuple-element.32), channel_id=1, source_target_pairs={{0,8},{2,10},{4,12},{6,14},{8,16},{10,18},{12,20},{14,22},{16,24},... | collective-permute-start | bytes 811016 | tf_op jit(solution)/shard_map/ppermute | solution.py:531
  43.9 3.2 %collective-permute-start.9 = (f32[264,256]{1,0:T(8,128)S(1)}, f32[264,256]{1,0:T(8,128)S(1)}, u32[]{:S(2)}, u32[]{:S(2)}) collective-permute-start(f32[264,256]{1,0:T(8,128)S(1)} %collective-permute-done.4.y1_ref), channel_id=1, source_target_pairs={{0,1},{1,0},{2,3},{3,2},{4,5},{5,4},{6,7},{7,6},{8,9},{9,8},{10,11... | collective-permute-start | bytes 811016 | tf_op jit(solution)/shard_map/ppermute | solution.py:521
  45.2 1.9 %collective-permute-start.10 = (f32[264,256]{1,0:T(8,128)S(1)}, f32[264,256]{1,0:T(8,128)S(1)}, u32[]{:S(2)}, u32[]{:S(2)}) collective-permute-start(f32[264,256]{1,0:T(8,128)S(1)} %collective-permute-done.5.y2_ref), channel_id=1, source_target_pairs={{0,1},{1,0},{2,3},{3,2},{4,5},{5,4},{6,7},{7,6},{8,9},{9,8},{10,11... | collective-permute-start | bytes 811016 | tf_op jit(solution)/shard_map/ppermute | solution.py:521
  45.7 1.4 %collective-permute-start.7 = (f32[8,256]{1,0:T(8,128)S(1)}, f32[8,256]{1,0:T(8,128)S(1)}, u32[]{:S(2)}, u32[]{:S(2)}) collective-permute-start(f32[8,256]{1,0:T(8,128)S(1)} %get-tuple-element.38), channel_id=1, source_target_pairs={{0,1},{1,0},{2,3},{3,2},{4,5},{5,4},{6,7},{7,6},{8,9},{9,8},{10,11... | collective-permute-start | bytes 24584 | tf_op jit(solution)/shard_map/ppermute | solution.py:521

commit v4 on v3

--- a/solution.py
+++ b/solution.py
@@ -17,7 +17,7 @@
 NN = (((1,), (0,)), ((), ()))
 MIB = 1 << 20
 PARTS = 4
-DEPTH = 2
+DEPTH = 3
 VM = pl.BlockSpec(memory_space=pltpu.VMEM)
 SM = pl.BlockSpec(memory_space=pltpu.SMEM)
 ANY = pl.BlockSpec(memory_space=pl.ANY)

time: 105 us -> 105 us (level)
  no operation moved by 1% of the time
where the time goes in v4:
time: 105 us
  blocking collectives  50.5 us (48%)
  Pallas kernels  29.9 us (28%)
  starting transfers between devices  15.3 us (15%)
  waiting for transfers between devices  7.19 us (7%)
    all_to_all x3, blocking collectives, exchange(): return lax.all_to_all(a, 'sub', 0, 0)  34.5 us
    all_to_all x1, blocking collectives, shards(): spread_windows = lax.all_to_all(sent, ('tracer', 'sub'), 0, 0)  16 us
    pallas_call x1, Pallas kernels, shards(): call(functools.partial(composites_kernel, blocks, scale), (shape(AUG, B),...  8.33 us
    pallas_call x1, Pallas kernels, shards(): call(functools.partial(prefixes_kernel, blocks, scale), (near(blocks, ROW...  7.67 us
    pallas_call x1, Pallas kernels, shards(): call(functools.partial(lines_kernel, blocks), (near(blocks, ROWS + B, B),...  5.77 us
    ppermute x5, starting transfers between devices, swap(): return lax.ppermute(a, 'sub', [(d, d ^ 1) for d in range(32)])  5.34 us
    ppermute x3, starting transfers between devices, along_y(): return lax.ppermute(a, 'sub', pairs)  4.99 us
    ppermute x3, starting transfers between devices, along_x(): return lax.ppermute(a, 'sub', pairs)  4.97 us
  transfers between devices with their start and end apart: 11, of which 5 were waited for; matrix products, arithmetic and copies ran while one was open for 0% of the time, Pallas kernels for 13%

profile of v4, /device:TPU:1, one launch (start us, length us, event | category | flops | bytes accessed | tf_op | source)
XLA Modules:
  0.0 104.9 jit_solution(13647059202079370733)
XLA Ops:
  0.6 0.7 copy-done.2
  1.3 8.3 %composites.1 = (f32[264,256]{1,0:T(8,128)S(1)}, f32[264,256]{1,0:T(8,128)S(1)}, f32[16,256,256]{2,1,0:T(8,128)S(1)}, f32[16,256,256]{2,1,0:T(8,128)S(1)}) custom-call(f32[16,256,256]{2,1,0:T(8,128)} %bitcast.7, f32[16,256,256]{2,1,0:T(8,128)} %bitcast.8, f32[16,256]{1,0:T(8,128)} %bitcast.5, s32[16,256]{1,0:T(8,128)} %reg_ref.1, f32[600]{0:T(1024)S(1)} %copy-done.2), custom_call_target="tpu_custom_call" | custom-call | flops 3221225472 | bytes 8388608 | tf_op jit(solution)/shard_map/composites/pallas_call | solution.py:537
  9.7 1.5 %collective-permute-start = (f32[264,256]{1,0:T(8,128)S(1)}, f32[264,256]{1,0:T(8,128)S(1)}, u32[]{:S(2)}, u32[]{:S(2)}) collective-permute-start(f32[264,256]{1,0:T(8,128)S(1)} %get-tuple-element.28), channel_id=1, source_target_pairs={{0,1},{1,0},{2,3},{3,2},{4,5},{5,4},{6,7},{7,6},{8,9},{9,8},{10,11... | collective-permute-start | bytes 811016 | tf_op jit(solution)/shard_map/ppermute | solution.py:521
  11.2 1.2 %collective-permute-done.got_ref.near1_ref.got0_ref = f32[264,256]{1,0:T(8,128)S(1)} collective-permute-done((f32[264,256]{1,0:T(8,128)S(1)}, f32[264,256]{1,0:T(8,128)S(1)}, u32[]{:S(2)}, u32[]{:S(2)}) %collective-permute-start) | collective-permute-done | bytes 270368 | tf_op jit(solution)/shard_map/ppermute | solution.py:521
  12.3 0.3 chip.1.dep_ref.own_ref
  12.6 1.4 %collective-permute-start.3 = (f32[264,256]{1,0:T(8,128)S(1)}, f32[264,256]{1,0:T(8,128)S(1)}, u32[]{:S(2)}, u32[]{:S(2)}) collective-permute-start(f32[264,256]{1,0:T(8,128)S(1)} %chip.1.dep_ref.own_ref), channel_id=1, source_target_pairs={{0,6},{2,0},{4,2},{6,4},{8,14},{10,8},{12,10},{14,12},{16,22},{18,... | collective-permute-start | bytes 811016 | tf_op jit(solution)/shard_map/ppermute | solution.py:526
  14.0 2.4 %collective-permute-start.2 = (f32[264,256]{1,0:T(8,128)S(1)}, f32[264,256]{1,0:T(8,128)S(1)}, u32[]{:S(2)}, u32[]{:S(2)}) collective-permute-start(f32[264,256]{1,0:T(8,128)S(1)} %chip.1.dep_ref.own_ref), channel_id=1, source_target_pairs={{0,4},{2,6},{4,0},{6,2},{8,12},{10,14},{12,8},{14,10},{16,20},{18,... | collective-permute-start | bytes 811016 | tf_op jit(solution)/shard_map/ppermute | solution.py:526
  16.4 1.2 %collective-permute-start.1 = (f32[264,256]{1,0:T(8,128)S(1)}, f32[264,256]{1,0:T(8,128)S(1)}, u32[]{:S(2)}, u32[]{:S(2)}) collective-permute-start(f32[264,256]{1,0:T(8,128)S(1)} %chip.1.dep_ref.own_ref), channel_id=1, source_target_pairs={{0,2},{2,4},{4,6},{6,0},{8,10},{10,12},{12,14},{14,8},{16,18},{18,... | collective-permute-start | bytes 811016 | tf_op jit(solution)/shard_map/ppermute | solution.py:526
  17.6 7.7 %prefixes.1 = (f32[16,288,256]{2,1,0:T(8,128)S(1)}, f32[32,256]{1,0:T(8,128)S(1)}, f32[16,256]{1,0:T(8,128)S(1)}, f32[16,256]{1,0:T(8,128)S(1)}, f32[32,128]{1,0:T(8,128)S(1)}) custom-call(f32[16,256,256]{2,1,0:T(8,128)S(1)} %get-tuple-element.29.low, f32[16,256,256]{2,1,0:T(8,128)} %bitcast.9, f32[16,256]{1,0:T(8,128)S(1)} %bitcast.6, ...), custom_call_target="tpu_custom_call" | custom-call | flops 3221225472 | bytes 8388608 | tf_op jit(solution)/shard_map/prefixes/pallas_call | solution.py:551
  25.3 1.0 collective-permute-done.2.r2_ref
  26.3 1.6 %collective-permute-done.1.r1_ref = f32[264,256]{1,0:T(8,128)S(1)} collective-permute-done((f32[264,256]{1,0:T(8,128)S(1)}, f32[264,256]{1,0:T(8,128)S(1)}, u32[]{:S(2)}, u32[]{:S(2)}) %collective-permute-start.1) | collective-permute-done | bytes 270368 | tf_op jit(solution)/shard_map/ppermute | solution.py:526
  28.0 1.3 %line.1 = (f32[5,264,256]{2,1,0:T(8,128)S(1)}, f32[264,256]{1,0:T(8,128)S(1)}, f32[8,256]{1,0:T(8,128)S(1)}) custom-call(f32[264,256]{1,0:T(8,128)S(1)} %chip.1.dep_ref.own_ref, f32[264,256]{1,0:T(8,128)S(1)} %get-tuple-element.27.own_ref.mine_ref, f32[264,256]{1,0:T(8,128)S(1)} %collective-permute-done.1.r1_ref, ...), custom_call_target="tpu_custom_call" | custom-call | flops 603979776 | tf_op jit(solution)/shard_map/line/pallas_call | solution.py:561
  29.3 2.0 %collective-permute-start.8 = (f32[5,264,256]{2,1,0:T(8,128)S(1)}, f32[5,264,256]{2,1,0:T(8,128)S(1)}, u32[]{:S(2)}, u32[]{:S(2)}) collective-permute-start(f32[5,264,256]{2,1,0:T(8,128)S(1)} %get-tuple-element.31.maps_ref), channel_id=1, source_target_pairs={{0,1},{1,0},{2,3},{3,2},{4,5},{5,4},{6,7},{7,6},{8,9},{9,8},{10,11... | collective-permute-start | bytes 4055048 | tf_op jit(solution)/shard_map/ppermute | solution.py:521
  31.2 1.3 %collective-permute-start.6 = (f32[8,256]{1,0:T(8,128)S(1)}, f32[8,256]{1,0:T(8,128)S(1)}, u32[]{:S(2)}, u32[]{:S(2)}) collective-permute-start(f32[8,256]{1,0:T(8,128)S(1)} %get-tuple-element.33), channel_id=1, source_target_pairs={{0,24},{2,26},{4,28},{6,30},{8,0},{10,2},{12,4},{14,6},{16,8},{18,... | collective-permute-start | bytes 24584 | tf_op jit(solution)/shard_map/ppermute | solution.py:531
  32.5 2.6 %collective-permute-start.5 = (f32[264,256]{1,0:T(8,128)S(1)}, f32[264,256]{1,0:T(8,128)S(1)}, u32[]{:S(2)}, u32[]{:S(2)}) collective-permute-start(f32[264,256]{1,0:T(8,128)S(1)} %get-tuple-element.32), channel_id=1, source_target_pairs={{0,16},{2,18},{4,20},{6,22},{8,24},{10,26},{12,28},{14,30},{16,0},... | collective-permute-start | bytes 811016 | tf_op jit(solution)/shard_map/ppermute | solution.py:531
  35.2 1.1 %collective-permute-start.4 = (f32[264,256]{1,0:T(8,128)S(1)}, f32[264,256]{1,0:T(8,128)S(1)}, u32[]{:S(2)}, u32[]{:S(2)}) collective-permute-start(f32[264,256]{1,0:T(8,128)S(1)} %get-tuple-element.32), channel_id=1, source_target_pairs={{0,8},{2,10},{4,12},{6,14},{8,16},{10,18},{12,20},{14,22},{16,24},... | collective-permute-start | bytes 811016 | tf_op jit(solution)/shard_map/ppermute | solution.py:531
  36.2 5.8 %lines.1 = (f32[16,544,256]{2,1,0:T(8,128)S(1)}, f32[8,128]{1,0:T(8,128)S(1)}) custom-call(f32[16,256,256]{2,1,0:T(8,128)S(1)} %get-tuple-element.34.up, f32[16,288,256]{2,1,0:T(8,128)S(1)} %get-tuple-element.35.z_ref, f32[8,256]{1,0:T(8,128)S(1)} %collective-permute-done.6.dep_ref.t3_ref), custom_call_target="tpu_custom_call" | custom-call | flops 4831838208 | bytes 8388608 | tf_op jit(solution)/shard_map/lines/pallas_call | solution.py:567
  42.0 2.5 %collective-permute-done.4.y1_ref = f32[264,256]{1,0:T(8,128)S(1)} collective-permute-done((f32[264,256]{1,0:T(8,128)S(1)}, f32[264,256]{1,0:T(8,128)S(1)}, u32[]{:S(2)}, u32[]{:S(2)}) %collective-permute-start.4) | collective-permute-done | bytes 270368 | tf_op jit(solution)/shard_map/ppermute | solution.py:531
  44.5 1.3 %collective-permute-start.9 = (f32[264,256]{1,0:T(8,128)S(1)}, f32[264,256]{1,0:T(8,128)S(1)}, u32[]{:S(2)}, u32[]{:S(2)}) collective-permute-start(f32[264,256]{1,0:T(8,128)S(1)} %collective-permute-done.4.y1_ref), channel_id=1, source_target_pairs={{0,1},{1,0},{2,3},{3,2},{4,5},{5,4},{6,7},{7,6},{8,9},{9,8},{10,11... | collective-permute-start | bytes 811016 | tf_op jit(solution)/shard_map/ppermute | solution.py:521
  45.8 0.5 entering.1
  46.4 0.6 collective-permute-start.7
  46.9 0.8 collective-permute-done.7.got_ref
  47.8 0.4 start.1
  48.2 13.0 %all_to_all.20.got_ref = f32[32,2,128]{2,1,0:T(2,128)S(1)} all-to-all(f32[32,2,128]{2,1,0:T(2,128)S(1)} %get-tuple-element.43), channel_id=1, replica_groups=mesh['tracer'=4,'sub'=32] {'sub'}, dimensions={0} | all-to-all | bytes 65536 | tf_op jit(solution)/shard_map/all_to_all | solution.py:534
  61.2 3.6 %middle.1 = (f32[16,256]{1,0:T(8,128)}, f32[32,2,128]{2,1,0:T(2,128)S(1)}, f32[288,128]{1,0:T(8,128)S(1)}) custom-call(f32[32,2,128]{2,1,0:T(2,128)S(1)} %all_to_all.20.got_ref, f32[264,256]{1,0:T(8,128)S(1)} %collective-permute-done.got_ref.near1_ref.got0_ref, f32[5,264,256]{2,1,0:T(8,128)S(1)} %get-tuple-element.31.maps_ref, ...), custom_call_target="tpu_custom_call" | custom-call | tf_op jit(solution)/shard_map/middle/pallas_call | solution.py:584
  64.8 10.7 %all_to_all.21.got_ref = f32[32,2,128]{2,1,0:T(2,128)S(1)} all-to-all(f32[32,2,128]{2,1,0:T(2,128)S(1)} %get-tuple-element.46), channel_id=1, replica_groups=mesh['tracer'=4,'sub'=32] {'sub'}, dimensions={0} | all-to-all | bytes 65536 | tf_op jit(solution)/shard_map/all_to_all | solution.py:534
  75.5 1.4 %return.1 = (f32[32,2,128]{2,1,0:T(2,128)S(1)}, f32[32,128]{1,0:T(8,128)S(1)}) custom-call(f32[32,2,128]{2,1,0:T(2,128)S(1)} %all_to_all.21.got_ref, f32[264,256]{1,0:T(8,128)S(1)} %collective-permute-done.got_ref.near1_ref.got0_ref, f32[5,264,256]{2,1,0:T(8,128)S(1)} %get-tuple-element.31.maps_ref, f32[5,264,256]{2,1,0:T(8,128)S(1)} %collective-permute-done.8.mapso_ref, ...), custom_call_target="tpu_custom_call" | custom-call | tf_op jit(solution)/shard_map/return/pallas_call | solution.py:592
  77.0 10.7 %all_to_all.22.got_ref = f32[32,2,128]{2,1,0:T(2,128)S(1)} all-to-all(f32[32,2,128]{2,1,0:T(2,128)S(1)} %get-tuple-element.48), channel_id=1, replica_groups=mesh['tracer'=4,'sub'=32] {'sub'}, dimensions={0} | all-to-all | bytes 65536 | tf_op jit(solution)/shard_map/all_to_all | solution.py:534
  87.7 0.5 window.1
  88.3 16.0 %all_to_all.23.got_ref = f32[128,1,128]{2,1,0:T(1,128)S(1)} all-to-all(f32[128,1,128]{2,1,0:T(1,128)S(1)} %window.1), channel_id=1, replica_groups=mesh['tracer'=4,'sub'=32] {'tracer','sub'}, dimensions={0} | all-to-all | bytes 131072 | tf_op jit(solution)/shard_map/all_to_all | solution.py:599
  104.3 0.1 total.1
  104.3 0.6 reduce
  (18 shorter events, 0.0 us)
Async XLA Ops:
  0.6 0.7 copy-start.2
  1.3 16.3 %copy-start = (f32[1,16,256]{2,1,0:T(8,128)S(1)}, f32[1,16,256]{2,1,0:T(8,128)}, u32[]{:S(2)}) copy-start(f32[1,16,256]{2,1,0:T(8,128)} %param.11) | copy-start | bytes 49156
  1.3 16.3 %copy-start.1 = (s32[16,256]{1,0:T(8,128)S(1)}, s32[16,256]{1,0:T(8,128)}, u32[]{:S(2)}) copy-start(s32[16,256]{1,0:T(8,128)} %reg_ref.1) | copy-start | bytes 49156
  1.3 16.3 %copy-start.3 = (f32[600]{0:T(1024)S(1)}, f32[600]{0:T(1024)}, u32[]{:S(2)}) copy-start(f32[600]{0:T(1024)} %par_ref.1) | copy-start | bytes 7204
  1.3 16.3 %copy-start.4 = (s32[1,256]{1,0:T(1,128)S(1)}, s32[1,256]{1,0:T(1,128)}, u32[]{:S(2)}) copy-start(s32[1,256]{1,0:T(1,128)} %cells_ref.1) | copy-start | bytes 3076
  1.3 16.3 %copy-start.5 = (f32[1,256]{1,0:T(1,128)S(1)}, f32[1,256]{1,0:T(1,128)}, u32[]{:S(2)}) copy-start(f32[1,256]{1,0:T(1,128)} %values_ref.1) | copy-start | bytes 3076
  9.7 2.7 %collective-permute-start = (f32[264,256]{1,0:T(8,128)S(1)}, f32[264,256]{1,0:T(8,128)S(1)}, u32[]{:S(2)}, u32[]{:S(2)}) collective-permute-start(f32[264,256]{1,0:T(8,128)S(1)} %get-tuple-element.28), channel_id=1, source_target_pairs={{0,1},{1,0},{2,3},{3,2},{4,5},{5,4},{6,7},{7,6},{8,9},{9,8},{10,11... | collective-permute-start | bytes 811016 | tf_op jit(solution)/shard_map/ppermute | solution.py:521
  12.6 12.7 %collective-permute-start.3 = (f32[264,256]{1,0:T(8,128)S(1)}, f32[264,256]{1,0:T(8,128)S(1)}, u32[]{:S(2)}, u32[]{:S(2)}) collective-permute-start(f32[264,256]{1,0:T(8,128)S(1)} %chip.1.dep_ref.own_ref), channel_id=1, source_target_pairs={{0,6},{2,0},{4,2},{6,4},{8,14},{10,8},{12,10},{14,12},{16,22},{18,... | collective-permute-start | bytes 811016 | tf_op jit(solution)/shard_map/ppermute | solution.py:526
  14.0 12.4 %collective-permute-start.2 = (f32[264,256]{1,0:T(8,128)S(1)}, f32[264,256]{1,0:T(8,128)S(1)}, u32[]{:S(2)}, u32[]{:S(2)}) collective-permute-start(f32[264,256]{1,0:T(8,128)S(1)} %chip.1.dep_ref.own_ref), channel_id=1, source_target_pairs={{0,4},{2,6},{4,0},{6,2},{8,12},{10,14},{12,8},{14,10},{16,20},{18,... | collective-permute-start | bytes 811016 | tf_op jit(solution)/shard_map/ppermute | solution.py:526
  16.4 11.5 %collective-permute-start.1 = (f32[264,256]{1,0:T(8,128)S(1)}, f32[264,256]{1,0:T(8,128)S(1)}, u32[]{:S(2)}, u32[]{:S(2)}) collective-permute-start(f32[264,256]{1,0:T(8,128)S(1)} %chip.1.dep_ref.own_ref), channel_id=1, source_target_pairs={{0,2},{2,4},{4,6},{6,0},{8,10},{10,12},{12,14},{14,8},{16,18},{18,... | collective-permute-start | bytes 811016 | tf_op jit(solution)/shard_map/ppermute | solution.py:526
  29.3 18.5 %collective-permute-start.8 = (f32[5,264,256]{2,1,0:T(8,128)S(1)}, f32[5,264,256]{2,1,0:T(8,128)S(1)}, u32[]{:S(2)}, u32[]{:S(2)}) collective-permute-start(f32[5,264,256]{2,1,0:T(8,128)S(1)} %get-tuple-element.31.maps_ref), channel_id=1, source_target_pairs={{0,1},{1,0},{2,3},{3,2},{4,5},{5,4},{6,7},{7,6},{8,9},{9,8},{10,11... | collective-permute-start | bytes 4055048 | tf_op jit(solution)/shard_map/ppermute | solution.py:521
  31.2 5.0 %collective-permute-start.6 = (f32[8,256]{1,0:T(8,128)S(1)}, f32[8,256]{1,0:T(8,128)S(1)}, u32[]{:S(2)}, u32[]{:S(2)}) collective-permute-start(f32[8,256]{1,0:T(8,128)S(1)} %get-tuple-element.33), channel_id=1, source_target_pairs={{0,24},{2,26},{4,28},{6,30},{8,0},{10,2},{12,4},{14,6},{16,8},{18,... | collective-permute-start | bytes 24584 | tf_op jit(solution)/shard_map/ppermute | solution.py:531
  32.5 9.5 %collective-permute-start.5 = (f32[264,256]{1,0:T(8,128)S(1)}, f32[264,256]{1,0:T(8,128)S(1)}, u32[]{:S(2)}, u32[]{:S(2)}) collective-permute-start(f32[264,256]{1,0:T(8,128)S(1)} %get-tuple-element.32), channel_id=1, source_target_pairs={{0,16},{2,18},{4,20},{6,22},{8,24},{10,26},{12,28},{14,30},{16,0},... | collective-permute-start | bytes 811016 | tf_op jit(solution)/shard_map/ppermute | solution.py:531
  35.2 9.4 %collective-permute-start.4 = (f32[264,256]{1,0:T(8,128)S(1)}, f32[264,256]{1,0:T(8,128)S(1)}, u32[]{:S(2)}, u32[]{:S(2)}) collective-permute-start(f32[264,256]{1,0:T(8,128)S(1)} %get-tuple-element.32), channel_id=1, source_target_pairs={{0,8},{2,10},{4,12},{6,14},{8,16},{10,18},{12,20},{14,22},{16,24},... | collective-permute-start | bytes 811016 | tf_op jit(solution)/shard_map/ppermute | solution.py:531
  44.5 3.2 %collective-permute-start.9 = (f32[264,256]{1,0:T(8,128)S(1)}, f32[264,256]{1,0:T(8,128)S(1)}, u32[]{:S(2)}, u32[]{:S(2)}) collective-permute-start(f32[264,256]{1,0:T(8,128)S(1)} %collective-permute-done.4.y1_ref), channel_id=1, source_target_pairs={{0,1},{1,0},{2,3},{3,2},{4,5},{5,4},{6,7},{7,6},{8,9},{9,8},{10,11... | collective-permute-start | bytes 811016 | tf_op jit(solution)/shard_map/ppermute | solution.py:521
  45.8 1.9 %collective-permute-start.10 = (f32[264,256]{1,0:T(8,128)S(1)}, f32[264,256]{1,0:T(8,128)S(1)}, u32[]{:S(2)}, u32[]{:S(2)}) collective-permute-start(f32[264,256]{1,0:T(8,128)S(1)} %collective-permute-done.5.y2_ref), channel_id=1, source_target_pairs={{0,1},{1,0},{2,3},{3,2},{4,5},{5,4},{6,7},{7,6},{8,9},{9,8},{10,11... | collective-permute-start | bytes 811016 | tf_op jit(solution)/shard_map/ppermute | solution.py:521
  46.4 1.4 %collective-permute-start.7 = (f32[8,256]{1,0:T(8,128)S(1)}, f32[8,256]{1,0:T(8,128)S(1)}, u32[]{:S(2)}, u32[]{:S(2)}) collective-permute-start(f32[8,256]{1,0:T(8,128)S(1)} %get-tuple-element.38), channel_id=1, source_target_pairs={{0,1},{1,0},{2,3},{3,2},{4,5},{5,4},{6,7},{7,6},{8,9},{9,8},{10,11... | collective-permute-start | bytes 24584 | tf_op jit(solution)/shard_map/ppermute | solution.py:521

commit v5 on v3

--- a/solution.py
+++ b/solution.py
@@ -153,8 +153,7 @@
 
     for c in extras:
         c.start()
-    for k in range(DEPTH):
-        begin(k)
+    begin(0)
     y, x, core = place()
     count = par.shape[0]
     base = window_base(blocks, count)
@@ -165,6 +164,8 @@
     for w in range(WIN):
         value = jnp.where(rel == w, par[jnp.clip(base + w, 0, count - 1)], value)
     src[...] = scale * pat[...] * value
+    for k in range(1, DEPTH):
+        begin(k)
     for k in range(run):
         for c in copies(k):
             c.wait()

time: 105 us -> 105 us (level)
  no operation moved by 1% of the time
where the time goes in v5:
time: 105 us
  blocking collectives  50.5 us (48%)
  Pallas kernels  29.5 us (28%)
  starting transfers between devices  15.3 us (15%)
  waiting for transfers between devices  7.21 us (7%)
    all_to_all x3, blocking collectives, exchange(): return lax.all_to_all(a, 'sub', 0, 0)  34.5 us
    all_to_all x1, blocking collectives, shards(): spread_windows = lax.all_to_all(sent, ('tracer', 'sub'), 0, 0)  16 us
    pallas_call x1, Pallas kernels, shards(): call(functools.partial(composites_kernel, blocks, scale), (shape(AUG, B),...  7.91 us
    pallas_call x1, Pallas kernels, shards(): call(functools.partial(prefixes_kernel, blocks, scale), (near(blocks, ROW...  7.66 us
    pallas_call x1, Pallas kernels, shards(): call(functools.partial(lines_kernel, blocks), (near(blocks, ROWS + B, B),...  5.77 us
    ppermute x5, starting transfers between devices, swap(): return lax.ppermute(a, 'sub', [(d, d ^ 1) for d in range(32)])  5.35 us
    ppermute x3, starting transfers between devices, along_y(): return lax.ppermute(a, 'sub', pairs)  4.97 us
    ppermute x3, starting transfers between devices, along_x(): return lax.ppermute(a, 'sub', pairs)  4.96 us
  transfers between devices with their start and end apart: 11, of which 5 were waited for; matrix products, arithmetic and copies ran while one was open for 0% of the time, Pallas kernels for 13%

profile of v5, /device:TPU:1, one launch (start us, length us, event | category | flops | bytes accessed | tf_op | source)
XLA Modules:
  0.0 104.5 jit_solution(8776601632650049493)
XLA Ops:
  0.6 0.7 copy-done.2
  1.3 7.9 %composites.1 = (f32[264,256]{1,0:T(8,128)S(1)}, f32[264,256]{1,0:T(8,128)S(1)}, f32[16,256,256]{2,1,0:T(8,128)S(1)}, f32[16,256,256]{2,1,0:T(8,128)S(1)}) custom-call(f32[16,256,256]{2,1,0:T(8,128)} %bitcast.7, f32[16,256,256]{2,1,0:T(8,128)} %bitcast.8, f32[16,256]{1,0:T(8,128)} %bitcast.5, s32[16,256]{1,0:T(8,128)} %reg_ref.1, f32[600]{0:T(1024)S(1)} %copy-done.2), custom_call_target="tpu_custom_call" | custom-call | flops 3221225472 | bytes 8388608 | tf_op jit(solution)/shard_map/composites/pallas_call | solution.py:538
  9.3 1.5 %collective-permute-start = (f32[264,256]{1,0:T(8,128)S(1)}, f32[264,256]{1,0:T(8,128)S(1)}, u32[]{:S(2)}, u32[]{:S(2)}) collective-permute-start(f32[264,256]{1,0:T(8,128)S(1)} %get-tuple-element.28), channel_id=1, source_target_pairs={{0,1},{1,0},{2,3},{3,2},{4,5},{5,4},{6,7},{7,6},{8,9},{9,8},{10,11... | collective-permute-start | bytes 811016 | tf_op jit(solution)/shard_map/ppermute | solution.py:522
  10.8 1.2 %collective-permute-done.got_ref.near1_ref.got0_ref = f32[264,256]{1,0:T(8,128)S(1)} collective-permute-done((f32[264,256]{1,0:T(8,128)S(1)}, f32[264,256]{1,0:T(8,128)S(1)}, u32[]{:S(2)}, u32[]{:S(2)}) %collective-permute-start) | collective-permute-done | bytes 270368 | tf_op jit(solution)/shard_map/ppermute | solution.py:522
  11.9 0.3 chip.1.dep_ref.own_ref
  12.2 1.4 %collective-permute-start.3 = (f32[264,256]{1,0:T(8,128)S(1)}, f32[264,256]{1,0:T(8,128)S(1)}, u32[]{:S(2)}, u32[]{:S(2)}) collective-permute-start(f32[264,256]{1,0:T(8,128)S(1)} %chip.1.dep_ref.own_ref), channel_id=1, source_target_pairs={{0,6},{2,0},{4,2},{6,4},{8,14},{10,8},{12,10},{14,12},{16,22},{18,... | collective-permute-start | bytes 811016 | tf_op jit(solution)/shard_map/ppermute | solution.py:527
  13.6 2.4 %collective-permute-start.2 = (f32[264,256]{1,0:T(8,128)S(1)}, f32[264,256]{1,0:T(8,128)S(1)}, u32[]{:S(2)}, u32[]{:S(2)}) collective-permute-start(f32[264,256]{1,0:T(8,128)S(1)} %chip.1.dep_ref.own_ref), channel_id=1, source_target_pairs={{0,4},{2,6},{4,0},{6,2},{8,12},{10,14},{12,8},{14,10},{16,20},{18,... | collective-permute-start | bytes 811016 | tf_op jit(solution)/shard_map/ppermute | solution.py:527
  16.0 1.1 %collective-permute-start.1 = (f32[264,256]{1,0:T(8,128)S(1)}, f32[264,256]{1,0:T(8,128)S(1)}, u32[]{:S(2)}, u32[]{:S(2)}) collective-permute-start(f32[264,256]{1,0:T(8,128)S(1)} %chip.1.dep_ref.own_ref), channel_id=1, source_target_pairs={{0,2},{2,4},{4,6},{6,0},{8,10},{10,12},{12,14},{14,8},{16,18},{18,... | collective-permute-start | bytes 811016 | tf_op jit(solution)/shard_map/ppermute | solution.py:527
  17.2 7.7 %prefixes.1 = (f32[16,288,256]{2,1,0:T(8,128)S(1)}, f32[32,256]{1,0:T(8,128)S(1)}, f32[16,256]{1,0:T(8,128)S(1)}, f32[16,256]{1,0:T(8,128)S(1)}, f32[32,128]{1,0:T(8,128)S(1)}) custom-call(f32[16,256,256]{2,1,0:T(8,128)S(1)} %get-tuple-element.29.low, f32[16,256,256]{2,1,0:T(8,128)} %bitcast.9, f32[16,256]{1,0:T(8,128)S(1)} %bitcast.6, ...), custom_call_target="tpu_custom_call" | custom-call | flops 3221225472 | bytes 8388608 | tf_op jit(solution)/shard_map/prefixes/pallas_call | solution.py:552
  24.9 1.1 %collective-permute-done.2.r2_ref = f32[264,256]{1,0:T(8,128)S(1)} collective-permute-done((f32[264,256]{1,0:T(8,128)S(1)}, f32[264,256]{1,0:T(8,128)S(1)}, u32[]{:S(2)}, u32[]{:S(2)}) %collective-permute-start.2) | collective-permute-done | bytes 270368 | tf_op jit(solution)/shard_map/ppermute | solution.py:527
  25.9 1.6 %collective-permute-done.1.r1_ref = f32[264,256]{1,0:T(8,128)S(1)} collective-permute-done((f32[264,256]{1,0:T(8,128)S(1)}, f32[264,256]{1,0:T(8,128)S(1)}, u32[]{:S(2)}, u32[]{:S(2)}) %collective-permute-start.1) | collective-permute-done | bytes 270368 | tf_op jit(solution)/shard_map/ppermute | solution.py:527
  27.6 1.3 %line.1 = (f32[5,264,256]{2,1,0:T(8,128)S(1)}, f32[264,256]{1,0:T(8,128)S(1)}, f32[8,256]{1,0:T(8,128)S(1)}) custom-call(f32[264,256]{1,0:T(8,128)S(1)} %chip.1.dep_ref.own_ref, f32[264,256]{1,0:T(8,128)S(1)} %get-tuple-element.27.own_ref.mine_ref, f32[264,256]{1,0:T(8,128)S(1)} %collective-permute-done.1.r1_ref, ...), custom_call_target="tpu_custom_call" | custom-call | flops 603979776 | tf_op jit(solution)/shard_map/line/pallas_call | solution.py:562
  28.9 2.0 %collective-permute-start.8 = (f32[5,264,256]{2,1,0:T(8,128)S(1)}, f32[5,264,256]{2,1,0:T(8,128)S(1)}, u32[]{:S(2)}, u32[]{:S(2)}) collective-permute-start(f32[5,264,256]{2,1,0:T(8,128)S(1)} %get-tuple-element.31.maps_ref), channel_id=1, source_target_pairs={{0,1},{1,0},{2,3},{3,2},{4,5},{5,4},{6,7},{7,6},{8,9},{9,8},{10,11... | collective-permute-start | bytes 4055048 | tf_op jit(solution)/shard_map/ppermute | solution.py:522
  30.8 1.3 %collective-permute-start.6 = (f32[8,256]{1,0:T(8,128)S(1)}, f32[8,256]{1,0:T(8,128)S(1)}, u32[]{:S(2)}, u32[]{:S(2)}) collective-permute-start(f32[8,256]{1,0:T(8,128)S(1)} %get-tuple-element.33), channel_id=1, source_target_pairs={{0,24},{2,26},{4,28},{6,30},{8,0},{10,2},{12,4},{14,6},{16,8},{18,... | collective-permute-start | bytes 24584 | tf_op jit(solution)/shard_map/ppermute | solution.py:532
  32.1 2.6 %collective-permute-start.5 = (f32[264,256]{1,0:T(8,128)S(1)}, f32[264,256]{1,0:T(8,128)S(1)}, u32[]{:S(2)}, u32[]{:S(2)}) collective-permute-start(f32[264,256]{1,0:T(8,128)S(1)} %get-tuple-element.32), channel_id=1, source_target_pairs={{0,16},{2,18},{4,20},{6,22},{8,24},{10,26},{12,28},{14,30},{16,0},... | collective-permute-start | bytes 811016 | tf_op jit(solution)/shard_map/ppermute | solution.py:532
  34.7 1.1 %collective-permute-start.4 = (f32[264,256]{1,0:T(8,128)S(1)}, f32[264,256]{1,0:T(8,128)S(1)}, u32[]{:S(2)}, u32[]{:S(2)}) collective-permute-start(f32[264,256]{1,0:T(8,128)S(1)} %get-tuple-element.32), channel_id=1, source_target_pairs={{0,8},{2,10},{4,12},{6,14},{8,16},{10,18},{12,20},{14,22},{16,24},... | collective-permute-start | bytes 811016 | tf_op jit(solution)/shard_map/ppermute | solution.py:532
  35.8 5.8 %lines.1 = (f32[16,544,256]{2,1,0:T(8,128)S(1)}, f32[8,128]{1,0:T(8,128)S(1)}) custom-call(f32[16,256,256]{2,1,0:T(8,128)S(1)} %get-tuple-element.34.up, f32[16,288,256]{2,1,0:T(8,128)S(1)} %get-tuple-element.35.z_ref, f32[8,256]{1,0:T(8,128)S(1)} %collective-permute-done.6.dep_ref.t3_ref), custom_call_target="tpu_custom_call" | custom-call | flops 4831838208 | bytes 8388608 | tf_op jit(solution)/shard_map/lines/pallas_call | solution.py:568
  41.6 2.5 %collective-permute-done.4.y1_ref = f32[264,256]{1,0:T(8,128)S(1)} collective-permute-done((f32[264,256]{1,0:T(8,128)S(1)}, f32[264,256]{1,0:T(8,128)S(1)}, u32[]{:S(2)}, u32[]{:S(2)}) %collective-permute-start.4) | collective-permute-done | bytes 270368 | tf_op jit(solution)/shard_map/ppermute | solution.py:532
  44.1 1.3 %collective-permute-start.9 = (f32[264,256]{1,0:T(8,128)S(1)}, f32[264,256]{1,0:T(8,128)S(1)}, u32[]{:S(2)}, u32[]{:S(2)}) collective-permute-start(f32[264,256]{1,0:T(8,128)S(1)} %collective-permute-done.4.y1_ref), channel_id=1, source_target_pairs={{0,1},{1,0},{2,3},{3,2},{4,5},{5,4},{6,7},{7,6},{8,9},{9,8},{10,11... | collective-permute-start | bytes 811016 | tf_op jit(solution)/shard_map/ppermute | solution.py:522
  45.4 0.5 entering.1
  45.9 0.6 collective-permute-start.7
  46.5 0.8 collective-permute-done.7.got_ref
  47.4 0.4 start.1
  47.8 13.0 %all_to_all.20.got_ref = f32[32,2,128]{2,1,0:T(2,128)S(1)} all-to-all(f32[32,2,128]{2,1,0:T(2,128)S(1)} %get-tuple-element.43), channel_id=1, replica_groups=mesh['tracer'=4,'sub'=32] {'sub'}, dimensions={0} | all-to-all | bytes 65536 | tf_op jit(solution)/shard_map/all_to_all | solution.py:535
  60.8 3.6 %middle.1 = (f32[16,256]{1,0:T(8,128)}, f32[32,2,128]{2,1,0:T(2,128)S(1)}, f32[288,128]{1,0:T(8,128)S(1)}) custom-call(f32[32,2,128]{2,1,0:T(2,128)S(1)} %all_to_all.20.got_ref, f32[264,256]{1,0:T(8,128)S(1)} %collective-permute-done.got_ref.near1_ref.got0_ref, f32[5,264,256]{2,1,0:T(8,128)S(1)} %get-tuple-element.31.maps_ref, ...), custom_call_target="tpu_custom_call" | custom-call | tf_op jit(solution)/shard_map/middle/pallas_call | solution.py:585
  64.4 10.7 %all_to_all.21.got_ref = f32[32,2,128]{2,1,0:T(2,128)S(1)} all-to-all(f32[32,2,128]{2,1,0:T(2,128)S(1)} %get-tuple-element.46), channel_id=1, replica_groups=mesh['tracer'=4,'sub'=32] {'sub'}, dimensions={0} | all-to-all | bytes 65536 | tf_op jit(solution)/shard_map/all_to_all | solution.py:535
  75.1 1.4 %return.1 = (f32[32,2,128]{2,1,0:T(2,128)S(1)}, f32[32,128]{1,0:T(8,128)S(1)}) custom-call(f32[32,2,128]{2,1,0:T(2,128)S(1)} %all_to_all.21.got_ref, f32[264,256]{1,0:T(8,128)S(1)} %collective-permute-done.got_ref.near1_ref.got0_ref, f32[5,264,256]{2,1,0:T(8,128)S(1)} %get-tuple-element.31.maps_ref, f32[5,264,256]{2,1,0:T(8,128)S(1)} %collective-permute-done.8.mapso_ref, ...), custom_call_target="tpu_custom_call" | custom-call | tf_op jit(solution)/shard_map/return/pallas_call | solution.py:593
  76.6 10.7 %all_to_all.22.got_ref = f32[32,2,128]{2,1,0:T(2,128)S(1)} all-to-all(f32[32,2,128]{2,1,0:T(2,128)S(1)} %get-tuple-element.48), channel_id=1, replica_groups=mesh['tracer'=4,'sub'=32] {'sub'}, dimensions={0} | all-to-all | bytes 65536 | tf_op jit(solution)/shard_map/all_to_all | solution.py:535
  87.3 0.5 window.1
  87.8 16.0 %all_to_all.23.got_ref = f32[128,1,128]{2,1,0:T(1,128)S(1)} all-to-all(f32[128,1,128]{2,1,0:T(1,128)S(1)} %window.1), channel_id=1, replica_groups=mesh['tracer'=4,'sub'=32] {'tracer','sub'}, dimensions={0} | all-to-all | bytes 131072 | tf_op jit(solution)/shard_map/all_to_all | solution.py:600
  103.9 0.1 total.1
  103.9 0.6 reduce
  (18 shorter events, 0.0 us)
Async XLA Ops:
  0.6 0.7 copy-start.2
  1.3 15.9 %copy-start = (f32[1,16,256]{2,1,0:T(8,128)S(1)}, f32[1,16,256]{2,1,0:T(8,128)}, u32[]{:S(2)}) copy-start(f32[1,16,256]{2,1,0:T(8,128)} %param.11) | copy-start | bytes 49156
  1.3 15.9 %copy-start.1 = (s32[16,256]{1,0:T(8,128)S(1)}, s32[16,256]{1,0:T(8,128)}, u32[]{:S(2)}) copy-start(s32[16,256]{1,0:T(8,128)} %reg_ref.1) | copy-start | bytes 49156
  1.3 15.9 %copy-start.3 = (f32[600]{0:T(1024)S(1)}, f32[600]{0:T(1024)}, u32[]{:S(2)}) copy-start(f32[600]{0:T(1024)} %par_ref.1) | copy-start | bytes 7204
  1.3 15.9 %copy-start.4 = (s32[1,256]{1,0:T(1,128)S(1)}, s32[1,256]{1,0:T(1,128)}, u32[]{:S(2)}) copy-start(s32[1,256]{1,0:T(1,128)} %cells_ref.1) | copy-start | bytes 3076
  1.3 15.9 %copy-start.5 = (f32[1,256]{1,0:T(1,128)S(1)}, f32[1,256]{1,0:T(1,128)}, u32[]{:S(2)}) copy-start(f32[1,256]{1,0:T(1,128)} %values_ref.1) | copy-start | bytes 3076
  9.3 2.7 %collective-permute-start = (f32[264,256]{1,0:T(8,128)S(1)}, f32[264,256]{1,0:T(8,128)S(1)}, u32[]{:S(2)}, u32[]{:S(2)}) collective-permute-start(f32[264,256]{1,0:T(8,128)S(1)} %get-tuple-element.28), channel_id=1, source_target_pairs={{0,1},{1,0},{2,3},{3,2},{4,5},{5,4},{6,7},{7,6},{8,9},{9,8},{10,11... | collective-permute-start | bytes 811016 | tf_op jit(solution)/shard_map/ppermute | solution.py:522
  12.2 12.7 %collective-permute-start.3 = (f32[264,256]{1,0:T(8,128)S(1)}, f32[264,256]{1,0:T(8,128)S(1)}, u32[]{:S(2)}, u32[]{:S(2)}) collective-permute-start(f32[264,256]{1,0:T(8,128)S(1)} %chip.1.dep_ref.own_ref), channel_id=1, source_target_pairs={{0,6},{2,0},{4,2},{6,4},{8,14},{10,8},{12,10},{14,12},{16,22},{18,... | collective-permute-start | bytes 811016 | tf_op jit(solution)/shard_map/ppermute | solution.py:527
  13.6 12.3 %collective-permute-start.2 = (f32[264,256]{1,0:T(8,128)S(1)}, f32[264,256]{1,0:T(8,128)S(1)}, u32[]{:S(2)}, u32[]{:S(2)}) collective-permute-start(f32[264,256]{1,0:T(8,128)S(1)} %chip.1.dep_ref.own_ref), channel_id=1, source_target_pairs={{0,4},{2,6},{4,0},{6,2},{8,12},{10,14},{12,8},{14,10},{16,20},{18,... | collective-permute-start | bytes 811016 | tf_op jit(solution)/shard_map/ppermute | solution.py:527
  16.0 11.5 %collective-permute-start.1 = (f32[264,256]{1,0:T(8,128)S(1)}, f32[264,256]{1,0:T(8,128)S(1)}, u32[]{:S(2)}, u32[]{:S(2)}) collective-permute-start(f32[264,256]{1,0:T(8,128)S(1)} %chip.1.dep_ref.own_ref), channel_id=1, source_target_pairs={{0,2},{2,4},{4,6},{6,0},{8,10},{10,12},{12,14},{14,8},{16,18},{18,... | collective-permute-start | bytes 811016 | tf_op jit(solution)/shard_map/ppermute | solution.py:527
  28.9 18.5 %collective-permute-start.8 = (f32[5,264,256]{2,1,0:T(8,128)S(1)}, f32[5,264,256]{2,1,0:T(8,128)S(1)}, u32[]{:S(2)}, u32[]{:S(2)}) collective-permute-start(f32[5,264,256]{2,1,0:T(8,128)S(1)} %get-tuple-element.31.maps_ref), channel_id=1, source_target_pairs={{0,1},{1,0},{2,3},{3,2},{4,5},{5,4},{6,7},{7,6},{8,9},{9,8},{10,11... | collective-permute-start | bytes 4055048 | tf_op jit(solution)/shard_map/ppermute | solution.py:522
  30.8 5.0 %collective-permute-start.6 = (f32[8,256]{1,0:T(8,128)S(1)}, f32[8,256]{1,0:T(8,128)S(1)}, u32[]{:S(2)}, u32[]{:S(2)}) collective-permute-start(f32[8,256]{1,0:T(8,128)S(1)} %get-tuple-element.33), channel_id=1, source_target_pairs={{0,24},{2,26},{4,28},{6,30},{8,0},{10,2},{12,4},{14,6},{16,8},{18,... | collective-permute-start | bytes 24584 | tf_op jit(solution)/shard_map/ppermute | solution.py:532
  32.1 9.5 %collective-permute-start.5 = (f32[264,256]{1,0:T(8,128)S(1)}, f32[264,256]{1,0:T(8,128)S(1)}, u32[]{:S(2)}, u32[]{:S(2)}) collective-permute-start(f32[264,256]{1,0:T(8,128)S(1)} %get-tuple-element.32), channel_id=1, source_target_pairs={{0,16},{2,18},{4,20},{6,22},{8,24},{10,26},{12,28},{14,30},{16,0},... | collective-permute-start | bytes 811016 | tf_op jit(solution)/shard_map/ppermute | solution.py:532
  34.7 9.4 %collective-permute-start.4 = (f32[264,256]{1,0:T(8,128)S(1)}, f32[264,256]{1,0:T(8,128)S(1)}, u32[]{:S(2)}, u32[]{:S(2)}) collective-permute-start(f32[264,256]{1,0:T(8,128)S(1)} %get-tuple-element.32), channel_id=1, source_target_pairs={{0,8},{2,10},{4,12},{6,14},{8,16},{10,18},{12,20},{14,22},{16,24},... | collective-permute-start | bytes 811016 | tf_op jit(solution)/shard_map/ppermute | solution.py:532
  44.1 3.3 %collective-permute-start.9 = (f32[264,256]{1,0:T(8,128)S(1)}, f32[264,256]{1,0:T(8,128)S(1)}, u32[]{:S(2)}, u32[]{:S(2)}) collective-permute-start(f32[264,256]{1,0:T(8,128)S(1)} %collective-permute-done.4.y1_ref), channel_id=1, source_target_pairs={{0,1},{1,0},{2,3},{3,2},{4,5},{5,4},{6,7},{7,6},{8,9},{9,8},{10,11... | collective-permute-start | bytes 811016 | tf_op jit(solution)/shard_map/ppermute | solution.py:522
  45.4 1.9 %collective-permute-start.10 = (f32[264,256]{1,0:T(8,128)S(1)}, f32[264,256]{1,0:T(8,128)S(1)}, u32[]{:S(2)}, u32[]{:S(2)}) collective-permute-start(f32[264,256]{1,0:T(8,128)S(1)} %collective-permute-done.5.y2_ref), channel_id=1, source_target_pairs={{0,1},{1,0},{2,3},{3,2},{4,5},{5,4},{6,7},{7,6},{8,9},{9,8},{10,11... | collective-permute-start | bytes 811016 | tf_op jit(solution)/shard_map/ppermute | solution.py:522
  45.9 1.4 %collective-permute-start.7 = (f32[8,256]{1,0:T(8,128)S(1)}, f32[8,256]{1,0:T(8,128)S(1)}, u32[]{:S(2)}, u32[]{:S(2)}) collective-permute-start(f32[8,256]{1,0:T(8,128)S(1)} %get-tuple-element.38), channel_id=1, source_target_pairs={{0,1},{1,0},{2,3},{3,2},{4,5},{5,4},{6,7},{7,6},{8,9},{9,8},{10,11... | collective-permute-start | bytes 24584 | tf_op jit(solution)/shard_map/ppermute | solution.py:522
